TPU v7x, 32 devices: a whole 2x2x4 slice. The times are simulated.
32 devices in a mesh: fsdp: 8 (over y, x, core), dp: 4 (over z).
Axes of the slice: x: 2, y: 2, z: 4, core: 2. Of those that a mesh axis runs over, the one named last changes fastest.
Arguments:
- inputs: bfloat16 [8192, 1536], P(('fsdp', 'dp')), may hold values from -6 to 6
- cotangent: bfloat16 [8192, 1536], P(('fsdp', 'dp')), may hold values from -6 to 6
- needle: int32 [8192], P(('fsdp', 'dp')), may hold values from 0 to 1
- qkv_weight: float32 [1536, 4608], P(('fsdp', 'dp')), may hold values from -0.15625 to 0.15625
- qkv_first: float32 [1536, 4608], P(('fsdp', 'dp'))
- qkv_second: float32 [1536, 4608], P(('fsdp', 'dp')), may hold values from 327.68 to 1310.72
- out_weight: float32 [1536, 1536], P(('fsdp', 'dp')), may hold values from -0.15625 to 0.15625
- out_first: float32 [1536, 1536], P(('fsdp', 'dp'))
- out_second: float32 [1536, 1536], P(('fsdp', 'dp')), may hold values from 147.456 to 589.824
- gateup_weight: float32 [1536, 8192], P(('fsdp', 'dp')), may hold values from -0.15625 to 0.15625
- gateup_first: float32 [1536, 8192], P(('fsdp', 'dp'))
- gateup_second: float32 [1536, 8192], P(('fsdp', 'dp')), may hold values from 25.6 to 102.4
- down_weight: float32 [4096, 1536], P(('fsdp', 'dp')), may hold values from -0.09375 to 0.09375
- down_first: float32 [4096, 1536], P(('fsdp', 'dp'))
- down_second: float32 [4096, 1536], P(('fsdp', 'dp')), may hold values from 65.536 to 262.144
- norm_gains: float32 [2, 1536], P(None, ('fsdp', 'dp')), may hold values from 0.5 to 1.5
- gains_first: float32 [2, 1536], P(None, ('fsdp', 'dp'))
- gains_second: float32 [2, 1536], P(None, ('fsdp', 'dp')), as said below
- lambdas: float32 [4, 64], replicated, may hold values from -0.5 to 0.5
- lambdas_first: float32 [4, 64], replicated
- lambdas_second: float32 [4, 64], replicated, may hold values from 2457.6 to 9830.4
- head_gain: float32 [128], replicated, may hold values from 0.5 to 1.5
- head_first: float32 [128], replicated
- head_second: float32 [128], replicated, may hold values from 1638.4 to 6553.6
Outputs:
- layer_output: bfloat16 [8192, 1536], P(('fsdp', 'dp'))
- input_grad: float32 [8192, 1536], P(('fsdp', 'dp'))
- qkv_new: float32 [1536, 4608], P(('fsdp', 'dp'))
- qkv_first_new: float32 [1536, 4608], P(('fsdp', 'dp'))
- qkv_second_new: float32 [1536, 4608], P(('fsdp', 'dp'))
- out_new: float32 [1536, 1536], P(('fsdp', 'dp'))
- out_first_new: float32 [1536, 1536], P(('fsdp', 'dp'))
- out_second_new: float32 [1536, 1536], P(('fsdp', 'dp'))
- gateup_new: float32 [1536, 8192], P(('fsdp', 'dp'))
- gateup_first_new: float32 [1536, 8192], P(('fsdp', 'dp'))
- gateup_second_new: float32 [1536, 8192], P(('fsdp', 'dp'))
- down_new: float32 [4096, 1536], P(('fsdp', 'dp'))
- down_first_new: float32 [4096, 1536], P(('fsdp', 'dp'))
- down_second_new: float32 [4096, 1536], P(('fsdp', 'dp'))
- gains_new: float32 [2, 1536], P(None, ('fsdp', 'dp'))
- gains_first_new: float32 [2, 1536], P(None, ('fsdp', 'dp'))
- gains_second_new: float32 [2, 1536], P(None, ('fsdp', 'dp'))
- lambdas_new: float32 [4, 64], replicated
- lambdas_first_new: float32 [4, 64], replicated
- lambdas_second_new: float32 [4, 64], replicated
- head_new: float32 [128], replicated
- head_first_new: float32 [128], replicated
- head_second_new: float32 [128], replicated
Inputs may be any that keep to these rules, and one draw needn't show every extreme that they name: `gains_second`: positive.
All inputs are finite; a program needn't handle non-finite values.
Results may differ from a plain program's by a relative error of at most 0.028.
Values may be sent and summed in bfloat16 or wider, within the bound.
No kernel may reach another device: no remote copies, remote signals or barrier semaphores. Data moves between devices by JAX's collectives and lax.ppermute only.
A program may use at most 384 MiB of HBM per device.

v0:
```python
import jax
import jax.numpy as jnp
from jax import lax
from jax.sharding import PartitionSpec as P

HEADS = 12
HDIM = 64
FF = 4096
STEP = 10


NORM_EPSILON = 1e-05
LAMBDA_INIT = 0.2
BETA_FIRST = 0.9
BETA_SECOND = 0.95
ADAM_EPSILON = 1e-08
WEIGHT_DECAY = 0.1
RATE_MATRIX = 0.02
RATE_GAIN = 0.5
RATE_LAMBDA = 0.15
MASKED = -1000000000.0


def rms_scale(values):
    return lax.rsqrt(jnp.mean(values * values, axis=-1, keepdims=True) + NORM_EPSILON)


def contract_rows(left, right):
    return lax.dot_general(
        left, right, (((0,), (0,)), ((), ())), preferred_element_type=jnp.float32
    )


def contract_cols(left, right):
    return lax.dot_general(
        left, right, (((1,), (1,)), ((), ())), preferred_element_type=jnp.float32
    )


def norm_back(grad_normed, values, scale_rows, gain):
    scaled = grad_normed * gain
    unit_rows = values * scale_rows
    grad_values = scale_rows * (
        scaled - unit_rows * jnp.mean(scaled * unit_rows, axis=-1, keepdims=True)
    )
    grad_gain = jnp.sum(grad_normed * unit_rows, axis=0)
    return (grad_values, grad_gain)


def causal_scores(query_block, key_block, row_start, score_scale):
    scores = (
        jnp.einsum("bhcd,khcd->hcbk", query_block, key_block, preferred_element_type=jnp.float32)
        * score_scale
    )
    query_pos = row_start + jnp.arange(query_block.shape[0])
    key_pos = jnp.arange(key_block.shape[0])
    allowed = query_pos[:, None] >= key_pos[None, :]
    return jnp.where(allowed, scores, MASKED)


def adam_update(weight, first, second, grad, rate, decay):
    first_new = BETA_FIRST * first + (1.0 - BETA_FIRST) * grad
    second_new = BETA_SECOND * second + (1.0 - BETA_SECOND) * grad * grad
    corrected_first = first_new / (1.0 - BETA_FIRST**STEP)
    corrected_second = second_new / (1.0 - BETA_SECOND**STEP)
    weight_new = weight - rate * (
        corrected_first / (jnp.sqrt(corrected_second) + ADAM_EPSILON) + decay * weight
    )
    return (weight_new, first_new, second_new)


def per_device(
    inputs,
    cotangent,
    needle,
    qkv_weight,
    qkv_first,
    qkv_second,
    out_weight,
    out_first,
    out_second,
    gateup_weight,
    gateup_first,
    gateup_second,
    down_weight,
    down_first,
    down_second,
    norm_gains,
    gains_first,
    gains_second,
    lambdas,
    lambdas_first,
    lambdas_second,
    head_gain,
    head_first,
    head_second,
):
    shards = (
        qkv_weight.astype(jnp.bfloat16),
        out_weight.astype(jnp.bfloat16),
        gateup_weight.astype(jnp.bfloat16),
        down_weight.astype(jnp.bfloat16),
        norm_gains.T.astype(jnp.bfloat16),
    )
    qkv_full, out_full, gateup_full, down_full, gains_cols = (
        lax.all_gather(shards[0], ("fsdp", "dp"), axis=0, tiled=True),
        lax.all_gather(shards[1], ("fsdp", "dp"), axis=0, tiled=True),
        lax.all_gather(shards[2], ("fsdp", "dp"), axis=0, tiled=True),
        lax.all_gather(shards[3], ("fsdp", "dp"), axis=0, tiled=True),
        lax.all_gather(shards[4], ("fsdp", "dp"), axis=0, tiled=True),
    )
    gains_full = gains_cols.T
    length = inputs.shape[0]
    inner_width = HEADS * 2 * HDIM
    score_scale = HDIM ** (-0.5)
    factor = 1.0 - LAMBDA_INIT
    block_rows = min(512, length)
    activations = inputs.astype(jnp.float32)
    gain_one = gains_full[0].astype(jnp.float32)
    gain_two = gains_full[1].astype(jnp.float32)
    scale_one = rms_scale(activations)
    normed_one = (activations * scale_one * gain_one).astype(jnp.bfloat16)
    projected = jnp.dot(normed_one, qkv_full, preferred_element_type=jnp.float32).astype(
        jnp.bfloat16
    )
    queries = projected[:, :inner_width].reshape(length, HEADS, 2, HDIM)
    key_rows = projected[:, inner_width : 2 * inner_width].reshape(length, HEADS, 2, HDIM)
    value_rows = projected[:, 2 * inner_width :].reshape(length, HEADS, 2 * HDIM)
    first_term = jnp.exp(jnp.sum(lambdas[0] * lambdas[1]))
    second_term = jnp.exp(jnp.sum(lambdas[2] * lambdas[3]))
    mixing = first_term - second_term + LAMBDA_INIT
    block_index = 0
    row_start = block_index * block_rows
    scores = causal_scores(queries, key_rows, row_start, score_scale)
    row_top = jnp.max(scores, axis=-1, keepdims=True)
    exp_terms = jnp.exp(scores - row_top)
    row_total = jnp.sum(exp_terms, axis=-1, keepdims=True)
    probabilities = exp_terms / row_total
    lse_parts = [row_top + jnp.log(row_total)]
    mixed_rows = (probabilities[:, 0] - mixing * probabilities[:, 1]).astype(jnp.bfloat16)
    attended_parts = jnp.einsum(
        "hbk,khe->bhe", mixed_rows, value_rows, preferred_element_type=jnp.float32
    )
    head_scale = rms_scale(attended_parts)
    head_unit = attended_parts * head_scale
    merged = (head_unit * head_gain * factor).reshape(length, inner_width).astype(jnp.bfloat16)
    residual = activations + jnp.dot(merged, out_full, preferred_element_type=jnp.float32)
    scale_two = rms_scale(residual)
    normed_two = (residual * scale_two * gain_two).astype(jnp.bfloat16)
    gate_up = jnp.dot(normed_two, gateup_full, preferred_element_type=jnp.float32)
    gate_part = gate_up[:, :FF]
    up_part = gate_up[:, FF:]
    sigmoid_gate = jax.nn.sigmoid(gate_part)
    silu_gate = gate_part * sigmoid_gate
    hidden = (silu_gate * up_part).astype(jnp.bfloat16)
    layer_output = (
        residual + jnp.dot(hidden, down_full, preferred_element_type=jnp.float32)
    ).astype(jnp.bfloat16)
    qkv_full, out_full, gateup_full, down_full, gains_cols = (
        lax.all_gather(shards[0], ("fsdp", "dp"), axis=0, tiled=True),
        lax.all_gather(shards[1], ("fsdp", "dp"), axis=0, tiled=True),
        lax.all_gather(shards[2], ("fsdp", "dp"), axis=0, tiled=True),
        lax.all_gather(shards[3], ("fsdp", "dp"), axis=0, tiled=True),
        lax.all_gather(shards[4], ("fsdp", "dp"), axis=0, tiled=True),
    )
    grad_out = cotangent.astype(jnp.float32) * needle.astype(jnp.float32)[:, None]
    grad_out_low = grad_out.astype(jnp.bfloat16)
    grad_down = contract_rows(hidden, grad_out_low)
    grad_hidden = contract_cols(grad_out_low, down_full)
    grad_gate = grad_hidden * up_part * sigmoid_gate * (1.0 + gate_part * (1.0 - sigmoid_gate))
    grad_up = grad_hidden * silu_gate
    grad_gate_up = jnp.concatenate([grad_gate, grad_up], axis=1).astype(jnp.bfloat16)
    grad_gateup_w = contract_rows(normed_two, grad_gate_up)
    grad_normed_two = contract_cols(grad_gate_up, gateup_full)
    grad_residual_norm, grad_gain_two = norm_back(grad_normed_two, residual, scale_two, gain_two)
    grad_residual = grad_out + grad_residual_norm
    grad_residual_low = grad_residual.astype(jnp.bfloat16)
    grad_out_w = contract_rows(merged, grad_residual_low)
    grad_merged = contract_cols(grad_residual_low, out_full).reshape(length, HEADS, 2 * HDIM)
    grad_head_gain = factor * jnp.sum(grad_merged * head_unit, axis=(0, 1))
    scaled_heads = grad_merged * head_gain * factor
    grad_attended = head_scale * (
        scaled_heads - head_unit * jnp.mean(scaled_heads * head_unit, axis=-1, keepdims=True)
    )
    grad_attended_low = grad_attended.astype(jnp.bfloat16)
    grad_keys = jnp.zeros((length, HEADS, 2, HDIM), jnp.float32)
    grad_values = jnp.zeros((length, HEADS, 2 * HDIM), jnp.float32)
    grad_mixing = jnp.zeros((), jnp.float32)
    block_index = 0
    row_start = block_index * block_rows
    row_stop = row_start + block_rows
    scores = causal_scores(queries, key_rows, row_start, score_scale)
    probabilities = jnp.exp(scores - lse_parts[block_index])
    mixed_rows = (probabilities[:, 0] - mixing * probabilities[:, 1]).astype(jnp.bfloat16)
    grad_values = grad_values.at[:row_stop].add(
        jnp.einsum(
            "hbk,bhe->khe", mixed_rows, grad_attended_low, preferred_element_type=jnp.float32
        )
    )
    grad_mixed = jnp.einsum(
        "bhe,khe->hbk", grad_attended_low, value_rows, preferred_element_type=jnp.float32
    )
    grad_mixing = grad_mixing - jnp.sum(grad_mixed * probabilities[:, 1])
    grad_probs = jnp.stack([grad_mixed, -mixing * grad_mixed], axis=1)
    grad_scores = (
        probabilities * (grad_probs - jnp.sum(grad_probs * probabilities, axis=-1, keepdims=True))
    ).astype(jnp.bfloat16)
    grad_query_parts = (
        jnp.einsum("hcbk,khcd->bhcd", grad_scores, key_rows, preferred_element_type=jnp.float32)
        * score_scale
    )
    grad_keys = grad_keys.at[:row_stop].add(
        jnp.einsum("hcbk,bhcd->khcd", grad_scores, queries, preferred_element_type=jnp.float32)
        * score_scale
    )
    grad_projected = jnp.concatenate(
        [
            grad_query_parts.reshape(length, inner_width),
            grad_keys.reshape(length, inner_width),
            grad_values.reshape(length, inner_width),
        ],
        axis=1,
    ).astype(jnp.bfloat16)
    grad_qkv_w = contract_rows(normed_one, grad_projected)
    grad_normed_one = contract_cols(grad_projected, qkv_full)
    grad_inputs_norm, grad_gain_one = norm_back(grad_normed_one, activations, scale_one, gain_one)
    input_grad = grad_residual + grad_inputs_norm
    grad_gains_cols = jnp.stack([grad_gain_one, grad_gain_two], axis=1)
    total_mixing, total_head = lax.psum((grad_mixing, grad_head_gain), ("fsdp", "dp"))
    qkv_grad, out_grad, gateup_grad, down_grad, gains_cols_grad = (
        lax.psum_scatter(grad_qkv_w, ("fsdp", "dp"), scatter_dimension=0, tiled=True),
        lax.psum_scatter(grad_out_w, ("fsdp", "dp"), scatter_dimension=0, tiled=True),
        lax.psum_scatter(grad_gateup_w, ("fsdp", "dp"), scatter_dimension=0, tiled=True),
        lax.psum_scatter(grad_down, ("fsdp", "dp"), scatter_dimension=0, tiled=True),
        lax.psum_scatter(grad_gains_cols, ("fsdp", "dp"), scatter_dimension=0, tiled=True),
    )
    gains_grad = gains_cols_grad.T
    lambdas_grad = jnp.stack(
        [
            total_mixing * first_term * lambdas[1],
            total_mixing * first_term * lambdas[0],
            -total_mixing * second_term * lambdas[3],
            -total_mixing * second_term * lambdas[2],
        ]
    )
    qkv_res = adam_update(qkv_weight, qkv_first, qkv_second, qkv_grad, RATE_MATRIX, WEIGHT_DECAY)
    out_res = adam_update(out_weight, out_first, out_second, out_grad, RATE_MATRIX, WEIGHT_DECAY)
    gateup_res = adam_update(
        gateup_weight, gateup_first, gateup_second, gateup_grad, RATE_MATRIX, WEIGHT_DECAY
    )
    down_res = adam_update(
        down_weight, down_first, down_second, down_grad, RATE_MATRIX, WEIGHT_DECAY
    )
    gains_res = adam_update(norm_gains, gains_first, gains_second, gains_grad, RATE_GAIN, 0.0)
    lambdas_res = adam_update(
        lambdas, lambdas_first, lambdas_second, lambdas_grad, RATE_LAMBDA, 0.0
    )
    head_res = adam_update(head_gain, head_first, head_second, total_head, RATE_GAIN, 0.0)
    return (
        layer_output,
        input_grad,
        qkv_res[0],
        qkv_res[1],
        qkv_res[2],
        out_res[0],
        out_res[1],
        out_res[2],
        gateup_res[0],
        gateup_res[1],
        gateup_res[2],
        down_res[0],
        down_res[1],
        down_res[2],
        gains_res[0],
        gains_res[1],
        gains_res[2],
        lambdas_res[0],
        lambdas_res[1],
        lambdas_res[2],
        head_res[0],
        head_res[1],
        head_res[2],
    )


def solution(mesh):
    return jax.shard_map(
        per_device,
        mesh=mesh,
        in_specs=(
            P(("fsdp", "dp"), None),
            P(("fsdp", "dp"), None),
            P(("fsdp", "dp")),
            P(("fsdp", "dp"), None),
            P(("fsdp", "dp"), None),
            P(("fsdp", "dp"), None),
            P(("fsdp", "dp"), None),
            P(("fsdp", "dp"), None),
            P(("fsdp", "dp"), None),
            P(("fsdp", "dp"), None),
            P(("fsdp", "dp"), None),
            P(("fsdp", "dp"), None),
            P(("fsdp", "dp"), None),
            P(("fsdp", "dp"), None),
            P(("fsdp", "dp"), None),
            P(None, ("fsdp", "dp")),
            P(None, ("fsdp", "dp")),
            P(None, ("fsdp", "dp")),
            P(),
            P(),
            P(),
            P(),
            P(),
            P(),
        ),
        out_specs=(
            P(("fsdp", "dp"), None),
            P(("fsdp", "dp"), None),
            P(("fsdp", "dp"), None),
            P(("fsdp", "dp"), None),
            P(("fsdp", "dp"), None),
            P(("fsdp", "dp"), None),
            P(("fsdp", "dp"), None),
            P(("fsdp", "dp"), None),
            P(("fsdp", "dp"), None),
            P(("fsdp", "dp"), None),
            P(("fsdp", "dp"), None),
            P(("fsdp", "dp"), None),
            P(("fsdp", "dp"), None),
            P(("fsdp", "dp"), None),
            P(None, ("fsdp", "dp")),
            P(None, ("fsdp", "dp")),
            P(None, ("fsdp", "dp")),
            P(),
            P(),
            P(),
            P(),
            P(),
            P(),
        ),
        check_vma=False,
    )
```

profile of v0, /device:TPU:0, one launch (start us, length us, event | category | flops | bytes accessed | tf_op | source)
XLA Modules:
  0.0 1697.5 jit_solution(269064610050513931)
XLA Ops:
  15.2 69.7 %all-gather = bf16[32,48,2]{1,2,0:T(2,128)(2,1)S(1)} all-gather(bf16[1,48,2]{1,2,0:T(2,128)(2,1)S(1)} %convert_bitcast_fusion), channel_id=1, replica_groups=mesh['fsdp'=8,'dp'=4] {'fsdp','dp'}, dimensions={0}, use_global_device_ids=true | all-gather | bytes 6336 | tf_op jit(solution)/shard_map/all_gather | solution.py:110
  85.4 31.9 %all-gather.6.cloned.1.call-done = bf16[1536,4608]{1,0:T(8,128)(2,1)} async-done(((bf16[48,4608]{1,0:T(8,128)(2,1)}), bf16[1536,4608]{1,0:T(8,128)(2,1)}) %all-gather.6.cloned.1.call-update) | async-done | bytes 14155792 | tf_op jit(solution)/shard_map/all_gather | solution.py:106
  117.2 9.2 convolution_convert_fusion
  134.5 47.8 %all-gather.8.cloned.1.call-done = bf16[1536,1536]{1,0:T(8,128)(2,1)} async-done(((bf16[48,1536]{1,0:T(8,128)(2,1)}), bf16[1536,1536]{1,0:T(8,128)(2,1)}) %all-gather.8.cloned.1.call-update) | async-done | bytes 4718608 | tf_op jit(solution)/shard_map/all_gather | solution.py:107
  182.3 4.3 multiply_reduce_fusion.6
  186.6 152.7 %all-gather.10.cloned.1.call-done = bf16[1536,8192]{1,0:T(8,128)(2,1)} async-done(((bf16[48,8192]{1,0:T(8,128)(2,1)}), bf16[1536,8192]{1,0:T(8,128)(2,1)}) %all-gather.10.cloned.1.call-update) | async-done | bytes 25165840 | tf_op jit(solution)/shard_map/all_gather | solution.py:108
  339.3 13.6 fusion.60
  352.9 83.9 %all-gather.12.cloned.1.call-done = bf16[4096,1536]{1,0:T(8,128)(2,1)} async-done(((bf16[128,1536]{1,0:T(8,128)(2,1)}), bf16[4096,1536]{1,0:T(8,128)(2,1)}) %all-gather.12.cloned.1.call-update) | async-done | bytes 12582928 | tf_op jit(solution)/shard_map/all_gather | solution.py:109
  436.9 11.7 multiply_convert_fusion.2
  448.5 14.0 multiply_reduce_fusion.3
  479.8 10.7 fusion.20
  491.8 6.7 fusion.39
  498.7 13.9 fusion.43
  512.7 15.6 fusion.35
  528.3 22.2 %fusion.8 = f32[1536,8192]{1,0:T(8,128)} fusion(bf16[256,4096]{1,0:T(8,128)(2,1)} %get-tuple-element.99, bf16[256,4096]{1,0:T(8,128)(2,1)} %get-tuple-element.98, f32[256,1536]{1,0:T(8,128)} %copy-done.2, f32[1536]{0:T(1024)S(1)} %get-tuple-element.69, f32[256]{0:T(256)S(1)} %add_rsqrt_fusion.1), kind=kOutput, calls=%fused_computation.27 | convolution fusion | flops 6452019200 | bytes 56105984 | tf_op jit(solution)/shard_map/dot_general | solution.py:29
  554.6 39.0 %all-reduce = (f32[]{:T(128)}, f32[128]{0:T(128)S(1)}) all-reduce(f32[]{:T(128)S(6)} %sub.88, f32[128]{0:T(128)S(1)} %broadcast_multiply_fusion.3), channel_id=1, replica_groups=mesh['fsdp'=8,'dp'=4] {'fsdp','dp'}, use_global_device_ids=true, to_apply=%region_19.20 | all-reduce | flops 129 | bytes 1032 | tf_op jit(solution)/shard_map/psum | solution.py:229
  596.1 4.0 fusion.19
  600.1 8.1 fusion.10
  609.8 116.2 %reduce-scatter.10.cloned.1.call-done = f32[48,1536]{1,0:T(8,128)} async-done(((f32[1536,1536]{1,0:T(8,128)}), f32[48,1536]{1,0:T(8,128)}) %reduce-scatter.10.cloned.1.call-update) | async-done | bytes 294928 | tf_op jit(solution)/shard_map/reduce_scatter | solution.py:232
  727.9 250.1 %reduce-scatter.14.cloned.1.call-done = f32[128,1536]{1,0:T(8,128)} async-done(((f32[4096,1536]{1,0:T(8,128)}), f32[128,1536]{1,0:T(8,128)}) %reduce-scatter.14.cloned.1.call-update) | async-done | bytes 786448 | tf_op jit(solution)/shard_map/reduce_scatter | solution.py:234
  978.1 3.4 multiply_subtract_fusion.2
  981.5 266.3 %reduce-scatter.8.cloned.1.call-done = f32[48,4608]{1,0:T(8,128)} async-done(((f32[1536,4608]{1,0:T(8,128)}), f32[48,4608]{1,0:T(8,128)}) %reduce-scatter.8.cloned.1.call-update) | async-done | bytes 884752 | tf_op jit(solution)/shard_map/reduce_scatter | solution.py:231
  1251.2 434.3 %reduce-scatter.12.cloned.1.call-done = f32[48,8192]{1,0:T(8,128)} async-done(((f32[1536,8192]{1,0:T(8,128)}), f32[48,8192]{1,0:T(8,128)}) %reduce-scatter.12.cloned.1.call-update) | async-done | bytes 1572880 | tf_op jit(solution)/shard_map/reduce_scatter | solution.py:233
  1685.4 5.3 multiply_subtract_fusion
  (153 shorter events, 44.9 us)
Async XLA Ops:
  7.2 110.0 %all-gather.6.cloned.1.call-start = ((), (), s32[]{:S(2)}) async-start(), calls=%async_computation.5 | async-start | bytes 14598144 | tf_op jit(solution)/shard_map/all_gather | solution.py:106
  9.4 173.0 %all-gather.8.cloned.1.call-start = ((), (), s32[]{:S(2)}) async-start(), calls=%async_computation.6 | async-start | bytes 4866048 | tf_op jit(solution)/shard_map/all_gather | solution.py:107
  11.2 73.9 %copy-start.5 = (bf16[256,1536]{1,0:T(8,128)(2,1)S(1)}, bf16[256,1536]{1,0:T(8,128)(2,1)}, u32[]{:S(2)}) copy-start(bf16[256,1536]{1,0:T(8,128)(2,1)} %param.32) | copy-start | bytes 2359300
  11.2 328.1 %all-gather.10.cloned.1.call-start = ((), (), s32[]{:S(2)}) async-start(), calls=%async_computation.7 | async-start | bytes 25952256 | tf_op jit(solution)/shard_map/all_gather | solution.py:108
  12.2 424.6 %all-gather.12.cloned.1.call-start = ((), (), s32[]{:S(2)}) async-start(), calls=%async_computation.8 | async-start | bytes 12976128 | tf_op jit(solution)/shard_map/all_gather | solution.py:109
  13.1 595.2 %reduce-scatter.16.cloned.1.call-start = ((), (), s32[]{:S(2)}) async-start(), calls=%async_computation.13 | async-start | bytes 811008
  186.6 276.0 %copy-start.2 = (f32[256,1536]{1,0:T(8,128)}, f32[256,1536]{1,0:T(8,128)S(1)}, u32[]{:S(2)}) copy-start(f32[256,1536]{1,0:T(8,128)S(1)} %get-tuple-element.113) | copy-start | bytes 4718596
  436.9 27.9 %slice-start.2 = ((s8[4718592]{0:T(1024)(128)(4,1)}), s8[4194304]{0:T(1024)(128)(4,1)S(1)}, s32[]{:S(2)}) async-start(s8[4718592]{0:T(1024)(128)(4,1)} %bitcast.99), calls=%async_computation.16 | async-start | bytes 8388608
  491.8 234.2 %reduce-scatter.10.cloned.1.call-start = ((), (), s32[]{:S(2)}) async-start(), calls=%async_computation.10 | async-start | bytes 9732096 | tf_op jit(solution)/shard_map/reduce_scatter | solution.py:232
  498.5 479.6 %reduce-scatter.14.cloned.1.call-start = ((), (), s32[]{:S(2)}) async-start(), calls=%async_computation.12 | async-start | bytes 25952256 | tf_op jit(solution)/shard_map/reduce_scatter | solution.py:234
  512.6 735.2 %reduce-scatter.8.cloned.1.call-start = ((), (), s32[]{:S(2)}) async-start(), calls=%async_computation.9 | async-start | bytes 29196288 | tf_op jit(solution)/shard_map/reduce_scatter | solution.py:231
  528.2 1157.2 %reduce-scatter.12.cloned.1.call-start = ((), (), s32[]{:S(2)}) async-start(), calls=%async_computation.11 | async-start | bytes 51904512 | tf_op jit(solution)/shard_map/reduce_scatter | solution.py:233
  550.5 44.3 %copy-start.34 = (f32[128]{0:T(128)S(1)}, f32[128]{0:T(128)}, u32[]{:S(2)}) copy-start(f32[128]{0:T(128)} %param.54) | copy-start | bytes 1540
  550.5 44.3 %copy-start.35 = (f32[128]{0:T(128)S(1)}, f32[128]{0:T(128)}, u32[]{:S(2)}) copy-start(f32[128]{0:T(128)} %param.55) | copy-start | bytes 1540
  550.6 44.9 %copy-start.25 = (f32[4,64]{1,0:T(4,128)S(1)}, f32[4,64]{1,0:T(4,128)}, u32[]{:S(2)}) copy-start(f32[4,64]{1,0:T(4,128)} %param.50) | copy-start | bytes 3076
  550.6 44.9 %copy-start.27 = (f32[4,64]{1,0:T(4,128)S(1)}, f32[4,64]{1,0:T(4,128)}, u32[]{:S(2)}) copy-start(f32[4,64]{1,0:T(4,128)} %param.51) | copy-start | bytes 3076
  550.6 44.9 %copy-start.28 = (f32[4,64]{1,0:T(4,128)S(1)}, f32[4,64]{1,0:T(4,128)}, u32[]{:S(2)}) copy-start(f32[4,64]{1,0:T(4,128)} %param.52) | copy-start | bytes 3076
  600.1 125.8 %copy-start.20 = (f32[48,1536]{1,0:T(8,128)S(1)}, f32[48,1536]{1,0:T(8,128)}, u32[]{:S(2)}) copy-start(f32[48,1536]{1,0:T(8,128)} %param.38) | copy-start | bytes 884740
  600.1 125.8 %copy-start.22 = (f32[48,1536]{1,0:T(8,128)S(1)}, f32[48,1536]{1,0:T(8,128)}, u32[]{:S(2)}) copy-start(f32[48,1536]{1,0:T(8,128)} %param.39) | copy-start | bytes 884740
  600.1 125.8 %copy-start.23 = (f32[48,1536]{1,0:T(8,128)S(1)}, f32[48,1536]{1,0:T(8,128)}, u32[]{:S(2)}) copy-start(f32[48,1536]{1,0:T(8,128)} %param.40) | copy-start | bytes 884740
  608.3 369.8 %copy-start.18 = (f32[128,1536]{1,0:T(8,128)S(1)}, f32[128,1536]{1,0:T(8,128)}, u32[]{:S(2)}) copy-start(f32[128,1536]{1,0:T(8,128)} %param.44) | copy-start | bytes 2359300
  727.9 519.9 %copy-start.16 = (f32[48,4608]{1,0:T(8,128)S(1)}, f32[48,4608]{1,0:T(8,128)}, u32[]{:S(2)}) copy-start(f32[48,4608]{1,0:T(8,128)} %param.35) | copy-start | bytes 2654212
  727.9 519.9 %copy-start.21 = (f32[48,4608]{1,0:T(8,128)S(1)}, f32[48,4608]{1,0:T(8,128)}, u32[]{:S(2)}) copy-start(f32[48,4608]{1,0:T(8,128)} %param.36) | copy-start | bytes 2654212
  981.5 703.9 %copy-start.14 = (f32[48,8192]{1,0:T(8,128)S(1)}, f32[48,8192]{1,0:T(8,128)}, u32[]{:S(2)}) copy-start(f32[48,8192]{1,0:T(8,128)} %param.41) | copy-start | bytes 4718596
  (25 other events, 95.8 us)
Sparse Core Ops, SparseCore 0:
  11.4 105.7 all-gather.5
  120.6 61.6 all-gather.7
  185.8 153.4 all-gather.9
  342.6 94.2 all-gather.11
  491.9 93.7 reduce-scatter.15
  591.4 134.4 reduce-scatter.9
  733.5 244.5 reduce-scatter.13
  984.5 263.2 reduce-scatter.7
  1254.3 431.1 reduce-scatter.11
where the time goes:
time: 1710 us; the launch traced here: 1700 us
  waiting for transfers between devices  1380 us (81%)
  matrix products  139 us (8%)
  blocking collectives  109 us (6%)
  other arithmetic  41 us (2%)
  between operations  18 us (1%)
    reduce_scatter x1, waiting for transfers between devices, per_device(): lax.psum_scatter(grad_gateup_w, ('fsdp', 'dp'), scatter_dimension=0, tile...  434 us
    reduce_scatter x1, waiting for transfers between devices, per_device(): lax.psum_scatter(grad_qkv_w, ('fsdp', 'dp'), scatter_dimension=0, tiled=T...  266 us
    reduce_scatter x1, waiting for transfers between devices, per_device(): lax.psum_scatter(grad_down, ('fsdp', 'dp'), scatter_dimension=0, tiled=True)  250 us
    all_gather x1, waiting for transfers between devices, per_device(): lax.all_gather(shards[2], ('fsdp', 'dp'), axis=0, tiled=True)  153 us
    reduce_scatter x1, waiting for transfers between devices, per_device(): lax.psum_scatter(grad_out_w, ('fsdp', 'dp'), scatter_dimension=0, tiled=T...  116 us
    all_gather x1, waiting for transfers between devices, per_device(): lax.all_gather(shards[3], ('fsdp', 'dp'), axis=0, tiled=True)  83.9 us
    all_gather x1, blocking collectives, per_device(): lax.all_gather(shards[4], ('fsdp', 'dp'), axis=0, tiled=True)  69.7 us
    dot_general x4, matrix products, contract_rows(): lax.dot_general(left, right, (((0,), (0,)), ((), ())), preferred_element_...  58.3 us
  transfers between devices with their start and end apart: 9, of which 8 were waited for; matrix products, arithmetic and copies ran while one was open for 7% of the time, Pallas kernels for 0%

commit v1 on v0

v1 whole, which is shorter than its diff:
```python
import functools

import jax
import jax.numpy as jnp
from jax import lax
from jax.experimental import pallas as pl
from jax.experimental.pallas import tpu as pltpu
from jax.sharding import Mesh
from jax.sharding import PartitionSpec as P

HEADS = 12
HDIM = 64
HEAD = 2 * HDIM
FF = 4096
STEP = 10
PLANE = 4
LOCAL_HEADS = HEADS // PLANE
LOCAL_FF = FF // PLANE
LOCAL_Q = LOCAL_HEADS * HEAD

NORM_EPSILON = 1e-05
LAMBDA_INIT = 0.2
FACTOR = 1.0 - LAMBDA_INIT
BETA_FIRST = 0.9
BETA_SECOND = 0.95
ADAM_EPSILON = 1e-08
WEIGHT_DECAY = 0.1
RATE_MATRIX = 0.02
RATE_GAIN = 0.5
RATE_LAMBDA = 0.15
MASKED = -1000000000.0
SCALE = HDIM ** (-0.5)

BF16 = jnp.bfloat16
F32 = jnp.float32
VMEM_LIMIT = 48 * 1024 * 1024
AXES = ("j", "c", "dp")


def rms_scale(values):
    return lax.rsqrt(jnp.mean(values * values, axis=-1, keepdims=True) + NORM_EPSILON)


def mm(left, right):
    return lax.dot_general(left, right, (((1,), (0,)), ((), ())), preferred_element_type=F32)


def mm_nt(left, right):
    return lax.dot_general(left, right, (((1,), (1,)), ((), ())), preferred_element_type=F32)


def mm_tn(left, right):
    return lax.dot_general(left, right, (((0,), (0,)), ((), ())), preferred_element_type=F32)


def softmax_pair(q, k, rows):
    first = lax.broadcasted_iota(jnp.int32, (rows, HEAD), 1) < HDIM
    allowed = lax.broadcasted_iota(jnp.int32, (rows, rows), 0) >= lax.broadcasted_iota(
        jnp.int32, (rows, rows), 1
    )
    zero = jnp.zeros_like(q)
    result = []
    for half in (jnp.where(first, q, zero), jnp.where(first, zero, q)):
        scores = jnp.where(allowed, mm_nt(half, k) * SCALE, MASKED)
        terms = jnp.exp(scores - jnp.max(scores, axis=-1, keepdims=True))
        result.append(terms * (1.0 / jnp.sum(terms, axis=-1, keepdims=True)))
    return result


def attend_kernel(x_ref, gain_ref, wq_ref, wo_ref, lam_ref, hg_ref, n_ref, p_ref, g_ref, o_ref):
    rows = x_ref.shape[0]
    x = x_ref[...].astype(F32)
    n_ref[...] = (x * rms_scale(x) * gain_ref[...]).astype(BF16)
    for part in range(3):
        cols = pl.ds(part * LOCAL_Q, LOCAL_Q)
        p_ref[:, cols] = mm(n_ref[...], wq_ref[:, cols]).astype(BF16)
    lam = lam_ref[0, 0]
    for head in range(LOCAL_HEADS):
        q, k, v = (
            p_ref[:, pl.ds(part * LOCAL_Q + head * HEAD, HEAD)] for part in range(3)
        )
        a1, a2 = softmax_pair(q, k, rows)
        mixed = (a1 - lam * a2).astype(BF16)
        out = mm(mixed, v)
        g_ref[:, pl.ds(head * HEAD, HEAD)] = (
            out * rms_scale(out) * hg_ref[...] * FACTOR
        ).astype(BF16)
    o_ref[...] = mm(g_ref[...], wo_ref[...]).astype(BF16)


def ffn_kernel(count, *refs):
    n_refs, dy_refs, (wgu_ref, wd_ref) = refs[:count], refs[count : 2 * count], refs[2 * count :][:2]
    outs, (hidden_ref, grad_ref) = refs[2 * count + 2 : -2], refs[-2:]
    length = n_refs[0].shape[0]
    normed = jnp.concatenate([ref[...] for ref in n_refs], axis=0)
    gate = mm(normed, wgu_ref[:, :LOCAL_FF])
    up = mm(normed, wgu_ref[:, LOCAL_FF:])
    dh = mm_nt(jnp.concatenate([ref[...] for ref in dy_refs], axis=0), wd_ref[...])
    sig = 0.5 * jnp.tanh(0.5 * gate) + 0.5
    silu = gate * sig
    hidden_ref[...] = (silu * up).astype(BF16)
    grad_ref[:, :LOCAL_FF] = (dh * up * (sig + silu * (1.0 - sig))).astype(BF16)
    grad_ref[:, LOCAL_FF:] = (dh * silu).astype(BF16)
    out = mm(hidden_ref[...], wd_ref[...]).astype(BF16)
    back = mm_nt(grad_ref[...], wgu_ref[...]).astype(BF16)
    for i in range(count):
        at = slice(i * length, (i + 1) * length)
        y_ref, dn_ref, h_ref, du_ref = outs[4 * i : 4 * i + 4]
        y_ref[...] = out[at]
        dn_ref[...] = back[at]
        h_ref[...] = hidden_ref[at, :]
        du_ref[...] = grad_ref[at, :]


def attend_back_kernel(
    dh_ref, p_ref, wq_ref, wo_ref, lam_ref, hg_ref, dp_ref, dn_ref, stat_ref, dg_ref
):
    rows = dh_ref.shape[0]
    dg_ref[...] = mm_nt(dh_ref[...], wo_ref[...])
    lam = lam_ref[0, 0]
    hg = hg_ref[...]
    first = lax.broadcasted_iota(jnp.int32, (rows, HEAD), 1) < HDIM
    grad_hg = jnp.zeros((1, HEAD), F32)
    grad_lam = jnp.zeros((1, 1), F32)
    for head in range(LOCAL_HEADS):
        q, k, v = (
            p_ref[:, pl.ds(part * LOCAL_Q + head * HEAD, HEAD)] for part in range(3)
        )
        a1, a2 = softmax_pair(q, k, rows)
        mixed = (a1 - lam * a2).astype(BF16)
        out = mm(mixed, v)
        scale = rms_scale(out)
        unit = out * scale
        dg = dg_ref[:, pl.ds(head * HEAD, HEAD)]
        grad_hg = grad_hg + FACTOR * jnp.sum(dg * unit, axis=0, keepdims=True)
        u = dg * hg * FACTOR
        dout = (scale * (u - unit * jnp.mean(u * unit, axis=-1, keepdims=True))).astype(BF16)
        dv = mm_tn(mixed, dout)
        dm = mm_nt(dout, v)
        dot1 = jnp.sum(dm * a1, axis=-1, keepdims=True)
        dot2 = jnp.sum(dm * a2, axis=-1, keepdims=True)
        grad_lam = grad_lam - jnp.sum(dot2, axis=0, keepdims=True)
        ds1 = (a1 * (dm - dot1)).astype(BF16)
        ds2 = (-lam * a2 * (dm - dot2)).astype(BF16)
        dq = jnp.where(first, mm(ds1, k), mm(ds2, k)) * SCALE
        dk = jnp.where(first, mm_tn(ds1, q), mm_tn(ds2, q)) * SCALE
        for part, value in enumerate((dq, dk, dv)):
            dp_ref[:, pl.ds(part * LOCAL_Q + head * HEAD, HEAD)] = value.astype(BF16)
    stat_ref[0:1, :] = grad_hg
    stat_ref[1:2, :] = jnp.broadcast_to(grad_lam, (1, HEAD))
    dn_ref[...] = mm_nt(dp_ref[...], wq_ref[:, : 3 * LOCAL_Q]).astype(BF16)


def split_kernel(pos_ref, qkv_ref, gain_ref, gateup_ref, *outs):
    rows = qkv_ref.shape[0]
    gains = jnp.concatenate([gain_ref[...], jnp.zeros((HEAD - 2, rows), F32)], axis=0).T
    for r in range(PLANE):
        q = pos_ref[0] ^ r
        start = 0
        for w_ref, parts in ((qkv_ref, 3), (gateup_ref, 2)):
            width = w_ref.shape[1] // parts
            quarter = width // PLANE
            for part in range(parts):
                cols = pl.ds(pl.multiple_of(part * width + q * quarter, HEAD), quarter)
                outs[r][:, start : start + quarter] = w_ref[:, cols].astype(BF16)
                start += quarter
            if parts == 3:
                outs[r][:, start : start + HEAD] = gains.astype(BF16)
                start += HEAD


def reorder_kernel(in_ref, out_ref, sem):
    count = in_ref.shape[0]
    copies = [
        pltpu.make_async_copy(in_ref.at[k], out_ref.at[:, k], sem.at[k]) for k in range(count)
    ]
    for copy in copies:
        copy.start()
    for copy in copies:
        copy.wait()


def down_blocks(rows):
    tall, block = rows * 3 // 4, 512
    cuts = sorted({*range(0, 3 * rows + 1, rows), *range(0, 3 * rows + 1, tall)})
    for at, stop in zip(cuts, cuts[1:]):
        yield at % rows, at // rows * block, at % tall, at // tall * block, stop - at


def message_kernel(slot_ref, *refs):
    pieces, (weight_ref, down_ref, out_ref, second_ref, sem) = refs[:PLANE], refs[PLANE:]
    rows, columns = pieces[0].shape
    wide = columns - second_ref.shape[1]
    copies = []
    for r in range(PLANE):
        cols = pl.ds(pl.multiple_of(slot_ref[r] * wide, HEAD), wide)
        copies.append(
            pltpu.make_async_copy(pieces[r].at[:, pl.ds(0, wide)], out_ref.at[:, cols], sem.at[r, 0])
        )
        copies.append(
            pltpu.make_async_copy(
                pieces[r].at[:, pl.ds(wide, second_ref.shape[1])],
                second_ref.at[pl.ds(pl.multiple_of(slot_ref[r] * rows, 16), rows)],
                sem.at[r, 1],
            )
        )
    for copy in copies:
        copy.start()
    out_ref[:, PLANE * wide :] = weight_ref[...].astype(BF16)
    for row, col, to_row, to_col, count in down_blocks(down_ref.shape[0]):
        second_ref[pl.ds(PLANE * rows + to_row, count), pl.ds(to_col, 512)] = down_ref[
            row : row + count, col : col + 512
        ].astype(BF16)
    for copy in copies:
        copy.wait()


def message_plain_kernel(slot_ref, *refs):
    pieces, (weight_ref, out_ref, gateup_ref, sem) = refs[:PLANE], refs[PLANE:]
    wide = pieces[0].shape[1] - gateup_ref.shape[2]
    copies = []
    for r in range(PLANE):
        cols = pl.ds(pl.multiple_of(slot_ref[r] * wide, HEAD), wide)
        copies.append(
            pltpu.make_async_copy(pieces[r].at[:, pl.ds(0, wide)], out_ref.at[:, cols], sem.at[r, 0])
        )
        copies.append(
            pltpu.make_async_copy(
                pieces[r].at[:, pl.ds(wide, gateup_ref.shape[2])], gateup_ref.at[slot_ref[r]], sem.at[r, 1]
            )
        )
    for copy in copies:
        copy.start()
    out_ref[:, PLANE * wide :] = weight_ref[...].astype(BF16)
    for copy in copies:
        copy.wait()


def place_second_kernel(in_ref, blocks_ref, gateup_ref, down_ref, sem):
    rows, tall = gateup_ref.shape[2], down_ref.shape[1]
    copies = []
    for k in range(in_ref.shape[0]):
        copies.append((blocks_ref.at[k, pl.ds(0, PLANE)], gateup_ref.at[:, k]))
        for row, col, to_row, to_col, count in down_blocks(tall):
            copies.append(
                (
                    in_ref.at[k, pl.ds(PLANE * rows + to_row, count), pl.ds(to_col, 512)],
                    down_ref.at[k, pl.ds(row, count), pl.ds(col, 512)],
                )
            )
    copies = [pltpu.make_async_copy(a, b, sem.at[i]) for i, (a, b) in enumerate(copies)]
    for copy in copies:
        copy.start()
    for copy in copies:
        copy.wait()


def place_first_kernel(in_ref, qkv_ref, out_ref, gain_ref, sem):
    count, (rows, wide) = in_ref.shape[0], qkv_ref.shape[2:]
    copies = []
    for k in range(count):
        for j in range(PLANE):
            copies.append((in_ref.at[k, :, pl.ds(j * wide, wide)], qkv_ref.at[j, k]))
        copies.append((in_ref.at[k, :, pl.ds(PLANE * wide, out_ref.shape[2])], out_ref.at[k]))
    copies = [pltpu.make_async_copy(a, b, sem.at[i]) for i, (a, b) in enumerate(copies)]
    for copy in copies:
        copy.start()
    for copy in copies:
        copy.wait()
    columns = qkv_ref[:, :, :, 3 * LOCAL_Q :].astype(F32).reshape(PLANE * count * rows, HEAD)
    gain_ref[...] = columns.T[:8]


def weight_grad_kernel(m, pos_ref, *refs):
    lefts, rights, outs = refs[:PLANE], refs[PLANE : 2 * PLANE], refs[2 * PLANE : 2 * PLANE + m]
    left, right, total, sem = refs[2 * PLANE + m :]
    length = lefts[0].shape[0]
    copies = []
    for r in range(PLANE):
        for i, (src, dst) in enumerate(((lefts[r], left), (rights[r], right))):
            copies.append(
                pltpu.make_async_copy(
                    src, dst.at[pl.ds(r * length, length)], sem.at[2 * r + i]
                )
            )
            copies[-1].start()
    for copy in copies:
        copy.wait()
    rows, columns = total.shape
    share = rows // m
    for lead in range(outs[0].shape[0]):
        value = mm_tn(left[:, lead * rows : (lead + 1) * rows], right[...])
        if m == 2:
            top, low = value[:share].astype(BF16), value[share:].astype(BF16)
            outs[0][lead] = jnp.where(pos_ref[1] == 0, top, low)
            outs[1][lead] = jnp.where(pos_ref[1] == 0, low, top)
        else:
            total[...] = value
            for k in range(m):
                start = pl.multiple_of(((pos_ref[1] + k) % m) * share, 8)
                outs[k][lead] = total[pl.ds(start, share), :].astype(BF16)


def chunk_second_kernel(m, *refs):
    gateup, down, out = refs[:m], refs[m : 2 * m], refs[2 * m]
    d = out.shape[0]
    rows, tall = gateup[0].shape[1] // d, down[0].shape[1] // d
    for z in range(d):
        for j in range(PLANE):
            value = add_up([term[j, z * rows : (z + 1) * rows, :] for term in gateup])
            out[z, j * rows : (j + 1) * rows, :] = value.astype(BF16)
        value = add_up([term[0, z * tall : (z + 1) * tall, :] for term in down]).astype(BF16)
        for row, col, to_row, to_col, count in down_blocks(tall):
            out[z, pl.ds(PLANE * rows + to_row, count), pl.ds(to_col, 512)] = value[
                row : row + count, col : col + 512
            ]


def chunk_first_kernel(m, *refs):
    qkv, out_terms, out = refs[:m], refs[m : 2 * m], refs[2 * m]
    d, rows, _ = out.shape
    wide = qkv[0].shape[2]
    for z in range(d):
        for j in range(PLANE + 1):
            terms, lead = (qkv, j) if j < PLANE else (out_terms, 0)
            value = add_up([term[lead, z * rows : (z + 1) * rows, :] for term in terms])
            out[z, :, j * wide : j * wide + value.shape[1]] = value.astype(BF16)


def owner_first_kernel(pos_ref, in_ref, *outs):
    *outs, out_ref = outs
    wide = outs[0].shape[1]
    for r in range(PLANE):
        outs[r][...] = in_ref[:, pl.ds(pl.multiple_of((pos_ref[0] ^ r) * wide, HEAD), wide)]
    out_ref[...] = in_ref[:, PLANE * wide :].astype(F32)


def owner_second_kernel(pos_ref, in_ref, *outs):
    *outs, down_ref = outs
    rows, tall = outs[0].shape[0], down_ref.shape[0]
    for r in range(PLANE):
        outs[r][...] = in_ref[pl.ds(pl.multiple_of((pos_ref[0] ^ r) * rows, 16), rows), :]
    for row, col, to_row, to_col, count in down_blocks(tall):
        down_ref[row : row + count, col : col + 512] = in_ref[
            pl.ds(PLANE * rows + to_row, count), pl.ds(to_col, 512)
        ].astype(F32)


def adam_columns_kernel(parts, width, pos_ref, *refs):
    pieces, (w_ref, f_ref, s_ref, wn_ref, fn_ref, sn_ref, dot_ref) = refs[:PLANE], refs[PLANE:]
    quarter = width // PLANE
    dot = jnp.zeros((w_ref.shape[0], 1), F32)
    for r in range(PLANE):
        q = pos_ref[0] ^ r
        for part in range(parts):
            cols = pl.ds(pl.multiple_of(part * width + q * quarter, HEAD), quarter)
            grad = pieces[r][:, part * quarter : (part + 1) * quarter].astype(F32)
            weight = w_ref[:, cols]
            dot = dot + jnp.sum(weight.astype(BF16).astype(F32) * grad, axis=1, keepdims=True)
            wn_ref[:, cols], fn_ref[:, cols], sn_ref[:, cols] = adam_update(
                weight, f_ref[:, cols], s_ref[:, cols], grad, RATE_MATRIX, WEIGHT_DECAY
            )
    dot_ref[...] = jnp.broadcast_to(dot, (dot.shape[0], HEAD)).T[:8]


ANY = pl.BlockSpec(memory_space=pl.ANY)
VMEM = pl.BlockSpec(memory_space=pltpu.VMEM)
SMEM = pl.BlockSpec(memory_space=pltpu.SMEM)


def call(kernel, outs, operands, scratch=(), flops=0, specs=None, out_spec=VMEM):
    size = sum(a.size * a.dtype.itemsize for a in operands) + sum(
        o.size * o.dtype.itemsize for o in outs
    )
    return pl.pallas_call(
        kernel,
        out_shape=tuple(outs),
        in_specs=specs or [VMEM] * len(operands),
        out_specs=(out_spec,) * len(outs),
        scratch_shapes=list(scratch),
        compiler_params=pltpu.CompilerParams(vmem_limit_bytes=VMEM_LIMIT),
        cost_estimate=pl.CostEstimate(flops=0, bytes_accessed=0, transcendentals=0),
    )(*operands)


def shaped(*shape, dtype=BF16):
    return jax.ShapeDtypeStruct(shape, dtype)


def tie(value, *after):
    return lax.optimization_barrier((value, *after))[0]


class Group:
    def __init__(self, m, d):
        self.m, self.d = m, d
        self.j, self.c, self.z = (lax.axis_index(axis) for axis in AXES)
        self.pos = jnp.stack([self.j, self.c, self.z]).astype(jnp.int32)

    def plane(self, value, r):
        return lax.ppermute(value, "j", [(i, i ^ r) for i in range(PLANE)])

    def core(self, value, k):
        return lax.ppermute(value, "c", [(i, (i + k) % self.m) for i in range(self.m)])

    def everyone(self, value):
        n, step = PLANE * self.m * self.d, 1
        while step < n:
            value = value + lax.ppermute(value, AXES, [(i, i ^ step) for i in range(n)])
            step *= 2
        return value


def plane_near(grp, own):
    return [own, grp.plane(own, 1), grp.plane(own, 2)]


def plane_far(grp, near, *after):
    own, one, two = near
    half = own.shape[0] // 2
    if after:
        one, two = tie(one, *after), tie(two, *after)
    three = jnp.concatenate([grp.plane(one[:half], 2), grp.plane(two[half:], 1)], axis=0)
    return [own, one, two, three]


def plane_gather(grp, own):
    return plane_far(grp, plane_near(grp, own))


def plane_send(grp, parts):
    return [parts[0]] + [grp.plane(parts[r], r) for r in range(1, PLANE)]


def plane_scatter_first(grp, parts, axis):
    return grp.plane(jnp.concatenate([parts[axis], parts[3]], axis=0), axis)


def plane_scatter_second(grp, parts, axis, got):
    half = parts[0].shape[0]
    sent = add_up([parts[3 - axis], got[half:]]).astype(BF16)
    return [parts[0], got[:half], grp.plane(sent, 3 - axis)], sent


def add_up(terms):
    return sum(term.astype(F32) for term in terms)


def exchange(grp, pieces):
    return [pieces[0]] + [grp.plane(pieces[r], r) for r in range(1, PLANE)]


def core_terms(grp, halves):
    return [halves[0]] + [grp.core(halves[k], k) for k in range(1, grp.m)]


def spread(grp, kernel, shape, wide, tall):
    message = call(
        functools.partial(kernel, grp.m),
        (shaped(grp.d, *shape),),
        (*core_terms(grp, wide), *core_terms(grp, tall)),
    )[0]
    return message, lax.psum_scatter(message, "dp", scatter_dimension=0, tiled=False)


def owner(grp, kernel, message, piece, rest):
    *pieces, out = call(
        kernel,
        (shaped(*piece),) * PLANE + (shaped(*rest, dtype=F32),),
        (grp.pos, message),
        specs=[SMEM, VMEM],
    )
    return pieces, out


def owner_plain(grp, halves):
    d, m = grp.d, grp.m
    full = jnp.stack([lax.dynamic_index_in_dim(jnp.stack(halves), (k - grp.c) % m, 0, False) for k in range(m)])
    lead, rows, columns = halves[0].shape
    full = full.reshape(m, lead, d, rows // d, columns).transpose(0, 2, 1, 3, 4)
    full = full.reshape(m * d, lead, rows // d, columns)
    return lax.psum_scatter(full, ("c", "dp"), scatter_dimension=0, tiled=False).astype(F32)


def weight_grad(grp, lefts, rights, lead):
    length, rows = lefts[0].shape
    columns = rights[0].shape[1]
    share = rows // lead // grp.m
    return call(
        functools.partial(weight_grad_kernel, grp.m),
        (shaped(lead, share, columns),) * grp.m,
        (grp.pos, *lefts, *rights),
        scratch=(
            pltpu.VMEM((PLANE * length, rows), BF16),
            pltpu.VMEM((PLANE * length, columns), BF16),
            pltpu.VMEM((rows // lead, columns), F32),
            pltpu.SemaphoreType.DMA((2 * PLANE,)),
        ),
        specs=[SMEM] + [ANY] * (2 * PLANE),
        flops=2 * PLANE * length * rows * columns,
    )


def adam_columns(grp, pieces, weight, first, second, parts):
    rows, columns = weight.shape
    return call(
        functools.partial(adam_columns_kernel, parts, columns // parts),
        (shaped(rows, columns, dtype=F32),) * 3 + (shaped(8, rows, dtype=F32),),
        (grp.pos, *pieces, weight, first, second),
        specs=[SMEM] + [VMEM] * (PLANE + 3),
    )


def norm_back(grad_normed, values, gain):
    scale_rows = rms_scale(values)
    scaled = grad_normed * gain
    unit_rows = values * scale_rows
    return scale_rows * (
        scaled - unit_rows * jnp.mean(scaled * unit_rows, axis=-1, keepdims=True)
    )


def adam_update(weight, first, second, grad, rate, decay):
    first_new = BETA_FIRST * first + (1.0 - BETA_FIRST) * grad
    second_new = BETA_SECOND * second + (1.0 - BETA_SECOND) * grad * grad
    corrected_first = first_new / (1.0 - BETA_FIRST**STEP)
    corrected_second = second_new / (1.0 - BETA_SECOND**STEP)
    weight_new = weight - rate * (
        corrected_first / (jnp.sqrt(corrected_second) + ADAM_EPSILON) + decay * weight
    )
    return (weight_new, first_new, second_new)


def per_device(
    members,
    d,
    inputs,
    cotangent,
    needle,
    qkv_weight,
    qkv_first,
    qkv_second,
    out_weight,
    out_first,
    out_second,
    gateup_weight,
    gateup_first,
    gateup_second,
    down_weight,
    down_first,
    down_second,
    norm_gains,
    gains_first,
    gains_second,
    lambdas,
    lambdas_first,
    lambdas_second,
    head_gain,
    head_first,
    head_second,
):
    grp = Group(members, d)
    length, width = inputs.shape
    rows = qkv_weight.shape[0]
    struct = jax.ShapeDtypeStruct

    gains_low = norm_gains.astype(BF16)
    plane_slots = jnp.stack([grp.j ^ r for r in range(PLANE)]).astype(jnp.int32)
    wide = 3 * LOCAL_Q + HEAD
    quarters = call(
        split_kernel,
        (shaped(rows, wide + 2 * LOCAL_FF),) * PLANE,
        (grp.pos, qkv_weight, norm_gains, gateup_weight),
        specs=[SMEM] + [VMEM] * 3,
    )
    tuned = rows % 16 == 0
    count = members * d
    everywhere = functools.partial(lax.all_gather, axis_name=("c", "dp"), axis=0, tiled=False)
    exchanged = exchange(grp, quarters)
    if tuned:
        first_message, second_message = call(
            message_kernel,
            (
                shaped(rows, PLANE * wide + width),
                shaped(PLANE * rows + down_weight.shape[0] * 3 // 4, 2 * LOCAL_FF),
            ),
            (plane_slots, *exchanged, out_weight, down_weight),
            scratch=(pltpu.SemaphoreType.DMA((PLANE, 2)),),
            specs=[SMEM] + [ANY] * PLANE + [VMEM] * 2,
        )
    else:
        first_message, second_message = call(
            message_plain_kernel,
            (shaped(rows, PLANE * wide + width), shaped(PLANE, rows, 2 * LOCAL_FF)),
            (plane_slots, *exchanged, out_weight),
            scratch=(pltpu.SemaphoreType.DMA((PLANE, 2)),),
            specs=[SMEM] + [ANY] * PLANE + [VMEM],
        )
    x_blocks = plane_gather(grp, tie(inputs, first_message))
    first_all = everywhere(first_message)
    second_all = everywhere(tie(second_message, *x_blocks[1:3]))
    grad_out = cotangent.astype(F32) * needle.astype(F32)[:, None]
    dy_near = plane_near(grp, tie(grad_out, x_blocks[3]).astype(BF16))
    first_all = tie(first_all, x_blocks[3], *dy_near[1:])
    qkv_full, out_full, gains_full = call(
        place_first_kernel,
        (
            shaped(PLANE, count, rows, wide),
            shaped(count, rows, width),
            shaped(8, width, dtype=F32),
        ),
        (first_all,),
        scratch=(pltpu.SemaphoreType.DMA((count * (PLANE + 1),)),),
        specs=[ANY],
    )
    qkv_full, out_full = qkv_full.reshape(width, wide), out_full.reshape(LOCAL_Q, width)
    gain_one, gain_two = gains_full[0:1], gains_full[1:2]
    first_term = jnp.exp(jnp.sum(lambdas[0] * lambdas[1]))
    second_term = jnp.exp(jnp.sum(lambdas[2] * lambdas[3]))
    mixing = first_term - second_term + LAMBDA_INIT
    lam = jnp.broadcast_to(mixing, (1, HEAD))
    hg = head_gain.reshape(1, HEAD)

    activations = inputs.astype(F32)
    order = (3, 1, 2, 0)
    normed_one, projected, merged, parts = ([None] * PLANE for _ in range(4))
    for r in order:
        normed_one[r], projected[r], merged[r], parts[r] = call(
            attend_kernel,
            (
                struct((length, width), BF16),
                struct((length, 3 * LOCAL_Q), BF16),
                struct((length, LOCAL_Q), BF16),
                struct((length, width), BF16),
            ),
            (x_blocks[r], gain_one, qkv_full, out_full, lam, hg),
            flops=2 * length * width * 4 * LOCAL_Q,
        )
    dy_blocks = plane_far(grp, dy_near, parts[0])
    residual = activations + add_up(plane_send(grp, parts))
    normed_two = (residual * rms_scale(residual) * gain_two).astype(BF16)

    n2_near = plane_near(grp, normed_two)
    n2_blocks = plane_far(grp, n2_near)
    second_all = tie(second_all, n2_near[1], n2_near[2])
    if tuned:
        gateup_full, down_full = call(
            place_second_kernel,
            (
                shaped(PLANE, count, rows, 2 * LOCAL_FF),
                shaped(count, *down_weight.shape),
            ),
            (second_all, second_all.reshape(count, -1, rows, 2 * LOCAL_FF)),
            scratch=(pltpu.SemaphoreType.DMA((count * 7,)),),
            specs=[ANY] * 2,
        )
        gateup_full, down_full = gateup_full.reshape(width, -1), down_full.reshape(-1, width)
    else:
        gateup_full = second_all.transpose(1, 0, 2, 3).reshape(width, -1)
        down_full = everywhere(down_weight.astype(BF16)).reshape(-1, width)
    y_parts, dn2_parts, hidden, grad_gate_up, dn2_terms = ([None] * PLANE for _ in range(5))
    after = ()
    for pair in ((3, 1), (2, 0)):
        results = call(
            functools.partial(ffn_kernel, 2),
            (
                shaped(length, width),
                shaped(length, width),
                shaped(length, LOCAL_FF),
                shaped(length, 2 * LOCAL_FF),
            )
            * 2,
            (
                *(tie(n2_blocks[r], *after) if after else n2_blocks[r] for r in pair),
                *(dy_blocks[r] for r in pair),
                gateup_full,
                down_full,
            ),
            scratch=(
                pltpu.VMEM((2 * length, LOCAL_FF), BF16),
                pltpu.VMEM((2 * length, 2 * LOCAL_FF), BF16),
            ),
        )
        for i, r in enumerate(pair):
            y_parts[r], dn2_parts[r], hidden[r], grad_gate_up[r] = results[4 * i : 4 * i + 4]
            dn2_terms[r] = grp.plane(dn2_parts[r], r) if r else dn2_parts[r]
        after = (y_parts[1],)
    grad_residual = grad_out + norm_back(add_up(dn2_terms), residual, gain_two)
    gateup_halves = weight_grad(
        grp, [tie(n2_blocks[0], y_parts[0], dn2_terms[3]), *n2_blocks[1:]], grad_gate_up, PLANE
    )
    down_halves = weight_grad(grp, [tie(hidden[0], gateup_halves[0], *dn2_terms[1:3]), *hidden[1:]], dy_blocks, 1)
    if tuned:
        mark, second_sum = spread(
            grp,
            chunk_second_kernel,
            (PLANE * rows + down_weight.shape[0] * 3 // 4, 2 * LOCAL_FF),
            gateup_halves,
            down_halves,
        )
    else:
        mark = down_halves[0]

    dh_near = plane_near(grp, grad_residual.astype(BF16))
    dp_blocks, dn1_parts, stats = ([None] * PLANE for _ in range(3))
    for r in (0, 1, 2, 3):
        if r == 1:
            dh_blocks = plane_far(grp, dh_near)
        block = tie(dh_near[0], mark) if r == 0 else tie(dh_blocks[r], dp_blocks[r - 1])
        dp_blocks[r], dn1_parts[r], stats[r] = call(
            attend_back_kernel,
            (
                struct((length, 3 * LOCAL_Q), BF16),
                struct((length, width), BF16),
                struct((2, HEAD), F32),
            ),
            (
                block,
                projected[r],
                qkv_full,
                out_full,
                lam,
                hg,
            ),
            scratch=(pltpu.VMEM((length, LOCAL_Q), F32),),
            flops=2 * length * width * 5 * LOCAL_Q,
        )
    y_got = plane_scatter_first(grp, [tie(part, dp_blocks[1]) for part in y_parts], 1)
    qkv_halves = weight_grad(grp, normed_one, dp_blocks, PLANE)
    out_halves = weight_grad(grp, merged, dh_blocks, 1)
    y_terms, y_sent = plane_scatter_second(grp, y_parts, 1, tie(y_got, qkv_halves[0]))
    dn1_got = plane_scatter_first(grp, dn1_parts, 2)
    if tuned:
        mark, first_sum = spread(
            grp,
            chunk_first_kernel,
            (rows, PLANE * 3 * LOCAL_Q + width),
            [tie(qkv_halves[0], y_sent), *qkv_halves[1:]],
            out_halves,
        )
    else:
        mark = out_halves[0]
    late = lambda terms, mark: [terms[0]] + [tie(term, mark) for term in terms[1:]]

    if tuned:
        gateup_pieces, down_grad = owner(
            grp,
            owner_second_kernel,
            tie(second_sum, mark),
            (rows, 2 * LOCAL_FF),
            down_weight.shape,
        )
    else:
        down_grad, out_grad = owner_plain(grp, down_halves)[0], owner_plain(grp, out_halves)[0]
        gateup_pieces, qkv_pieces = (
            [
                lax.dynamic_index_in_dim(value, grp.j ^ r, 0, keepdims=False).astype(BF16)
                for r in range(PLANE)
            ]
            for value in (owner_plain(grp, gateup_halves), owner_plain(grp, qkv_halves))
        )
    dn1_terms, dn1_sent = plane_scatter_second(grp, dn1_parts, 2, tie(dn1_got, gateup_pieces[0]))
    stat = grp.everyone(add_up([tie(stats[0], gateup_pieces[0]), *stats[1:]]))
    layer_output = (residual + add_up(late(y_terms, dn1_sent))).astype(BF16)
    *gateup_res, gateup_dot = adam_columns(
        grp, late(exchange(grp, gateup_pieces), layer_output), gateup_weight, gateup_first, gateup_second, 2
    )
    input_grad = grad_residual + norm_back(
        add_up(late(dn1_terms, gateup_dot)), activations, gain_one
    )
    if tuned:
        qkv_pieces, out_grad = owner(
            grp,
            owner_first_kernel,
            tie(first_sum, input_grad, gateup_dot, stat),
            (rows, 3 * LOCAL_Q),
            out_weight.shape,
        )
    *qkv_res, qkv_dot = adam_columns(
        grp, exchange(grp, qkv_pieces), qkv_weight, qkv_first, qkv_second, 3
    )
    total_head, total_mixing = stat[0], stat[1, 0]
    gains_grad = jnp.concatenate([qkv_dot[:1], gateup_dot[:1]]) / gains_low.astype(F32)
    lambdas_grad = jnp.stack(
        [
            total_mixing * first_term * lambdas[1],
            total_mixing * first_term * lambdas[0],
            -total_mixing * second_term * lambdas[3],
            -total_mixing * second_term * lambdas[2],
        ]
    )
    out_res = adam_update(out_weight, out_first, out_second, out_grad, RATE_MATRIX, WEIGHT_DECAY)
    down_res = adam_update(
        down_weight, down_first, down_second, down_grad, RATE_MATRIX, WEIGHT_DECAY
    )
    gains_res = adam_update(norm_gains, gains_first, gains_second, gains_grad, RATE_GAIN, 0.0)
    lambdas_res = adam_update(
        lambdas, lambdas_first, lambdas_second, lambdas_grad, RATE_LAMBDA, 0.0
    )
    head_res = adam_update(head_gain, head_first, head_second, total_head, RATE_GAIN, 0.0)
    return (
        layer_output,
        input_grad,
        *qkv_res,
        *out_res,
        *gateup_res,
        *down_res,
        *gains_res,
        *lambdas_res,
        *head_res,
    )


def solution(mesh):
    members, d = mesh.shape["fsdp"] // PLANE, mesh.shape["dp"]
    inner = Mesh(mesh.devices.reshape(PLANE, members, d), AXES)
    rows, cols, whole = P(AXES, None), P(None, AXES), P()
    return jax.shard_map(
        functools.partial(per_device, members, d),
        mesh=inner,
        in_specs=(rows, rows, P(AXES)) + (rows,) * 12 + (cols,) * 3 + (whole,) * 6,
        out_specs=(rows,) * 14 + (cols,) * 3 + (whole,) * 6,
        check_vma=False,
    )
```

time: 1710 us -> 475 us (0.28)
  waiting for transfers between devices: 1380 us -> 190 us
  Pallas kernels: 0 us -> 151 us
  matrix products: 139 us -> 0 us
  blocking collectives: 109 us -> 0 us
  starting transfers between devices: 0.55 us -> 48.8 us
  local copies, waits for them, and re-layouts: 6.51 us -> 34.8 us
    reduce_scatter x4 -> x2, waiting for transfers between devices: 1070 us -> 0.85 us  [spread(): lax.psum_scatter(message, 'dp', scatter_dimension=0, tiled=False)]
    all_gather x4 -> x2, waiting for transfers between devices: 316 us -> 8.11 us  [the longest x1 8.11 us: per_device(): first_all = everywhere(first_message)]
    ppermute x0 -> x44, waiting for transfers between devices: none -> 181 us  [the longest x35 163 us: plane(): return lax.ppermute(value, 'j', [(i, i ^ r) for i in range(PLANE)])]
    pallas_call x0 -> x24, Pallas kernels: none -> 151 us  [call(): pl.pallas_call(kernel, out_shape=tuple(outs), in_specs=specs or [VMEM] *...]
    dot_general x18 -> x0, matrix products: 139 us -> none  [the longest x4 58.3 us: contract_rows(): lax.dot_general(left, right, (((0,), (0,)), ((), ())), preferred_element_...]
    all_gather x1 -> x0, blocking collectives: 69.7 us -> none  [per_device(): lax.all_gather(shards[4], ('fsdp', 'dp'), axis=0, tiled=True)]
    ppermute x0 -> x44, starting transfers between devices: none -> 48.2 us  [the longest x35 41.5 us: plane(): return lax.ppermute(value, 'j', [(i, i ^ r) for i in range(PLANE)])]
    psum x1 -> x0, blocking collectives: 39 us -> none  [per_device(): lax.psum((grad_mixing, grad_head_gain), ('fsdp', 'dp'))]
  transfers between devices with their start and end apart: 9 -> 48, of which waited for: 8 -> 27; matrix products, arithmetic and copies ran while one was open for 7% -> 6% of each run, Pallas kernels for 0% -> 22%
where the time goes in v1:
time: 475 us; the launch traced here: 469 us
  waiting for transfers between devices  190 us (40%)
  Pallas kernels  151 us (32%)
  starting transfers between devices  48.8 us (10%)
  local copies, waits for them, and re-layouts  34.8 us (7%)
  other arithmetic  26.7 us (6%)
  between operations  17.9 us (4%)
    ppermute x35, waiting for transfers between devices, plane(): return lax.ppermute(value, 'j', [(i, i ^ r) for i in range(PLANE)])  163 us
    pallas_call x24, Pallas kernels, call(): pl.pallas_call(kernel, out_shape=tuple(outs), in_specs=specs or [VMEM] *...  151 us
    ppermute x35, starting transfers between devices, plane(): return lax.ppermute(value, 'j', [(i, i ^ r) for i in range(PLANE)])  41.5 us
    unnamed x226, local copies, waits for them, and re-layouts  31.2 us
    ppermute x5, waiting for transfers between devices, everyone(): value = value + lax.ppermute(value, AXES, [(i, i ^ step) for i in range(n)])  14.9 us
  transfers between devices with their start and end apart: 48, of which 27 were waited for; matrix products, arithmetic and copies ran while one was open for 6% of the time, Pallas kernels for 22%

profile of v1, /device:TPU:0, one launch (start us, length us, event | category | flops | bytes accessed | tf_op | source)
XLA Modules:
  0.0 469.4 jit_solution(14166692649080926692)
XLA Ops:
  16.6 7.0 %collective-permute-done.refs_1_ = bf16[48,3328]{1,0:T(8,128)(2,1)S(1)} collective-permute-done((bf16[48,3328]{1,0:T(8,128)(2,1)}, bf16[48,3328]{1,0:T(8,128)(2,1)S(1)}, u32[]{:S(2)}, u32[]{:S(2)}) %collective-permute-start) | collective-permute-done | bytes 319520 | tf_op jit(solution)/shard_map/ppermute | solution.py:401
  23.6 7.5 %collective-permute-done.1.refs_2_ = bf16[48,3328]{1,0:T(8,128)(2,1)S(1)} collective-permute-done((bf16[48,3328]{1,0:T(8,128)(2,1)}, bf16[48,3328]{1,0:T(8,128)(2,1)S(1)}, u32[]{:S(2)}, u32[]{:S(2)}) %collective-permute-start.1) | collective-permute-done | bytes 319520 | tf_op jit(solution)/shard_map/ppermute | solution.py:401
  35.5 16.1 %collective-permute-done.5.x_ref = bf16[256,1536]{1,0:T(8,128)(2,1)S(1)} collective-permute-done((bf16[256,1536]{1,0:T(8,128)(2,1)S(1)}, bf16[256,1536]{1,0:T(8,128)(2,1)S(1)}, u32[]{:S(2)}, u32[]{:S(2)}) %collective-permute-start.5) | collective-permute-done | bytes 786464 | tf_op jit(solution)/shard_map/ppermute | solution.py:401
  67.1 12.4 %collective-permute-done.8.refs_2_.refs_6_ = bf16[256,1536]{1,0:T(8,128)(2,1)S(1)} collective-permute-done((bf16[256,1536]{1,0:T(8,128)(2,1)S(1)}, bf16[256,1536]{1,0:T(8,128)(2,1)S(1)}, u32[]{:S(2)}, u32[]{:S(2)}) %collective-permute-start.8) | collective-permute-done | bytes 786464 | tf_op jit(solution)/shard_map/ppermute | solution.py:401
  80.7 8.1 %all-gather.5.cloned.1.call-done = bf16[384,6656]{1,0:T(8,128)(2,1)} async-done(((bf16[48,6656]{1,0:T(8,128)(2,1)}), bf16[384,6656]{1,0:T(8,128)(2,1)}) %all-gather.5.cloned.1.call-update) | async-done | bytes 5111824 | tf_op jit(solution)/shard_map/all_gather | solution.py:600
  126.4 13.7 %collective-permute-done.10 = bf16[256,1536]{1,0:T(8,128)(2,1)S(1)} collective-permute-done((bf16[256,1536]{1,0:T(8,128)(2,1)S(1)}, bf16[256,1536]{1,0:T(8,128)(2,1)S(1)}, u32[]{:S(2)}, u32[]{:S(2)}) %collective-permute-start.10) | collective-permute-done | bytes 786464 | tf_op jit(solution)/shard_map/ppermute | solution.py:401
  146.2 15.9 %collective-permute-done.13.refs_1_ = bf16[256,1536]{1,0:T(8,128)(2,1)S(1)} collective-permute-done((bf16[256,1536]{1,0:T(8,128)(2,1)S(1)}, bf16[256,1536]{1,0:T(8,128)(2,1)S(1)}, u32[]{:S(2)}, u32[]{:S(2)}) %collective-permute-start.13) | collective-permute-done | bytes 786464 | tf_op jit(solution)/shard_map/ppermute | solution.py:401
  163.6 8.4 %collective-permute-done.16 = bf16[128,1536]{1,0:T(8,128)(2,1)S(1)} collective-permute-done((bf16[128,1536]{1,0:T(8,128)(2,1)S(1)}, bf16[128,1536]{1,0:T(8,128)(2,1)S(1)}, u32[]{:S(2)}, u32[]{:S(2)}) %collective-permute-start.16) | collective-permute-done | bytes 393248 | tf_op jit(solution)/shard_map/ppermute | solution.py:401
  172.8 6.5 %collective-permute-done.14 = bf16[128,1536]{1,0:T(8,128)(2,1)S(1)} collective-permute-done((bf16[128,1536]{1,0:T(8,128)(2,1)S(1)}, bf16[128,1536]{1,0:T(8,128)(2,1)S(1)}, u32[]{:S(2)}, u32[]{:S(2)}) %collective-permute-start.14) | collective-permute-done | bytes 393248 | tf_op jit(solution)/shard_map/ppermute | solution.py:401
  182.0 6.9 %shard_map.414 = (bf16[4,8,48,2048]{3,2,1,0:T(8,128)(2,1)}, bf16[8,128,1536]{2,1,0:T(8,128)(2,1)S(1)}) custom-call(bf16[8,288,2048]{2,1,0:T(8,128)(2,1)} %bitcast.52, bf16[8,6,48,2048]{3,2,1,0:T(8,128)(2,1)} %bitcast.53), custom_call_target="tpu_custom_call" | custom-call | tf_op jit(solution)/shard_map/pallas_call | solution.py:375
  190.6 14.6 %shard_map.415 = (bf16[256,1536]{1,0:T(8,128)(2,1)S(1)}, bf16[256,1536]{1,0:T(8,128)(2,1)S(1)}, bf16[256,1024]{1,0:T(8,128)(2,1)S(1)}, bf16[256,2048]{1,0:T(8,12...) custom-call(bf16[256,1536]{1,0:T(8,128)(2,1)S(1)} %copy-done.19, ...), custom_call_target="tpu_custom_call" | custom-call | tf_op jit(solution)/shard_map/pallas_call | solution.py:375
  208.5 25.5 %shard_map.416 = (bf16[256,1536]{1,0:T(8,128)(2,1)S(1)}, bf16[256,1536]{1,0:T(8,128)(2,1)S(1)}, bf16[256,1024]{1,0:T(8,128)(2,1)S(1)}, bf16[256,2048]{1,0:T(8,12...) custom-call(bf16[256,1536]{1,0:T(8,128)(2,1)S(1)} %copy-done.15, ...), custom_call_target="tpu_custom_call" | custom-call | tf_op jit(solution)/shard_map/pallas_call | solution.py:375
  237.9 12.0 %shard_map.417 = (bf16[4,192,2048]{2,1,0:T(8,128)(2,1)}, bf16[4,192,2048]{2,1,0:T(8,128)(2,1)}) custom-call(s32[3]{0:T(128)S(1)} %pad_add_fusion.1.pos_ref, bf16[256,1536]{1,0:T(8,128)(2,1)S(1)} %multiply_convert_fusion.refs_1_.refs_0_, bf16[256,1536]{1,0:T(8,128)(2,1)S(1)} %copy-done.13, bf16[256,1536]{1,0:T(8,128)(2,1)S(1)} %copy-done.15, ...), custom_call_target="tpu_custom_call" | custom-call | tf_op jit(solution)/shard_map/pallas_call | solution.py:375
  252.0 17.9 %collective-permute-done.19 = bf16[256,1536]{1,0:T(8,128)(2,1)S(1)} collective-permute-done((bf16[256,1536]{1,0:T(8,128)(2,1)S(1)}, bf16[256,1536]{1,0:T(8,128)(2,1)S(1)}, u32[]{:S(2)}, u32[]{:S(2)}) %collective-permute-start.19) | collective-permute-done | bytes 786464 | tf_op jit(solution)/shard_map/ppermute | solution.py:401
  298.5 16.7 %collective-permute-done.21.dh_ref.refs_5_ = bf16[256,1536]{1,0:T(8,128)(2,1)S(1)} collective-permute-done((bf16[256,1536]{1,0:T(8,128)(2,1)S(1)}, bf16[256,1536]{1,0:T(8,128)(2,1)S(1)}, u32[]{:S(2)}, u32[]{:S(2)}) %collective-permute-start.21) | collective-permute-done | bytes 786464 | tf_op jit(solution)/shard_map/ppermute | solution.py:401
  318.2 7.0 %shard_map.420 = (bf16[256,1152]{1,0:T(8,128)(2,1)S(1)}, bf16[256,1536]{1,0:T(8,128)(2,1)S(1)}, f32[2,128]{1,0:T(2,128)S(1)}) custom-call(bf16[256,1536]{1,0:T(8,128)(2,1)S(1)} %get-tuple-element.178.dh_ref.refs_4_, bf16[256,1152]{1,0:T(8,128)(2,1)S(1)} %copy-done.67, bf16[1536,1280]{1,0:T(8,128)(2,1)} %bitcast.28, bf16[384,1536]{1,0:T(8,128)(2,1)S(1)} %bitcast.36, ...), custom_call_target="tpu_custom_call" | custom-call | tf_op jit(solution)/shard_map/pallas_call | solution.py:375
  325.3 7.3 %shard_map.421 = (bf16[256,1152]{1,0:T(8,128)(2,1)S(1)}, bf16[256,1536]{1,0:T(8,128)(2,1)S(1)}, f32[2,128]{1,0:T(2,128)S(1)}) custom-call(bf16[256,1536]{1,0:T(8,128)(2,1)S(1)} %collective-permute-done.21.dh_ref.refs_5_, bf16[256,1152]{1,0:T(8,128)(2,1)S(1)} %copy-done.65, bf16[1536,1280]{1,0:T(8,128)(2,1)} %bitcast.29, bf16[384,1536]{1,0:T(8,128)(2,1)S(1)} %bitcast.37, ...), custom_call_target="tpu_custom_call" | custom-call | tf_op jit(solution)/shard_map/pallas_call | solution.py:375
  334.9 7.1 %shard_map.422 = (bf16[256,1152]{1,0:T(8,128)(2,1)S(1)}, bf16[256,1536]{1,0:T(8,128)(2,1)S(1)}, f32[2,128]{1,0:T(2,128)S(1)}) custom-call(bf16[256,1536]{1,0:T(8,128)(2,1)S(1)} %collective-permute-done.25.dh_ref.refs_6_, bf16[256,1152]{1,0:T(8,128)(2,1)S(1)} %copy-done.63, bf16[1536,1280]{1,0:T(8,128)(2,1)} %bitcast.30, bf16[384,1536]{1,0:T(8,128)(2,1)S(1)} %bitcast.38, ...), custom_call_target="tpu_custom_call" | custom-call | tf_op jit(solution)/shard_map/pallas_call | solution.py:375
  342.1 7.1 %shard_map.423 = (bf16[256,1152]{1,0:T(8,128)(2,1)S(1)}, bf16[256,1536]{1,0:T(8,128)(2,1)S(1)}, f32[2,128]{1,0:T(2,128)S(1)}) custom-call(bf16[256,1536]{1,0:T(8,128)(2,1)S(1)} %constant_dynamic-update-slice_fusion.6.dh_ref.refs_7_, bf16[256,1152]{1,0:T(8,128)(2,1)S(1)} %copy-done.61, bf16[1536,1280]{1,0:T(8,128)(2,1)} %bitcast.31, ...), custom_call_target="tpu_custom_call" | custom-call | tf_op jit(solution)/shard_map/pallas_call | solution.py:375
  349.3 7.4 %shard_map.424 = (bf16[4,192,1152]{2,1,0:T(8,128)(2,1)}, bf16[4,192,1152]{2,1,0:T(8,128)(2,1)}) custom-call(s32[3]{0:T(128)S(1)} %pad_add_fusion.1.pos_ref, bf16[256,1536]{1,0:T(8,128)(2,1)S(1)} %copy-done.58, bf16[256,1536]{1,0:T(8,128)(2,1)S(1)} %copy-done.56, bf16[256,1536]{1,0:T(8,128)(2,1)S(1)} %copy-done.54, bf16[256,1536]{1,0:T(8,128)(2,1)S(1)} %copy-done.52, ...), custom_call_target="tpu_custom_call" | custom-call | tf_op jit(solution)/shard_map/pallas_call | solution.py:375
  362.6 6.5 %collective-permute-done.24 = bf16[512,1536]{1,0:T(8,128)(2,1)S(1)} collective-permute-done((bf16[512,1536]{1,0:T(8,128)(2,1)}, bf16[512,1536]{1,0:T(8,128)(2,1)S(1)}, u32[]{:S(2)}, u32[]{:S(2)}) %collective-permute-start.24) | collective-permute-done | bytes 1572896 | tf_op jit(solution)/shard_map/ppermute | solution.py:401
  384.1 15.6 %collective-permute-done.28 = bf16[512,1536]{1,0:T(8,128)(2,1)} collective-permute-done((bf16[512,1536]{1,0:T(8,128)(2,1)}, bf16[512,1536]{1,0:T(8,128)(2,1)}, u32[]{:S(2)}, u32[]{:S(2)}) %collective-permute-start.28) | collective-permute-done | bytes 1572896 | tf_op jit(solution)/shard_map/ppermute | solution.py:401
  409.1 6.4 %collective-permute-done.31 = bf16[256,1536]{1,0:T(8,128)(2,1)S(1)} collective-permute-done((bf16[256,1536]{1,0:T(8,128)(2,1)S(1)}, bf16[256,1536]{1,0:T(8,128)(2,1)S(1)}, u32[]{:S(2)}, u32[]{:S(2)}) %collective-permute-start.31) | collective-permute-done | bytes 786464 | tf_op jit(solution)/shard_map/ppermute | solution.py:401
  418.0 11.0 %collective-permute-done.39 = f32[2,128]{1,0:T(2,128)S(1)} collective-permute-done((f32[2,128]{1,0:T(2,128)S(1)}, f32[2,128]{1,0:T(2,128)S(1)}, u32[]{:S(2)}, u32[]{:S(2)}) %collective-permute-start.39) | collective-permute-done | bytes 1056 | tf_op jit(solution)/shard_map/ppermute | solution.py:409
  (378 shorter events, 186.9 us)
Async XLA Ops:
  7.2 81.6 %all-gather.5.cloned.1.call-start = ((), (), s32[]{:S(2)}) async-start(), calls=%async_computation.4 | async-start | bytes 5750784 | tf_op jit(solution)/shard_map/all_gather | solution.py:600
  33.3 148.7 %all-gather.7.cloned.1.call-start = ((), (), s32[]{:S(2)}) async-start(), calls=%async_computation.5 | async-start | bytes 10616832 | tf_op jit(solution)/shard_map/all_gather | solution.py:601
  51.9 321.5 %reduce-scatter.3.cloned.1.call-start = ((), (), s32[]{:S(2)}) async-start(), calls=%async_computation.2 | async-start | bytes 5898240 | tf_op jit(solution)/shard_map/reduce_scatter | solution.py:463
  102.7 23.7 %collective-permute-start.11 = (bf16[256,1536]{1,0:T(8,128)(2,1)S(1)}, bf16[256,1536]{1,0:T(8,128)(2,1)S(1)}, u32[]{:S(2)}, u32[]{:S(2)}) collective-permute-start(bf16[256,1536]{1,0:T(8,128)(2,1)S(1)} %get-tuple-element.148), channel_id=1, source_target_pairs={{0,24},{8,16},{16,8},{24,0},{1,25},{9,17},{17,9},{25,1},{2,26},{10... | collective-permute-start | bytes 2359304 | tf_op jit(solution)/shard_map/ppermute | solution.py:401
  112.2 27.9 %collective-permute-start.10 = (bf16[256,1536]{1,0:T(8,128)(2,1)S(1)}, bf16[256,1536]{1,0:T(8,128)(2,1)S(1)}, u32[]{:S(2)}, u32[]{:S(2)}) collective-permute-start(bf16[256,1536]{1,0:T(8,128)(2,1)S(1)} %get-tuple-element.147), channel_id=1, source_target_pairs={{0,16},{8,24},{16,0},{24,8},{1,17},{9,25},{17,1},{25,9},{2,18},{10... | collective-permute-start | bytes 2359304 | tf_op jit(solution)/shard_map/ppermute | solution.py:401
  120.0 20.2 %collective-permute-start.9 = (bf16[256,1536]{1,0:T(8,128)(2,1)S(1)}, bf16[256,1536]{1,0:T(8,128)(2,1)S(1)}, u32[]{:S(2)}, u32[]{:S(2)}) collective-permute-start(bf16[256,1536]{1,0:T(8,128)(2,1)S(1)} %get-tuple-element.146), channel_id=1, source_target_pairs={{0,8},{8,0},{16,24},{24,16},{1,9},{9,1},{17,25},{25,17},{2,10},{10... | collective-permute-start | bytes 2359304 | tf_op jit(solution)/shard_map/ppermute | solution.py:401
  141.7 20.5 %collective-permute-start.13 = (bf16[256,1536]{1,0:T(8,128)(2,1)S(1)}, bf16[256,1536]{1,0:T(8,128)(2,1)S(1)}, u32[]{:S(2)}, u32[]{:S(2)}) collective-permute-start(bf16[256,1536]{1,0:T(8,128)(2,1)S(1)} %multiply_convert_fusion.refs_1_.refs_0_), channel_id=1, source_target_pairs={{0,8},{8,0},{16,24},{24,16},{1,9},{9,1},{17,25},{25,17},{2,10},{10... | collective-permute-start | bytes 2359304 | tf_op jit(solution)/shard_map/ppermute | solution.py:401
  143.2 28.9 %collective-permute-start.12 = (bf16[256,1536]{1,0:T(8,128)(2,1)S(1)}, bf16[256,1536]{1,0:T(8,128)(2,1)S(1)}, u32[]{:S(2)}, u32[]{:S(2)}) collective-permute-start(bf16[256,1536]{1,0:T(8,128)(2,1)S(1)} %multiply_convert_fusion.refs_1_.refs_0_), channel_id=1, source_target_pairs={{0,16},{8,24},{16,0},{24,8},{1,17},{9,25},{17,1},{25,9},{2,18},{10... | collective-permute-start | bytes 2359304 | tf_op jit(solution)/shard_map/ppermute | solution.py:401
  144.7 27.4 %collective-permute-start.16 = (bf16[128,1536]{1,0:T(8,128)(2,1)S(1)}, bf16[128,1536]{1,0:T(8,128)(2,1)S(1)}, u32[]{:S(2)}, u32[]{:S(2)}) collective-permute-start(bf16[128,1536]{1,0:T(8,128)(2,1)S(1)} %slice.80), channel_id=1, source_target_pairs={{0,16},{8,24},{16,0},{24,8},{1,17},{9,25},{17,1},{25,9},{2,18},{10... | collective-permute-start | bytes 1179656 | tf_op jit(solution)/shard_map/ppermute | solution.py:401
  145.4 27.4 %collective-permute-start.17 = (bf16[128,1536]{1,0:T(8,128)(2,1)S(1)}, bf16[128,1536]{1,0:T(8,128)(2,1)S(1)}, u32[]{:S(2)}, u32[]{:S(2)}) collective-permute-start(bf16[128,1536]{1,0:T(8,128)(2,1)S(1)} %slice.81), channel_id=1, source_target_pairs={{0,8},{8,0},{16,24},{24,16},{1,9},{9,1},{17,25},{25,17},{2,10},{10... | collective-permute-start | bytes 1179656 | tf_op jit(solution)/shard_map/ppermute | solution.py:401
  207.0 28.8 %collective-permute-start.20 = (bf16[256,1536]{1,0:T(8,128)(2,1)S(1)}, bf16[256,1536]{1,0:T(8,128)(2,1)S(1)}, u32[]{:S(2)}, u32[]{:S(2)}) collective-permute-start(bf16[256,1536]{1,0:T(8,128)(2,1)S(1)} %get-tuple-element.163), channel_id=1, source_target_pairs={{0,24},{8,16},{16,8},{24,0},{1,25},{9,17},{17,9},{25,1},{2,26},{10... | collective-permute-start | bytes 2359304 | tf_op jit(solution)/shard_map/ppermute | solution.py:401
  249.9 30.2 %collective-permute-start.22 = (bf16[4,192,2048]{2,1,0:T(8,128)(2,1)}, bf16[4,192,2048]{2,1,0:T(8,128)(2,1)S(1)}, u32[]{:S(2)}, u32[]{:S(2)}) collective-permute-start(bf16[4,192,2048]{2,1,0:T(8,128)(2,1)} %get-tuple-element.170), channel_id=1, source_target_pairs={{0,4},{4,0},{1,5},{5,1},{2,6},{6,2},{3,7},{7,3},{8,12},{12,8},{9,1... | collective-permute-start | bytes 9437192 | tf_op jit(solution)/shard_map/ppermute | solution.py:404
  250.0 20.0 %collective-permute-start.19 = (bf16[256,1536]{1,0:T(8,128)(2,1)S(1)}, bf16[256,1536]{1,0:T(8,128)(2,1)S(1)}, u32[]{:S(2)}, u32[]{:S(2)}) collective-permute-start(bf16[256,1536]{1,0:T(8,128)(2,1)S(1)} %get-tuple-element.162), channel_id=1, source_target_pairs={{0,16},{8,24},{16,0},{24,8},{1,17},{9,25},{17,1},{25,9},{2,18},{10... | collective-permute-start | bytes 2359304 | tf_op jit(solution)/shard_map/ppermute | solution.py:401
  289.4 160.6 %reduce-scatter.5.cloned.1.call-start = ((), (), s32[]{:S(2)}) async-start(), calls=%async_computation.3 | async-start | bytes 2949120 | tf_op jit(solution)/shard_map/reduce_scatter | solution.py:463
  296.9 19.7 %collective-permute-start.25 = (bf16[256,1536]{1,0:T(8,128)(2,1)S(1)}, bf16[256,1536]{1,0:T(8,128)(2,1)S(1)}, u32[]{:S(2)}, u32[]{:S(2)}) collective-permute-start(bf16[256,1536]{1,0:T(8,128)(2,1)S(1)} %get-tuple-element.178.dh_ref.refs_4_), channel_id=1, source_target_pairs={{0,16},{8,24},{16,0},{24,8},{1,17},{9,25},{17,1},{25,9},{2,18},{10... | collective-permute-start | bytes 2359304 | tf_op jit(solution)/shard_map/ppermute | solution.py:401
  333.9 35.3 %collective-permute-start.24 = (bf16[512,1536]{1,0:T(8,128)(2,1)}, bf16[512,1536]{1,0:T(8,128)(2,1)S(1)}, u32[]{:S(2)}, u32[]{:S(2)}) collective-permute-start(bf16[512,1536]{1,0:T(8,128)(2,1)} %pad_maximum_fusion), channel_id=1, source_target_pairs={{0,8},{8,0},{16,24},{24,16},{1,9},{9,1},{17,25},{25,17},{2,10},{10... | collective-permute-start | bytes 4718600 | tf_op jit(solution)/shard_map/ppermute | solution.py:401
  362.1 37.6 %collective-permute-start.28 = (bf16[512,1536]{1,0:T(8,128)(2,1)}, bf16[512,1536]{1,0:T(8,128)(2,1)}, u32[]{:S(2)}, u32[]{:S(2)}) collective-permute-start(bf16[512,1536]{1,0:T(8,128)(2,1)} %pad_maximum_fusion.1), channel_id=1, source_target_pairs={{0,16},{8,24},{16,0},{24,8},{1,17},{9,25},{17,1},{25,9},{2,18},{10... | collective-permute-start | bytes 4718600 | tf_op jit(solution)/shard_map/ppermute | solution.py:401
  379.6 20.1 %collective-permute-start.37 = (f32[2,128]{1,0:T(2,128)S(1)}, f32[2,128]{1,0:T(2,128)S(1)}, u32[]{:S(2)}, u32[]{:S(2)}) collective-permute-start(f32[2,128]{1,0:T(2,128)S(1)} %add.193), channel_id=1, source_target_pairs={{0,2},{1,3},{2,0},{3,1},{4,6},{5,7},{6,4},{7,5},{8,10},{9,11},{10,... | collective-permute-start | bytes 3080 | tf_op jit(solution)/shard_map/ppermute | solution.py:409
  382.5 33.0 %collective-permute-start.31 = (bf16[256,1536]{1,0:T(8,128)(2,1)S(1)}, bf16[256,1536]{1,0:T(8,128)(2,1)S(1)}, u32[]{:S(2)}, u32[]{:S(2)}) collective-permute-start(bf16[256,1536]{1,0:T(8,128)(2,1)S(1)} %copy-done.93), channel_id=1, source_target_pairs={{0,16},{8,24},{16,0},{24,8},{1,17},{9,25},{17,1},{25,9},{2,18},{10... | collective-permute-start | bytes 2359304 | tf_op jit(solution)/shard_map/ppermute | solution.py:401
  404.2 33.5 %collective-permute-start.32 = (bf16[48,2048]{1,0:T(8,128)(2,1)}, bf16[48,2048]{1,0:T(8,128)(2,1)S(1)}, u32[]{:S(2)}, u32[]{:S(2)}) collective-permute-start(bf16[48,2048]{1,0:T(8,128)(2,1)} %get-tuple-element.217), channel_id=1, source_target_pairs={{0,8},{8,0},{16,24},{24,16},{1,9},{9,1},{17,25},{25,17},{2,10},{10... | collective-permute-start | bytes 589832 | tf_op jit(solution)/shard_map/ppermute | solution.py:401
  405.2 39.8 %collective-permute-start.35 = (bf16[256,1536]{1,0:T(8,128)(2,1)}, bf16[256,1536]{1,0:T(8,128)(2,1)}, u32[]{:S(2)}, u32[]{:S(2)}) collective-permute-start(bf16[256,1536]{1,0:T(8,128)(2,1)} %add_convert_fusion.1), channel_id=1, source_target_pairs={{0,8},{8,0},{16,24},{24,16},{1,9},{9,1},{17,25},{25,17},{2,10},{10... | collective-permute-start | bytes 2359304 | tf_op jit(solution)/shard_map/ppermute | solution.py:401
  406.2 22.8 %collective-permute-start.39 = (f32[2,128]{1,0:T(2,128)S(1)}, f32[2,128]{1,0:T(2,128)S(1)}, u32[]{:S(2)}, u32[]{:S(2)}) collective-permute-start(f32[2,128]{1,0:T(2,128)S(1)} %add.195), channel_id=1, source_target_pairs={{0,8},{1,9},{2,10},{3,11},{4,12},{5,13},{6,14},{7,15},{8,0},{9,1},... | collective-permute-start | bytes 3080 | tf_op jit(solution)/shard_map/ppermute | solution.py:409
  415.5 22.1 %collective-permute-start.33 = (bf16[48,2048]{1,0:T(8,128)(2,1)S(1)}, bf16[48,2048]{1,0:T(8,128)(2,1)S(1)}, u32[]{:S(2)}, u32[]{:S(2)}) collective-permute-start(bf16[48,2048]{1,0:T(8,128)(2,1)S(1)} %get-tuple-element.219), channel_id=1, source_target_pairs={{0,16},{8,24},{16,0},{24,8},{1,17},{9,25},{17,1},{25,9},{2,18},{10... | collective-permute-start | bytes 589832 | tf_op jit(solution)/shard_map/ppermute | solution.py:401
  416.0 21.6 %collective-permute-start.34 = (bf16[48,2048]{1,0:T(8,128)(2,1)S(1)}, bf16[48,2048]{1,0:T(8,128)(2,1)S(1)}, u32[]{:S(2)}, u32[]{:S(2)}) collective-permute-start(bf16[48,2048]{1,0:T(8,128)(2,1)S(1)} %get-tuple-element.221), channel_id=1, source_target_pairs={{0,24},{8,16},{16,8},{24,0},{1,25},{9,17},{17,9},{25,1},{2,26},{10... | collective-permute-start | bytes 589832 | tf_op jit(solution)/shard_map/ppermute | solution.py:401
  (136 other events, 1284.8 us)
Sparse Core Ops, SparseCore 0:
  33.4 55.2 all-gather.4
  90.9 89.4 all-gather.6
  289.5 83.8 reduce-scatter.2
  375.6 48.5 reduce-scatter.4

commit v2 on v1

v2 whole, which is shorter than its diff:
```python
import functools

import jax
import jax.numpy as jnp
from jax import lax
from jax.experimental import pallas as pl
from jax.experimental.pallas import tpu as pltpu
from jax.sharding import Mesh
from jax.sharding import PartitionSpec as P

HEADS = 12
HDIM = 64
HEAD = 2 * HDIM
FF = 4096
STEP = 10
PLANE = 4
LOCAL_HEADS = HEADS // PLANE
LOCAL_FF = FF // PLANE
LOCAL_Q = LOCAL_HEADS * HEAD

NORM_EPSILON = 1e-05
LAMBDA_INIT = 0.2
FACTOR = 1.0 - LAMBDA_INIT
BETA_FIRST = 0.9
BETA_SECOND = 0.95
ADAM_EPSILON = 1e-08
WEIGHT_DECAY = 0.1
RATE_MATRIX = 0.02
RATE_GAIN = 0.5
RATE_LAMBDA = 0.15
MASKED = -1000000000.0
SCALE = HDIM ** (-0.5)

BF16 = jnp.bfloat16
F32 = jnp.float32
VMEM_LIMIT = 28 * 1024 * 1024
AXES = ("j", "c", "dp")


def rms_scale(values):
    return lax.rsqrt(jnp.mean(values * values, axis=-1, keepdims=True) + NORM_EPSILON)


def mm(left, right):
    return lax.dot_general(left, right, (((1,), (0,)), ((), ())), preferred_element_type=F32)


def mm_nt(left, right):
    return lax.dot_general(left, right, (((1,), (1,)), ((), ())), preferred_element_type=F32)


def mm_tn(left, right):
    return lax.dot_general(left, right, (((0,), (0,)), ((), ())), preferred_element_type=F32)


def softmax_pair(q, k, rows):
    first = lax.broadcasted_iota(jnp.int32, (rows, HEAD), 1) < HDIM
    allowed = lax.broadcasted_iota(jnp.int32, (rows, rows), 0) >= lax.broadcasted_iota(
        jnp.int32, (rows, rows), 1
    )
    zero = jnp.zeros_like(q)
    result = []
    for half in (jnp.where(first, q, zero), jnp.where(first, zero, q)):
        scores = jnp.where(allowed, mm_nt(half, k) * SCALE, MASKED)
        terms = jnp.exp(scores - jnp.max(scores, axis=-1, keepdims=True))
        result.append(terms * (1.0 / jnp.sum(terms, axis=-1, keepdims=True)))
    return result


def attend_kernel(x_ref, gain_ref, wq_ref, wo_ref, lam_ref, hg_ref, n_ref, p_ref, g_ref, o_ref):
    rows = x_ref.shape[0]
    x = x_ref[...].astype(F32)
    n_ref[...] = (x * rms_scale(x) * gain_ref[...]).astype(BF16)
    for part in range(3):
        cols = pl.ds(part * LOCAL_Q, LOCAL_Q)
        p_ref[:, cols] = mm(n_ref[...], wq_ref[:, cols]).astype(BF16)
    lam = lam_ref[0, 0]
    for head in range(LOCAL_HEADS):
        q, k, v = (
            p_ref[:, pl.ds(part * LOCAL_Q + head * HEAD, HEAD)] for part in range(3)
        )
        a1, a2 = softmax_pair(q, k, rows)
        mixed = (a1 - lam * a2).astype(BF16)
        out = mm(mixed, v)
        g_ref[:, pl.ds(head * HEAD, HEAD)] = (
            out * rms_scale(out) * hg_ref[...] * FACTOR
        ).astype(BF16)
    o_ref[...] = mm(g_ref[...], wo_ref[...]).astype(BF16)


def join(refs):
    return jnp.concatenate([ref[...] for ref in refs], axis=0)


def part_of(refs, value):
    length = refs[0].shape[0]
    for i, ref in enumerate(refs):
        ref[...] = value[i * length : (i + 1) * length]


def down_blocks(rows):
    tall, block = rows * 3 // 4, 512
    cuts = sorted({*range(0, 3 * rows + 1, rows), *range(0, 3 * rows + 1, tall)})
    for at, stop in zip(cuts, cuts[1:]):
        yield at % rows, at // rows * block, at % tall, at // tall * block, stop - at


def pick(pos, pieces, k):
    m = len(pieces)
    value = pieces[0]
    for i in range(1, m):
        value = jnp.where((pos + k) % m == i, pieces[i], value)
    return value


def hidden_kernel(count, m, pos_ref, *refs):
    n_refs, (wgu_ref, h_ref, gate_ref, up_ref, *outs) = refs[:count], refs[count:]
    normed = join(n_refs)
    gate = mm(normed, wgu_ref[:, :LOCAL_FF])
    up = mm(normed, wgu_ref[:, LOCAL_FF:])
    sig = 0.5 * jnp.tanh(0.5 * gate) + 0.5
    silu = gate * sig
    h_ref[...] = (silu * up).astype(BF16)
    gate_ref[...] = (up * (sig + silu * (1.0 - sig))).astype(BF16)
    up_ref[...] = silu.astype(BF16)
    split_columns(m, pos_ref[1], normed, outs)


def split_columns(m, c, value, outs):
    width = value.shape[1] // PLANE
    share = width // m
    for k in range(m):
        columns = []
        for j in range(PLANE):
            pieces = [
                value[:, j * width + i * share : j * width + (i + 1) * share] for i in range(m)
            ]
            columns.append(pick(c, pieces, k))
        outs[k][...] = jnp.concatenate(columns, axis=1)


def hidden_back_kernel(count, *refs):
    dy_refs, (gate_ref, up_ref, wgu_ref, wd_ref, *outs, grad_ref) = refs[:count], refs[count:]
    dh = mm_nt(join(dy_refs), wd_ref[...])
    grad_ref[:, :LOCAL_FF] = (dh * gate_ref[...].astype(F32)).astype(BF16)
    grad_ref[:, LOCAL_FF:] = (dh * up_ref[...].astype(F32)).astype(BF16)
    part_of(outs, mm_nt(grad_ref[...], wgu_ref[...]).astype(BF16))


def down_grad_kernel(count, m, pos_ref, *refs):
    h_refs, dy_refs, outs = refs[:count], refs[count:-m], refs[-m:]
    per = len(dy_refs) // count
    share = outs[0].shape[0]
    for k in range(m):
        cols = pl.ds(pl.multiple_of((pos_ref[1] + k) % m * share, HEAD), share)
        value = sum(
            mm_tn(h_refs[i][:, cols], join(dy_refs[i * per : (i + 1) * per])) for i in range(count)
        )
        outs[k][...] = value.astype(BF16)


def second_grad_kernel(count, down_terms, *refs):
    lefts, rights, downs, out = (
        refs[:count],
        refs[count : 2 * count],
        refs[2 * count : 2 * count + down_terms],
        refs[-1],
    )
    d, tile = out.shape[0], 512
    tall = downs[0].shape[0] // d
    rows = lefts[0].shape[1] // PLANE // d
    for at in range(0, rights[0].shape[1], tile):
        cols = slice(at, at + tile)
        value = sum(mm_tn(left[...], right[:, cols]) for left, right in zip(lefts, rights))
        value = value.astype(BF16)
        for z in range(d):
            for j in range(PLANE):
                start = (j * d + z) * rows
                out[z, j * rows : (j + 1) * rows, cols] = value[start : start + rows]
    for z in range(d):
        value = add_up([term[z * tall : (z + 1) * tall, :] for term in downs]).astype(BF16)
        for row, col, to_row, to_col, size in down_blocks(tall):
            out[z, PLANE * rows + to_row : PLANE * rows + to_row + size, to_col : to_col + 512] = (
                value[row : row + size, col : col + 512]
            )


def down_kernel(count, *refs):
    h_refs, wd_ref, (own_ref, two_ref, message_ref) = refs[:count], refs[count], refs[count + 1 :]
    length = own_ref.shape[0]
    for i, (even_ref, h_ref) in enumerate(zip((own_ref, two_ref), h_refs)):
        value = mm(h_ref[...], wd_ref[...]).astype(BF16)
        even_ref[...] = value[:length]
        message_ref[i * length : (i + 1) * length, :] = value[length:]


def attend_back_kernel(
    dh_ref, p_ref, wq_ref, wo_ref, lam_ref, hg_ref, dp_ref, dn_ref, stat_ref, dg_ref
):
    rows = dh_ref.shape[0]
    dg_ref[...] = mm_nt(dh_ref[...], wo_ref[...])
    lam = lam_ref[0, 0]
    hg = hg_ref[...]
    first = lax.broadcasted_iota(jnp.int32, (rows, HEAD), 1) < HDIM
    grad_hg = jnp.zeros((1, HEAD), F32)
    grad_lam = jnp.zeros((1, 1), F32)
    for head in range(LOCAL_HEADS):
        q, k, v = (
            p_ref[:, pl.ds(part * LOCAL_Q + head * HEAD, HEAD)] for part in range(3)
        )
        a1, a2 = softmax_pair(q, k, rows)
        mixed = (a1 - lam * a2).astype(BF16)
        out = mm(mixed, v)
        scale = rms_scale(out)
        unit = out * scale
        dg = dg_ref[:, pl.ds(head * HEAD, HEAD)]
        grad_hg = grad_hg + FACTOR * jnp.sum(dg * unit, axis=0, keepdims=True)
        u = dg * hg * FACTOR
        dout = (scale * (u - unit * jnp.mean(u * unit, axis=-1, keepdims=True))).astype(BF16)
        dv = mm_tn(mixed, dout)
        dm = mm_nt(dout, v)
        dot1 = jnp.sum(dm * a1, axis=-1, keepdims=True)
        dot2 = jnp.sum(dm * a2, axis=-1, keepdims=True)
        grad_lam = grad_lam - jnp.sum(dot2, axis=0, keepdims=True)
        ds1 = (a1 * (dm - dot1)).astype(BF16)
        ds2 = (-lam * a2 * (dm - dot2)).astype(BF16)
        dq = jnp.where(first, mm(ds1, k), mm(ds2, k)) * SCALE
        dk = jnp.where(first, mm_tn(ds1, q), mm_tn(ds2, q)) * SCALE
        for part, value in enumerate((dq, dk, dv)):
            dp_ref[:, pl.ds(part * LOCAL_Q + head * HEAD, HEAD)] = value.astype(BF16)
    stat_ref[0:1, :] = grad_hg
    stat_ref[1:2, :] = jnp.broadcast_to(grad_lam, (1, HEAD))
    dn_ref[...] = mm_nt(dp_ref[...], wq_ref[:, : 3 * LOCAL_Q]).astype(BF16)


def split_kernel(parts, pos_ref, w_ref, *refs):
    gain_refs, outs = refs[:-PLANE], refs[-PLANE:]
    width = w_ref.shape[1] // parts
    quarter = width // PLANE
    rows = w_ref.shape[0]
    for r, out in enumerate(outs):
        q = pos_ref[0] ^ r
        for part in range(parts):
            cols = pl.ds(pl.multiple_of(part * width + q * quarter, HEAD), quarter)
            out[:, part * quarter : (part + 1) * quarter] = w_ref[:, cols].astype(BF16)
        for gain_ref in gain_refs:
            gains = jnp.concatenate([gain_ref[...], jnp.zeros((HEAD - 2, rows), F32)], axis=0).T
            out[:, parts * quarter :] = gains.astype(BF16)


def message_kernel(slot_ref, *refs):
    pieces, (weight_ref, out_ref, sem) = refs[:PLANE], refs[PLANE:]
    wide = pieces[0].shape[1]
    copies = []
    for r in range(PLANE):
        cols = pl.ds(pl.multiple_of(slot_ref[r] * wide, HEAD), wide)
        copies.append((pieces[r], out_ref.at[:, cols]))
    copy_all(copies, sem, lambda: store_low(out_ref, PLANE * wide, weight_ref))


def stack_kernel(slot_ref, *refs):
    pieces, (out_ref, sem) = refs[:PLANE], refs[PLANE:]
    copy_all([(pieces[r], out_ref.at[slot_ref[r]]) for r in range(PLANE)], sem)


def store_low(out_ref, start, in_ref):
    out_ref[:, start:] = in_ref[...].astype(BF16)


def copy_all(pairs, sem, meanwhile=lambda: None):
    copies = [pltpu.make_async_copy(a, b, sem.at[i]) for i, (a, b) in enumerate(pairs)]
    for copy in copies:
        copy.start()
    meanwhile()
    for copy in copies:
        copy.wait()


def place_second_kernel(in_ref, out_ref, sem):
    copy_all([(in_ref.at[k], out_ref.at[:, k]) for k in range(in_ref.shape[0])], sem)


def place_first_kernel(in_ref, qkv_ref, out_ref, gain_ref, sem):
    count, (rows, wide) = in_ref.shape[0], qkv_ref.shape[2:]
    copies = []
    for k in range(count):
        for j in range(PLANE):
            copies.append((in_ref.at[k, :, pl.ds(j * wide, wide)], qkv_ref.at[j, k]))
        copies.append((in_ref.at[k, :, pl.ds(PLANE * wide, out_ref.shape[2])], out_ref.at[k]))
    copy_all(copies, sem)
    columns = qkv_ref[:, :, :, 3 * LOCAL_Q :].astype(F32).reshape(PLANE * count * rows, HEAD)
    gain_ref[...] = columns.T[:8]


def weight_grad_kernel(m, pos_ref, *refs):
    lefts, rights, outs = refs[:PLANE], refs[PLANE : 2 * PLANE], refs[2 * PLANE : 2 * PLANE + m]
    left, right, total, sem = refs[2 * PLANE + m :]
    length = lefts[0].shape[0]
    copies = []
    for r in range(PLANE):
        for i, (src, dst) in enumerate(((lefts[r], left), (rights[r], right))):
            copies.append(
                pltpu.make_async_copy(
                    src, dst.at[pl.ds(r * length, length)], sem.at[2 * r + i]
                )
            )
            copies[-1].start()
    for copy in copies:
        copy.wait()
    rows, columns = total.shape
    share = rows // m
    for lead in range(outs[0].shape[0]):
        value = mm_tn(left[:, lead * rows : (lead + 1) * rows], right[...])
        if m == 2:
            top, low = value[:share].astype(BF16), value[share:].astype(BF16)
            outs[0][lead] = jnp.where(pos_ref[1] == 0, top, low)
            outs[1][lead] = jnp.where(pos_ref[1] == 0, low, top)
        else:
            total[...] = value
            for k in range(m):
                start = pl.multiple_of(((pos_ref[1] + k) % m) * share, 8)
                outs[k][lead] = total[pl.ds(start, share), :].astype(BF16)


def chunk_first_kernel(m, *refs):
    qkv, out_terms, out = refs[:m], refs[m : 2 * m], refs[2 * m]
    d, rows, _ = out.shape
    wide = qkv[0].shape[2]
    for z in range(d):
        for j in range(PLANE + 1):
            terms, lead = (qkv, j) if j < PLANE else (out_terms, 0)
            value = add_up([term[lead, z * rows : (z + 1) * rows, :] for term in terms])
            out[z, :, j * wide : j * wide + value.shape[1]] = value.astype(BF16)


def owner_first_kernel(pos_ref, in_ref, *outs):
    *outs, out_ref = outs
    wide = outs[0].shape[1]
    for r in range(PLANE):
        outs[r][...] = in_ref[:, pl.ds(pl.multiple_of((pos_ref[0] ^ r) * wide, HEAD), wide)]
    out_ref[...] = in_ref[:, PLANE * wide :].astype(F32)


def owner_second_kernel(pos_ref, in_ref, *outs):
    *outs, down_ref = outs
    rows, tall = outs[0].shape[0], down_ref.shape[0]
    for r in range(PLANE):
        q = pos_ref[0] ^ r
        if rows % 16 == 0:
            outs[r][...] = in_ref[pl.ds(pl.multiple_of(q * rows, 16), rows), :]
        else:
            outs[r][...] = pick(q, [in_ref[i * rows : (i + 1) * rows, :] for i in range(PLANE)], 0)
    for row, col, to_row, to_col, size in down_blocks(tall):
        down_ref[row : row + size, col : col + 512] = in_ref[
            PLANE * rows + to_row : PLANE * rows + to_row + size, to_col : to_col + 512
        ].astype(F32)


def adam_columns_kernel(parts, width, pos_ref, *refs):
    pieces, (w_ref, f_ref, s_ref, wn_ref, fn_ref, sn_ref, dot_ref) = refs[:PLANE], refs[PLANE:]
    quarter = width // PLANE
    dot = jnp.zeros((w_ref.shape[0], 1), F32)
    for r in range(PLANE):
        q = pos_ref[0] ^ r
        for part in range(parts):
            cols = pl.ds(pl.multiple_of(part * width + q * quarter, HEAD), quarter)
            grad = pieces[r][:, part * quarter : (part + 1) * quarter].astype(F32)
            weight = w_ref[:, cols]
            dot = dot + jnp.sum(weight.astype(BF16).astype(F32) * grad, axis=1, keepdims=True)
            wn_ref[:, cols], fn_ref[:, cols], sn_ref[:, cols] = adam_update(
                weight, f_ref[:, cols], s_ref[:, cols], grad, RATE_MATRIX, WEIGHT_DECAY
            )
    dot_ref[...] = jnp.broadcast_to(dot, (dot.shape[0], HEAD)).T[:8]


ANY = pl.BlockSpec(memory_space=pl.ANY)
VMEM = pl.BlockSpec(memory_space=pltpu.VMEM)
SMEM = pl.BlockSpec(memory_space=pltpu.SMEM)


COSTS = {
    split_kernel: 1.0,
    message_kernel: 1.5,
    stack_kernel: 1.0,
    place_first_kernel: 2.0,
    attend_kernel: 3.5,
    place_second_kernel: 3.0,
    hidden_kernel: 5.0,
    down_grad_kernel: 4.0,
    hidden_back_kernel: 5.0,
    second_grad_kernel: 7.5,
    down_kernel: 4.5,
    attend_back_kernel: 5.0,
    weight_grad_kernel: 5.0,
    chunk_first_kernel: 2.0,
    owner_first_kernel: 1.0,
    owner_second_kernel: 1.0,
    adam_columns_kernel: 4.0,
}


def call(kernel, outs, operands, scratch=(), flops=0, specs=None, out_spec=VMEM):
    size = sum(a.size * a.dtype.itemsize for a in operands) + sum(
        o.size * o.dtype.itemsize for o in outs
    )
    return pl.pallas_call(
        kernel,
        out_shape=tuple(outs),
        in_specs=specs or [VMEM] * len(operands),
        out_specs=(out_spec,) * len(outs),
        scratch_shapes=list(scratch),
        compiler_params=pltpu.CompilerParams(vmem_limit_bytes=VMEM_LIMIT),
        cost_estimate=pl.CostEstimate(flops=int(COSTS[getattr(kernel, "func", kernel)] * 1.15e9), bytes_accessed=0, transcendentals=0),
    )(*operands)


def shaped(*shape, dtype=BF16):
    return jax.ShapeDtypeStruct(shape, dtype)


def tie(value, *after):
    return lax.optimization_barrier((value, *after))[0]


class Group:
    def __init__(self, m, d):
        self.m, self.d = m, d
        self.j, self.c, self.z = (lax.axis_index(axis) for axis in AXES)
        self.pos = jnp.stack([self.j, self.c, self.z]).astype(jnp.int32)

    def plane(self, value, r):
        return lax.ppermute(value, "j", [(i, i ^ r) for i in range(PLANE)])

    def core(self, value, k):
        return lax.ppermute(value, "c", [(i, (i + k) % self.m) for i in range(self.m)])

    def everyone(self, value, step):
        n = PLANE * self.m * self.d
        return value + lax.ppermute(value, AXES, [(i, i ^ step) for i in range(n)])


def plane_near(grp, own):
    return [own, grp.plane(own, 1), grp.plane(own, 2)]


def plane_far(grp, near, *after):
    own, one, two = near
    half = own.shape[0] // 2
    top, low = grp.plane(one[:half], 2), grp.plane(two[half:], 1)
    if after:
        top, low = tie(top, *after), tie(low, *after)
    return [own, one, two, jnp.concatenate([top, low], axis=0)]


def plane_gather(grp, own):
    return plane_far(grp, plane_near(grp, own))


def plane_send(grp, parts):
    return [parts[0]] + [grp.plane(parts[r], r) for r in range(1, PLANE)]


def plane_scatter_second(grp, part, axis, got):
    sent = add_up([part, got[part.shape[0] :]]).astype(BF16)
    return sent, grp.plane(sent, 3 - axis)


def add_up(terms):
    return sum(term.astype(F32) for term in terms)


def exchange(grp, pieces):
    return [pieces[0]] + [grp.plane(pieces[r], r) for r in range(1, PLANE)]


def core_terms(grp, halves):
    return [halves[0]] + [grp.core(halves[k], k) for k in range(1, grp.m)]


def owner(grp, kernel, message, piece, rest=()):
    return call(
        kernel,
        (shaped(*piece),) * PLANE + rest,
        (grp.pos, message),
        specs=[SMEM, VMEM],
    )


def weight_grad(grp, lefts, rights, lead):
    length, rows = lefts[0].shape
    columns = rights[0].shape[1]
    share = rows // lead // grp.m
    return call(
        functools.partial(weight_grad_kernel, grp.m),
        (shaped(lead, share, columns),) * grp.m,
        (grp.pos, *lefts, *rights),
        scratch=(
            pltpu.VMEM((PLANE * length, rows), BF16),
            pltpu.VMEM((PLANE * length, columns), BF16),
            pltpu.VMEM((rows // lead, columns), F32),
            pltpu.SemaphoreType.DMA((2 * PLANE,)),
        ),
        specs=[SMEM] + [ANY] * (2 * PLANE),
        flops=2 * PLANE * length * rows * columns,
    )


def adam_columns(grp, pieces, weight, first, second, parts):
    rows, columns = weight.shape
    return call(
        functools.partial(adam_columns_kernel, parts, columns // parts),
        (shaped(rows, columns, dtype=F32),) * 3 + (shaped(8, rows, dtype=F32),),
        (grp.pos, *pieces, weight, first, second),
        specs=[SMEM] + [VMEM] * (PLANE + 3),
    )


def norm_back(grad_normed, values, gain):
    scale_rows = rms_scale(values)
    scaled = grad_normed * gain
    unit_rows = values * scale_rows
    return scale_rows * (
        scaled - unit_rows * jnp.mean(scaled * unit_rows, axis=-1, keepdims=True)
    )


def adam_update(weight, first, second, grad, rate, decay):
    first_new = BETA_FIRST * first + (1.0 - BETA_FIRST) * grad
    second_new = BETA_SECOND * second + (1.0 - BETA_SECOND) * grad * grad
    corrected_first = first_new / (1.0 - BETA_FIRST**STEP)
    corrected_second = second_new / (1.0 - BETA_SECOND**STEP)
    weight_new = weight - rate * (
        corrected_first / (jnp.sqrt(corrected_second) + ADAM_EPSILON) + decay * weight
    )
    return (weight_new, first_new, second_new)


def per_device(
    members,
    d,
    inputs,
    cotangent,
    needle,
    qkv_weight,
    qkv_first,
    qkv_second,
    out_weight,
    out_first,
    out_second,
    gateup_weight,
    gateup_first,
    gateup_second,
    down_weight,
    down_first,
    down_second,
    norm_gains,
    gains_first,
    gains_second,
    lambdas,
    lambdas_first,
    lambdas_second,
    head_gain,
    head_first,
    head_second,
):
    grp = Group(members, d)
    length, width = inputs.shape
    rows = qkv_weight.shape[0]

    gains_low = norm_gains.astype(BF16)
    plane_slots = jnp.stack([grp.j ^ r for r in range(PLANE)]).astype(jnp.int32)
    wide = 3 * LOCAL_Q + HEAD
    count = members * d
    everywhere = functools.partial(lax.all_gather, axis_name=("c", "dp"), axis=0, tiled=False)
    to_owner = functools.partial(lax.psum_scatter, axis_name="dp", scatter_dimension=0, tiled=False)
    late = lambda terms, *marks: [terms[0]] + [tie(term, *marks) for term in terms[1:]]
    first_quarters = call(
        functools.partial(split_kernel, 3),
        (shaped(rows, wide),) * PLANE,
        (grp.pos, qkv_weight, norm_gains),
        specs=[SMEM] + [VMEM] * 2,
    )
    first_message = call(
        message_kernel,
        (shaped(rows, PLANE * wide + width),),
        (plane_slots, *exchange(grp, first_quarters), out_weight),
        scratch=(pltpu.SemaphoreType.DMA((PLANE,)),),
        specs=[SMEM] + [ANY] * PLANE + [VMEM],
    )[0]
    second_quarters = call(
        functools.partial(split_kernel, 2),
        (shaped(rows, 2 * LOCAL_FF),) * PLANE,
        (grp.pos, tie(gateup_weight, first_quarters[0])),
        specs=[SMEM, VMEM],
    )
    second_message = call(
        stack_kernel,
        (shaped(PLANE, rows, 2 * LOCAL_FF),),
        (plane_slots, *exchange(grp, second_quarters)),
        scratch=(pltpu.SemaphoreType.DMA((PLANE,)),),
        specs=[SMEM] + [ANY] * PLANE,
    )[0]
    first_all = everywhere(first_message)
    x_near = plane_near(grp, tie(inputs, first_message))
    second_all = everywhere(tie(second_message, *x_near[1:]))
    x_blocks = plane_far(grp, x_near)
    down_all = everywhere(tie(down_weight, x_blocks[3]).astype(BF16))
    grad_out = cotangent.astype(F32) * needle.astype(F32)[:, None]
    dy_blocks = plane_gather(grp, tie(grad_out, x_blocks[3]).astype(BF16))
    qkv_full, out_full, gains_full = call(
        place_first_kernel,
        (
            shaped(PLANE, count, rows, wide),
            shaped(count, rows, width),
            shaped(8, width, dtype=F32),
        ),
        (tie(first_all, *dy_blocks[1:]),),
        scratch=(pltpu.SemaphoreType.DMA((count * (PLANE + 1),)),),
        specs=[ANY],
    )
    qkv_full, out_full = qkv_full.reshape(width, wide), out_full.reshape(LOCAL_Q, width)
    gain_one, gain_two = gains_full[0:1], gains_full[1:2]
    first_term = jnp.exp(jnp.sum(lambdas[0] * lambdas[1]))
    second_term = jnp.exp(jnp.sum(lambdas[2] * lambdas[3]))
    mixing = first_term - second_term + LAMBDA_INIT
    lam = jnp.broadcast_to(mixing, (1, HEAD))
    hg = head_gain.reshape(1, HEAD)

    activations = inputs.astype(F32)
    normed_one, projected, merged, parts = ([None] * PLANE for _ in range(4))
    for r in (3, 1, 2, 0):
        normed_one[r], projected[r], merged[r], parts[r] = call(
            attend_kernel,
            (
                shaped(length, width),
                shaped(length, 3 * LOCAL_Q),
                shaped(length, LOCAL_Q),
                shaped(length, width),
            ),
            (x_blocks[r], gain_one, qkv_full, out_full, lam, hg),
        )
    residual = activations + add_up(plane_send(grp, parts))
    normed_two = (residual * rms_scale(residual) * gain_two).astype(BF16)

    n2_near = plane_near(grp, normed_two)
    gateup_full = call(
        place_second_kernel,
        (shaped(PLANE, count, rows, 2 * LOCAL_FF),),
        (tie(second_all, normed_two),),
        scratch=(pltpu.SemaphoreType.DMA((count,)),),
        specs=[ANY],
    )[0].reshape(width, -1)
    n2_near[1:] = [tie(block, gateup_full) for block in n2_near[1:]]
    pairs = ((0, 1), (2, 3))
    flat = lambda lists: [item for items in lists for item in items]
    hidden, gate_factor, up_factor, lefts = ([] for _ in range(4))
    n2_blocks = n2_near
    for pair in pairs:
        if pair[1] == 3:
            n2_blocks = plane_far(grp, n2_near, hidden[0])
        h, gate, up, *columns = call(
            functools.partial(hidden_kernel, 2, members),
            (shaped(2 * length, LOCAL_FF),) * 3
            + (shaped(2 * length, width // members),) * members,
            (grp.pos, *(n2_blocks[r] for r in pair), gateup_full),
            specs=[SMEM] + [VMEM] * 3,
        )
        hidden.append(h)
        gate_factor.append(gate)
        up_factor.append(up)
        lefts.append(core_terms(grp, columns))

    down_halves = call(
        functools.partial(down_grad_kernel, 2, members),
        (shaped(LOCAL_FF // members, width),) * members,
        (grp.pos, *hidden, *dy_blocks),
        specs=[SMEM] + [VMEM] * (2 + PLANE),
    )
    down_full = tie(down_all, down_halves[0]).reshape(LOCAL_FF, width)
    dn2_terms, rights = [None] * PLANE, [None] * 2
    for i in (1, 0):
        pair = pairs[i]
        *sent, grad = call(
            functools.partial(hidden_back_kernel, 2),
            (shaped(length, width),) * 2 + (shaped(2 * length, 2 * LOCAL_FF),),
            (
                *(dy_blocks[r] for r in pair),
                tie(gate_factor[i], *flat(lefts)) if i else gate_factor[i],
                up_factor[i],
                gateup_full,
                down_full,
            ),
        )
        rights[i] = [grad] + [grp.core(grad, k) for k in range(1, members)]
        for r, block in zip(pair, sent):
            dn2_terms[r] = grp.plane(block, r) if r else block
    down_terms = core_terms(grp, down_halves)
    second_message = call(
        functools.partial(second_grad_kernel, 2 * members, members),
        (shaped(d, PLANE * rows + down_weight.shape[0] * 3 // 4, 2 * LOCAL_FF),),
        (*flat(lefts), *flat(rights), *down_terms),
    )[0]
    second_sum = to_owner(second_message)
    grad_residual = grad_out + norm_back(add_up(dn2_terms), residual, gain_two)

    dh_near = plane_near(grp, grad_residual.astype(BF16))
    dh_blocks = plane_far(grp, dh_near)
    y_parts = call(
        functools.partial(down_kernel, 2),
        (shaped(length, width),) * 2 + (shaped(2 * length, width),),
        (*hidden, tie(down_full, grad_residual)),
    )
    dp_blocks, dn1_parts, stats = ([None] * PLANE for _ in range(3))
    for r in range(PLANE):
        block = tie(dh_blocks[r], dp_blocks[r - 1] if r else y_parts[0])
        dp_blocks[r], dn1_parts[r], stats[r] = call(
            attend_back_kernel,
            (
                shaped(length, 3 * LOCAL_Q),
                shaped(length, width),
                shaped(2, HEAD, dtype=F32),
            ),
            (block, projected[r], qkv_full, out_full, lam, hg),
            scratch=(pltpu.VMEM((length, LOCAL_Q), F32),),
        )
    y_got = grp.plane(tie(y_parts[2], dp_blocks[0]), 1)
    qkv_halves = weight_grad(grp, normed_one, dp_blocks, PLANE)
    out_halves = weight_grad(grp, merged, dh_blocks, 1)
    half = PLANE * count // 2
    stat = grp.everyone(add_up(stats), half)
    dn1_got = grp.plane(tie(jnp.concatenate([dn1_parts[2], dn1_parts[3]], axis=0), stat), 2)
    step = half // 4
    while step:
        stat = grp.everyone(stat, step)
        step //= 2
    first_chunks = call(
        functools.partial(chunk_first_kernel, members),
        (shaped(d, rows, PLANE * 3 * LOCAL_Q + width),),
        (*core_terms(grp, qkv_halves), *core_terms(grp, out_halves)),
    )[0]
    first_sum = to_owner(first_chunks)

    *gateup_pieces, down_grad = owner(
        grp,
        owner_second_kernel,
        tie(second_sum, first_chunks),
        (rows, 2 * LOCAL_FF),
        (shaped(*down_weight.shape, dtype=F32),),
    )
    gateup_pieces = exchange(grp, gateup_pieces)
    y_got = tie(y_got, gateup_pieces[0])
    y_sent, y_last = plane_scatter_second(grp, y_parts[1], 1, y_got)
    dn1_got = tie(dn1_got, y_sent)
    dn1_sent, dn1_last = plane_scatter_second(grp, dn1_parts[1], 2, dn1_got)
    *gateup_res, gateup_dot = adam_columns(
        grp, late(gateup_pieces, dn1_sent), gateup_weight, gateup_first, gateup_second, 2
    )
    y_got, y_last = tie(y_got, gateup_dot), tie(y_last, gateup_dot)
    layer_output = (residual + add_up([y_parts[0], y_got[:length], y_last])).astype(BF16)
    stat = grp.everyone(tie(stat, dn1_sent), half // 2)
    dn1_got, dn1_last = tie(dn1_got, layer_output), tie(dn1_last, layer_output)
    input_grad = grad_residual + norm_back(
        add_up([dn1_parts[0], dn1_got[:length], dn1_last]), activations, gain_one
    )
    *qkv_pieces, out_grad = owner(
        grp,
        owner_first_kernel,
        tie(first_sum, input_grad, stat),
        (rows, 3 * LOCAL_Q),
        (shaped(*out_weight.shape, dtype=F32),),
    )
    *qkv_res, qkv_dot = adam_columns(
        grp, exchange(grp, qkv_pieces), qkv_weight, qkv_first, qkv_second, 3
    )
    total_head, total_mixing = stat[0], stat[1, 0]
    gains_grad = jnp.concatenate([qkv_dot[:1], gateup_dot[:1]]) / gains_low.astype(F32)
    lambdas_grad = jnp.stack(
        [
            total_mixing * first_term * lambdas[1],
            total_mixing * first_term * lambdas[0],
            -total_mixing * second_term * lambdas[3],
            -total_mixing * second_term * lambdas[2],
        ]
    )
    out_res = adam_update(out_weight, out_first, out_second, out_grad, RATE_MATRIX, WEIGHT_DECAY)
    down_res = adam_update(
        down_weight, down_first, down_second, down_grad, RATE_MATRIX, WEIGHT_DECAY
    )
    gains_res = adam_update(norm_gains, gains_first, gains_second, gains_grad, RATE_GAIN, 0.0)
    lambdas_res = adam_update(
        lambdas, lambdas_first, lambdas_second, lambdas_grad, RATE_LAMBDA, 0.0
    )
    head_res = adam_update(head_gain, head_first, head_second, total_head, RATE_GAIN, 0.0)
    return (
        layer_output,
        input_grad,
        *qkv_res,
        *out_res,
        *gateup_res,
        *down_res,
        *gains_res,
        *lambdas_res,
        *head_res,
    )


def solution(mesh):
    members, d = mesh.shape["fsdp"] // PLANE, mesh.shape["dp"]
    inner = Mesh(mesh.devices.reshape(PLANE, members, d), AXES)
    rows, cols, whole = P(AXES, None), P(None, AXES), P()
    return jax.shard_map(
        functools.partial(per_device, members, d),
        mesh=inner,
        in_specs=(rows, rows, P(AXES)) + (rows,) * 12 + (cols,) * 3 + (whole,) * 6,
        out_specs=(rows,) * 14 + (cols,) * 3 + (whole,) * 6,
        check_vma=False,
    )
```

time: 475 us -> 426 us (0.90)
  Pallas kernels: 151 us -> 98.3 us
  local copies, waits for them, and re-layouts: 34.8 us -> 51.2 us
  waiting for transfers between devices: 190 us -> 179 us
    pallas_call x24 -> x28, Pallas kernels: 151 us -> 98.3 us  [call(): pl.pallas_call(kernel, out_shape=tuple(outs), in_specs=specs or [VMEM] *...]
    unnamed x226 -> x221, local copies, waits for them, and re-layouts: 31.2 us -> 45.8 us
    ppermute x35 -> x38, waiting for transfers between devices: 163 us -> 149 us  [plane(): return lax.ppermute(value, 'j', [(i, i ^ r) for i in range(PLANE)])]
    all_gather x1, waiting for transfers between devices: 8.11 us -> 0.01 us  [per_device(): first_all = everywhere(first_message)]
    all_gather x1 -> x2, waiting for transfers between devices: 0.01 us -> 5.22 us  [the longest x1 5.22 us: per_device(): second_all = everywhere(tie(second_message, *x_near[1:]))]
    ppermute x35 -> x38, starting transfers between devices: 41.5 us -> 39.6 us  [plane(): return lax.ppermute(value, 'j', [(i, i ^ r) for i in range(PLANE)])]
  transfers between devices with their start and end apart: 48 -> 55, of which waited for: 27 -> 30; matrix products, arithmetic and copies ran while one was open for 6% -> 8% of each run, Pallas kernels for 22% -> 20%
where the time goes in v2:
time: 426 us; the launch traced here: 423 us
  waiting for transfers between devices  179 us (42%)
  Pallas kernels  98.3 us (23%)
  local copies, waits for them, and re-layouts  51.2 us (12%)
  starting transfers between devices  47.4 us (11%)
  other arithmetic  27.8 us (7%)
  between operations  18.5 us (4%)
    ppermute x38, waiting for transfers between devices, plane(): return lax.ppermute(value, 'j', [(i, i ^ r) for i in range(PLANE)])  149 us
    pallas_call x28, Pallas kernels, call(): pl.pallas_call(kernel, out_shape=tuple(outs), in_specs=specs or [VMEM] *...  98.3 us
    unnamed x221, local copies, waits for them, and re-layouts  45.8 us
    ppermute x38, starting transfers between devices, plane(): return lax.ppermute(value, 'j', [(i, i ^ r) for i in range(PLANE)])  39.6 us
    ppermute x5, waiting for transfers between devices, everyone(): return value + lax.ppermute(value, AXES, [(i, i ^ step) for i in range(n)])  19.1 us
  transfers between devices with their start and end apart: 55, of which 30 were waited for; matrix products, arithmetic and copies ran while one was open for 8% of the time, Pallas kernels for 20%

profile of v2, /device:TPU:0, one launch (start us, length us, event | category | flops | bytes accessed | tf_op | source)
XLA Modules:
  0.0 422.5 jit_solution(6311501283080028183)
XLA Ops:
  29.6 16.9 %collective-permute-done.15.refs_1_ = bf16[48,2048]{1,0:T(8,128)(2,1)S(1)} collective-permute-done((bf16[48,2048]{1,0:T(8,128)(2,1)S(1)}, bf16[48,2048]{1,0:T(8,128)(2,1)S(1)}, u32[]{:S(2)}, u32[]{:S(2)}) %collective-permute-start.15) | collective-permute-done | bytes 196640 | tf_op jit(solution)/shard_map/ppermute | solution.py:432
  55.9 6.8 %collective-permute-done.4 = bf16[128,1536]{1,0:T(8,128)(2,1)S(1)} collective-permute-done((bf16[128,1536]{1,0:T(8,128)(2,1)S(1)}, bf16[128,1536]{1,0:T(8,128)(2,1)S(1)}, u32[]{:S(2)}, u32[]{:S(2)}) %collective-permute-start.4) | collective-permute-done | bytes 393248 | tf_op jit(solution)/shard_map/ppermute | solution.py:432
  64.7 15.1 %collective-permute-done.7.refs_3_.refs_1_ = bf16[256,1536]{1,0:T(8,128)(2,1)S(1)} collective-permute-done((bf16[256,1536]{1,0:T(8,128)(2,1)S(1)}, bf16[256,1536]{1,0:T(8,128)(2,1)S(1)}, u32[]{:S(2)}, u32[]{:S(2)}) %collective-permute-start.7) | collective-permute-done | bytes 786464 | tf_op jit(solution)/shard_map/ppermute | solution.py:432
  115.9 6.6 %collective-permute-done.13 = bf16[256,1536]{1,0:T(8,128)(2,1)S(1)} collective-permute-done((bf16[256,1536]{1,0:T(8,128)(2,1)S(1)}, bf16[256,1536]{1,0:T(8,128)(2,1)S(1)}, u32[]{:S(2)}, u32[]{:S(2)}) %collective-permute-start.13) | collective-permute-done | bytes 786464 | tf_op jit(solution)/shard_map/ppermute | solution.py:432
  122.5 11.6 %collective-permute-done.12 = bf16[256,1536]{1,0:T(8,128)(2,1)S(1)} collective-permute-done((bf16[256,1536]{1,0:T(8,128)(2,1)S(1)}, bf16[256,1536]{1,0:T(8,128)(2,1)S(1)}, u32[]{:S(2)}, u32[]{:S(2)}) %collective-permute-start.12) | collective-permute-done | bytes 786464 | tf_op jit(solution)/shard_map/ppermute | solution.py:432
  137.8 5.2 %all-gather.9.cloned.1.call-done = bf16[32,48,2048]{2,1,0:T(8,128)(2,1)} async-done(((bf16[4,48,2048]{2,1,0:T(8,128)(2,1)}), bf16[32,48,2048]{2,1,0:T(8,128)(2,1)}) %all-gather.9.cloned.1.call-update) | async-done | bytes 6291472 | tf_op jit(solution)/shard_map/all_gather | solution.py:605
  146.3 9.5 %collective-permute-done.18.refs_0_ = bf16[256,1536]{1,0:T(8,128)(2,1)} collective-permute-done((bf16[256,1536]{1,0:T(8,128)(2,1)S(1)}, bf16[256,1536]{1,0:T(8,128)(2,1)}, u32[]{:S(2)}, u32[]{:S(2)}) %collective-permute-start.18) | collective-permute-done | bytes 786464 | tf_op jit(solution)/shard_map/ppermute | solution.py:432
  159.6 5.3 %shard_map.417 = (bf16[512,1024]{1,0:T(8,128)(2,1)S(1)}, bf16[512,1024]{1,0:T(8,128)(2,1)S(1)}, bf16[512,1024]{1,0:T(8,128)(2,1)S(1)}, bf16[512,768]{1,0:T(8,128)(2,1)S(1)}, bf16[512,768]{1,0:T(8,128)(2,1)}) custom-call(s32[3]{0:T(128)S(1)} %pad_add_fusion.1.pos_ref, bf16[256,1536]{1,0:T(8,128)(2,1)S(1)} %multiply_convert_fusion.refs_0_, ...), custom_call_target="tpu_custom_call" | custom-call | flops 5750000128 | tf_op jit(solution)/shard_map/pallas_call | solution.py:406
  168.8 5.5 %shard_map.418 = (bf16[512,1024]{1,0:T(8,128)(2,1)S(1)}, bf16[512,1024]{1,0:T(8,128)(2,1)S(1)}, bf16[512,1024]{1,0:T(8,128)(2,1)S(1)}, bf16[512,768]{1,0:T(8,128)(2,1)S(1)}, bf16[512,768]{1,0:T(8,128)(2,1)}) custom-call(s32[3]{0:T(128)S(1)} %pad_add_fusion.1.pos_ref, bf16[256,1536]{1,0:T(8,128)(2,1)} %collective-permute-done.18.refs_0_, ...), custom_call_target="tpu_custom_call" | custom-call | flops 5750000128 | tf_op jit(solution)/shard_map/pallas_call | solution.py:406
  192.8 5.2 %shard_map.420 = (bf16[256,1536]{1,0:T(8,128)(2,1)S(1)}, bf16[256,1536]{1,0:T(8,128)(2,1)S(1)}, bf16[512,2048]{1,0:T(8,128)(2,1)S(1)}) custom-call(bf16[256,1536]{1,0:T(8,128)(2,1)S(1)} %convert_multiply_fusion.2.refs_2_.refs_0_, bf16[256,1536]{1,0:T(8,128)(2,1)S(1)} %copy-done.8, bf16[512,1024]{1,0:T(8,128)(2,1)S(1)} %copy-done.50, ...), custom_call_target="tpu_custom_call" | custom-call | flops 5750000128 | tf_op jit(solution)/shard_map/pallas_call | solution.py:406
  199.9 5.2 %shard_map.421 = (bf16[256,1536]{1,0:T(8,128)(2,1)S(1)}, bf16[256,1536]{1,0:T(8,128)(2,1)S(1)}, bf16[512,2048]{1,0:T(8,128)(2,1)S(1)}) custom-call(bf16[256,1536]{1,0:T(8,128)(2,1)S(1)} %collective-permute-done.8.refs_4_.refs_0_, bf16[256,1536]{1,0:T(8,128)(2,1)S(1)} %copy-done.15, bf16[512,1024]{1,0:T(8,128)(2,1)S(1)} %copy-done.54, ...), custom_call_target="tpu_custom_call" | custom-call | flops 5750000128 | tf_op jit(solution)/shard_map/pallas_call | solution.py:406
  207.4 5.9 %collective-permute-done.29.refs_9_ = bf16[512,1536]{1,0:T(8,128)(2,1)S(1)} collective-permute-done((bf16[512,1536]{1,0:T(8,128)(2,1)S(1)}, bf16[512,1536]{1,0:T(8,128)(2,1)S(1)}, u32[]{:S(2)}, u32[]{:S(2)}) %collective-permute-start.29) | collective-permute-done | bytes 1572896 | tf_op jit(solution)/shard_map/ppermute | solution.py:435
  213.3 8.8 %shard_map.424 = bf16[4,288,2048]{2,1,0:T(8,128)(2,1)S(1)} custom-call(bf16[512,768]{1,0:T(8,128)(2,1)S(1)} %copy-done.80, bf16[512,768]{1,0:T(8,128)(2,1)} %collective-permute-done.22.refs_1_, bf16[512,768]{1,0:T(8,128)(2,1)S(1)} %copy-done.82, bf16[512,768]{1,0:T(8,128)(2,1)} %collective-permute-done.23.refs_3_, ...), custom_call_target="tpu_custom_call" | custom-call | flops 8625000448 | tf_op jit(solution)/shard_map/pallas_call | solution.py:406
  228.9 16.9 %collective-permute-done.21 = bf16[256,1536]{1,0:T(8,128)(2,1)S(1)} collective-permute-done((bf16[256,1536]{1,0:T(8,128)(2,1)S(1)}, bf16[256,1536]{1,0:T(8,128)(2,1)S(1)}, u32[]{:S(2)}, u32[]{:S(2)}) %collective-permute-start.21) | collective-permute-done | bytes 786464 | tf_op jit(solution)/shard_map/ppermute | solution.py:432
  245.7 17.2 %collective-permute-done.24 = bf16[256,1536]{1,0:T(8,128)(2,1)S(1)} collective-permute-done((bf16[256,1536]{1,0:T(8,128)(2,1)}, bf16[256,1536]{1,0:T(8,128)(2,1)S(1)}, u32[]{:S(2)}, u32[]{:S(2)}) %collective-permute-start.24) | collective-permute-done | bytes 786464 | tf_op jit(solution)/shard_map/ppermute | solution.py:432
  273.6 4.8 %shard_map.423 = (bf16[256,1152]{1,0:T(8,128)(2,1)S(1)}, bf16[256,1536]{1,0:T(8,128)(2,1)S(1)}, f32[2,128]{1,0:T(2,128)S(1)}) custom-call(bf16[256,1536]{1,0:T(8,128)(2,1)S(1)} %get-tuple-element.183.dh_ref.refs_4_, bf16[256,1152]{1,0:T(8,128)(2,1)S(1)} %copy-done.78, bf16[1536,1280]{1,0:T(8,128)(2,1)S(1)} %bitcast.44, bf16[384,1536]{1,0:T(8,128)(2,1)S(1)} %bitcast.52, ...), custom_call_target="tpu_custom_call" | custom-call | flops 5750000128 | tf_op jit(solution)/shard_map/pallas_call | solution.py:406
  278.5 7.0 %collective-permute-done.31.dh_ref.refs_6_ = bf16[256,1536]{1,0:T(8,128)(2,1)S(1)} collective-permute-done((bf16[256,1536]{1,0:T(8,128)(2,1)S(1)}, bf16[256,1536]{1,0:T(8,128)(2,1)S(1)}, u32[]{:S(2)}, u32[]{:S(2)}) %collective-permute-start.31) | collective-permute-done | bytes 786464 | tf_op jit(solution)/shard_map/ppermute | solution.py:432
  288.0 4.8 %shard_map.425 = (bf16[256,1152]{1,0:T(8,128)(2,1)S(1)}, bf16[256,1536]{1,0:T(8,128)(2,1)S(1)}, f32[2,128]{1,0:T(2,128)S(1)}) custom-call(bf16[256,1536]{1,0:T(8,128)(2,1)S(1)} %collective-permute-done.30.dh_ref.refs_5_, bf16[256,1152]{1,0:T(8,128)(2,1)S(1)} %copy-done.76, bf16[1536,1280]{1,0:T(8,128)(2,1)S(1)} %bitcast.45, bf16[384,1536]{1,0:T(8,128)(2,1)S(1)} %bitcast.53, ...), custom_call_target="tpu_custom_call" | custom-call | flops 5750000128 | tf_op jit(solution)/shard_map/pallas_call | solution.py:406
  293.7 5.0 %shard_map.426 = (bf16[256,1152]{1,0:T(8,128)(2,1)S(1)}, bf16[256,1536]{1,0:T(8,128)(2,1)S(1)}, f32[2,128]{1,0:T(2,128)S(1)}) custom-call(bf16[256,1536]{1,0:T(8,128)(2,1)S(1)} %collective-permute-done.31.dh_ref.refs_6_, bf16[256,1152]{1,0:T(8,128)(2,1)S(1)} %copy-done.74, bf16[1536,1280]{1,0:T(8,128)(2,1)S(1)} %bitcast.46, bf16[384,1536]{1,0:T(8,128)(2,1)S(1)} %bitcast.54, ...), custom_call_target="tpu_custom_call" | custom-call | flops 5750000128 | tf_op jit(solution)/shard_map/pallas_call | solution.py:406
  299.8 4.8 %shard_map.427 = (bf16[256,1152]{1,0:T(8,128)(2,1)S(1)}, bf16[256,1536]{1,0:T(8,128)(2,1)S(1)}, f32[2,128]{1,0:T(2,128)S(1)}) custom-call(bf16[256,1536]{1,0:T(8,128)(2,1)S(1)} %constant_dynamic-update-slice_fusion.4.dh_ref.refs_7_, bf16[256,1152]{1,0:T(8,128)(2,1)S(1)} %copy-done.72, bf16[1536,1280]{1,0:T(8,128)(2,1)S(1)} %bitcast.47, ...), custom_call_target="tpu_custom_call" | custom-call | flops 5750000128 | tf_op jit(solution)/shard_map/pallas_call | solution.py:406
  304.7 5.6 %shard_map.428 = (bf16[4,192,1152]{2,1,0:T(8,128)(2,1)S(1)}, bf16[4,192,1152]{2,1,0:T(8,128)(2,1)S(1)}) custom-call(s32[3]{0:T(128)S(1)} %pad_add_fusion.1.pos_ref, bf16[256,1536]{1,0:T(8,128)(2,1)S(1)} %copy-done.66, bf16[256,1536]{1,0:T(8,128)(2,1)S(1)} %copy-done.64, bf16[256,1536]{1,0:T(8,128)(2,1)S(1)} %copy-done.62, bf16[256,1536]{1,0:T(8,128)(2,1)S(1)} %copy-done.60, ...), custom_call_target="tpu_custom_call" | custom-call | flops 5750000128 | tf_op jit(solution)/shard_map/pallas_call | solution.py:406
  331.7 15.8 %collective-permute-done.26 = bf16[512,1536]{1,0:T(8,128)(2,1)} collective-permute-done((bf16[512,1536]{1,0:T(8,128)(2,1)}, bf16[512,1536]{1,0:T(8,128)(2,1)}, u32[]{:S(2)}, u32[]{:S(2)}) %collective-permute-start.26) | collective-permute-done | bytes 1572896 | tf_op jit(solution)/shard_map/ppermute | solution.py:432
  350.3 5.8 %collective-permute-done.38 = bf16[512,1536]{1,0:T(8,128)(2,1)} collective-permute-done((bf16[512,1536]{1,0:T(8,128)(2,1)}, bf16[512,1536]{1,0:T(8,128)(2,1)}, u32[]{:S(2)}, u32[]{:S(2)}) %collective-permute-start.38) | collective-permute-done | bytes 1572896 | tf_op jit(solution)/shard_map/ppermute | solution.py:432
  364.2 15.0 %collective-permute-done.46 = f32[2,128]{1,0:T(2,128)S(1)} collective-permute-done((f32[2,128]{1,0:T(2,128)S(1)}, f32[2,128]{1,0:T(2,128)S(1)}, u32[]{:S(2)}, u32[]{:S(2)}) %collective-permute-start.46) | collective-permute-done | bytes 1056 | tf_op jit(solution)/shard_map/ppermute | solution.py:439
  (389 shorter events, 194.0 us)
Async XLA Ops:
  7.2 85.4 %all-gather.7.cloned.1.call-start = ((), (), s32[]{:S(2)}) async-start(), calls=%async_computation.4 | async-start | bytes 5750784 | tf_op jit(solution)/shard_map/all_gather | solution.py:603
  21.9 121.1 %all-gather.9.cloned.1.call-start = ((), (), s32[]{:S(2)}) async-start(), calls=%async_computation.5 | async-start | bytes 7077888 | tf_op jit(solution)/shard_map/all_gather | solution.py:605
  22.0 30.0 %collective-permute-start.5 = (bf16[256,1536]{1,0:T(8,128)(2,1)S(1)}, bf16[256,1536]{1,0:T(8,128)(2,1)S(1)}, u32[]{:S(2)}, u32[]{:S(2)}) collective-permute-start(bf16[256,1536]{1,0:T(8,128)(2,1)S(1)} %copy-done), channel_id=1, source_target_pairs={{0,16},{8,24},{16,0},{24,8},{1,17},{9,25},{17,1},{25,9},{2,18},{10... | collective-permute-start | bytes 2359304 | tf_op jit(solution)/shard_map/ppermute | solution.py:432
  23.5 28.5 %collective-permute-start.3 = (bf16[256,1536]{1,0:T(8,128)(2,1)S(1)}, bf16[256,1536]{1,0:T(8,128)(2,1)S(1)}, u32[]{:S(2)}, u32[]{:S(2)}) collective-permute-start(bf16[256,1536]{1,0:T(8,128)(2,1)S(1)} %copy-done), channel_id=1, source_target_pairs={{0,8},{8,0},{16,24},{24,16},{1,9},{9,1},{17,25},{25,17},{2,10},{10... | collective-permute-start | bytes 2359304 | tf_op jit(solution)/shard_map/ppermute | solution.py:432
  26.0 20.4 %collective-permute-start.15 = (bf16[48,2048]{1,0:T(8,128)(2,1)S(1)}, bf16[48,2048]{1,0:T(8,128)(2,1)S(1)}, u32[]{:S(2)}, u32[]{:S(2)}) collective-permute-start(bf16[48,2048]{1,0:T(8,128)(2,1)S(1)} %get-tuple-element.153), channel_id=1, source_target_pairs={{0,8},{8,0},{16,24},{24,16},{1,9},{9,1},{17,25},{25,17},{2,10},{10... | collective-permute-start | bytes 589832 | tf_op jit(solution)/shard_map/ppermute | solution.py:432
  28.2 21.2 %collective-permute-start.17 = (bf16[48,2048]{1,0:T(8,128)(2,1)S(1)}, bf16[48,2048]{1,0:T(8,128)(2,1)S(1)}, u32[]{:S(2)}, u32[]{:S(2)}) collective-permute-start(bf16[48,2048]{1,0:T(8,128)(2,1)S(1)} %get-tuple-element.155), channel_id=1, source_target_pairs={{0,24},{8,16},{16,8},{24,0},{1,25},{9,17},{17,9},{25,1},{2,26},{10... | collective-permute-start | bytes 589832 | tf_op jit(solution)/shard_map/ppermute | solution.py:432
  52.0 132.6 %all-gather.11.cloned.1.call-start = ((), (), s32[]{:S(2)}) async-start(), calls=%async_computation.6 | async-start | bytes 3538944 | tf_op jit(solution)/shard_map/all_gather | solution.py:607
  87.1 241.9 %reduce-scatter.3.cloned.1.call-start = ((), (), s32[]{:S(2)}) async-start(), calls=%async_computation.2 | async-start | bytes 5898240 | tf_op jit(solution)/shard_map/reduce_scatter | solution.py:703
  101.1 21.4 %collective-permute-start.13 = (bf16[256,1536]{1,0:T(8,128)(2,1)S(1)}, bf16[256,1536]{1,0:T(8,128)(2,1)S(1)}, u32[]{:S(2)}, u32[]{:S(2)}) collective-permute-start(bf16[256,1536]{1,0:T(8,128)(2,1)S(1)} %get-tuple-element.150), channel_id=1, source_target_pairs={{0,24},{8,16},{16,8},{24,0},{1,25},{9,17},{17,9},{25,1},{2,26},{10... | collective-permute-start | bytes 2359304 | tf_op jit(solution)/shard_map/ppermute | solution.py:432
  106.0 28.2 %collective-permute-start.12 = (bf16[256,1536]{1,0:T(8,128)(2,1)S(1)}, bf16[256,1536]{1,0:T(8,128)(2,1)S(1)}, u32[]{:S(2)}, u32[]{:S(2)}) collective-permute-start(bf16[256,1536]{1,0:T(8,128)(2,1)S(1)} %get-tuple-element.149), channel_id=1, source_target_pairs={{0,16},{8,24},{16,0},{24,8},{1,17},{9,25},{17,1},{25,9},{2,18},{10... | collective-permute-start | bytes 2359304 | tf_op jit(solution)/shard_map/ppermute | solution.py:432
  110.7 23.5 %collective-permute-start.11 = (bf16[256,1536]{1,0:T(8,128)(2,1)S(1)}, bf16[256,1536]{1,0:T(8,128)(2,1)S(1)}, u32[]{:S(2)}, u32[]{:S(2)}) collective-permute-start(bf16[256,1536]{1,0:T(8,128)(2,1)S(1)} %get-tuple-element.148), channel_id=1, source_target_pairs={{0,8},{8,0},{16,24},{24,16},{1,9},{9,1},{17,25},{25,17},{2,10},{10... | collective-permute-start | bytes 2359304 | tf_op jit(solution)/shard_map/ppermute | solution.py:432
  136.7 20.9 %collective-permute-start.14 = (bf16[256,1536]{1,0:T(8,128)(2,1)S(1)}, bf16[256,1536]{1,0:T(8,128)(2,1)}, u32[]{:S(2)}, u32[]{:S(2)}) collective-permute-start(bf16[256,1536]{1,0:T(8,128)(2,1)S(1)} %multiply_convert_fusion.refs_0_), channel_id=1, source_target_pairs={{0,8},{8,0},{16,24},{24,16},{1,9},{9,1},{17,25},{25,17},{2,10},{10... | collective-permute-start | bytes 2359304 | tf_op jit(solution)/shard_map/ppermute | solution.py:432
  166.9 32.5 %collective-permute-start.22 = (bf16[512,768]{1,0:T(8,128)(2,1)}, bf16[512,768]{1,0:T(8,128)(2,1)}, u32[]{:S(2)}, u32[]{:S(2)}) collective-permute-start(bf16[512,768]{1,0:T(8,128)(2,1)} %get-tuple-element.173), channel_id=1, source_target_pairs={{0,4},{4,0},{1,5},{5,1},{2,6},{6,2},{3,7},{7,3},{8,12},{12,8},{9,1... | collective-permute-start | bytes 2359304 | tf_op jit(solution)/shard_map/ppermute | solution.py:435
  177.2 22.2 %collective-permute-start.23 = (bf16[512,768]{1,0:T(8,128)(2,1)}, bf16[512,768]{1,0:T(8,128)(2,1)}, u32[]{:S(2)}, u32[]{:S(2)}) collective-permute-start(bf16[512,768]{1,0:T(8,128)(2,1)} %get-tuple-element.175), channel_id=1, source_target_pairs={{0,4},{4,0},{1,5},{5,1},{2,6},{6,2},{3,7},{7,3},{8,12},{12,8},{9,1... | collective-permute-start | bytes 2359304 | tf_op jit(solution)/shard_map/ppermute | solution.py:435
  224.3 178.5 %reduce-scatter.5.cloned.1.call-start = ((), (), s32[]{:S(2)}) async-start(), calls=%async_computation.3 | async-start | bytes 2949120 | tf_op jit(solution)/shard_map/reduce_scatter | solution.py:741
  225.4 20.4 %collective-permute-start.21 = (bf16[256,1536]{1,0:T(8,128)(2,1)S(1)}, bf16[256,1536]{1,0:T(8,128)(2,1)S(1)}, u32[]{:S(2)}, u32[]{:S(2)}) collective-permute-start(bf16[256,1536]{1,0:T(8,128)(2,1)S(1)} %copy-done.35), channel_id=1, source_target_pairs={{0,8},{8,0},{16,24},{24,16},{1,9},{9,1},{17,25},{25,17},{2,10},{10... | collective-permute-start | bytes 2359304 | tf_op jit(solution)/shard_map/ppermute | solution.py:432
  226.6 36.4 %collective-permute-start.24 = (bf16[256,1536]{1,0:T(8,128)(2,1)}, bf16[256,1536]{1,0:T(8,128)(2,1)S(1)}, u32[]{:S(2)}, u32[]{:S(2)}) collective-permute-start(bf16[256,1536]{1,0:T(8,128)(2,1)} %copy-done.38), channel_id=1, source_target_pairs={{0,16},{8,24},{16,0},{24,8},{1,17},{9,25},{17,1},{25,9},{2,18},{10... | collective-permute-start | bytes 2359304 | tf_op jit(solution)/shard_map/ppermute | solution.py:432
  227.2 35.7 %collective-permute-start.25 = (bf16[256,1536]{1,0:T(8,128)(2,1)S(1)}, bf16[256,1536]{1,0:T(8,128)(2,1)S(1)}, u32[]{:S(2)}, u32[]{:S(2)}) collective-permute-start(bf16[256,1536]{1,0:T(8,128)(2,1)S(1)} %copy-done.37), channel_id=1, source_target_pairs={{0,24},{8,16},{16,8},{24,0},{1,25},{9,17},{17,9},{25,1},{2,26},{10... | collective-permute-start | bytes 2359304 | tf_op jit(solution)/shard_map/ppermute | solution.py:432
  310.3 37.1 %collective-permute-start.26 = (bf16[512,1536]{1,0:T(8,128)(2,1)}, bf16[512,1536]{1,0:T(8,128)(2,1)}, u32[]{:S(2)}, u32[]{:S(2)}) collective-permute-start(bf16[512,1536]{1,0:T(8,128)(2,1)} %get-tuple-element.186), channel_id=1, source_target_pairs={{0,8},{8,0},{16,24},{24,16},{1,9},{9,1},{17,25},{25,17},{2,10},{10... | collective-permute-start | bytes 4718600 | tf_op jit(solution)/shard_map/ppermute | solution.py:432
  318.5 37.6 %collective-permute-start.38 = (bf16[512,1536]{1,0:T(8,128)(2,1)}, bf16[512,1536]{1,0:T(8,128)(2,1)}, u32[]{:S(2)}, u32[]{:S(2)}) collective-permute-start(bf16[512,1536]{1,0:T(8,128)(2,1)} %pad_maximum_fusion), channel_id=1, source_target_pairs={{0,16},{8,24},{16,0},{24,8},{1,17},{9,25},{17,1},{25,9},{2,18},{10... | collective-permute-start | bytes 4718600 | tf_op jit(solution)/shard_map/ppermute | solution.py:432
  349.7 45.0 %collective-permute-start.41 = (bf16[256,1536]{1,0:T(8,128)(2,1)}, bf16[256,1536]{1,0:T(8,128)(2,1)}, u32[]{:S(2)}, u32[]{:S(2)}) collective-permute-start(bf16[256,1536]{1,0:T(8,128)(2,1)} %add_convert_fusion.2), channel_id=1, source_target_pairs={{0,16},{8,24},{16,0},{24,8},{1,17},{9,25},{17,1},{25,9},{2,18},{10... | collective-permute-start | bytes 2359304 | tf_op jit(solution)/shard_map/ppermute | solution.py:432
  358.4 38.9 %collective-permute-start.42 = (bf16[256,1536]{1,0:T(8,128)(2,1)}, bf16[256,1536]{1,0:T(8,128)(2,1)}, u32[]{:S(2)}, u32[]{:S(2)}) collective-permute-start(bf16[256,1536]{1,0:T(8,128)(2,1)} %add_convert_fusion.1), channel_id=1, source_target_pairs={{0,8},{8,0},{16,24},{24,16},{1,9},{9,1},{17,25},{25,17},{2,10},{10... | collective-permute-start | bytes 2359304 | tf_op jit(solution)/shard_map/ppermute | solution.py:432
  360.4 23.1 %collective-permute-start.36 = (bf16[48,2048]{1,0:T(8,128)(2,1)}, bf16[48,2048]{1,0:T(8,128)(2,1)S(1)}, u32[]{:S(2)}, u32[]{:S(2)}) collective-permute-start(bf16[48,2048]{1,0:T(8,128)(2,1)} %get-tuple-element.214), channel_id=1, source_target_pairs={{0,8},{8,0},{16,24},{24,16},{1,9},{9,1},{17,25},{25,17},{2,10},{10... | collective-permute-start | bytes 589832 | tf_op jit(solution)/shard_map/ppermute | solution.py:432
  361.7 21.9 %collective-permute-start.39 = (bf16[48,2048]{1,0:T(8,128)(2,1)}, bf16[48,2048]{1,0:T(8,128)(2,1)S(1)}, u32[]{:S(2)}, u32[]{:S(2)}) collective-permute-start(bf16[48,2048]{1,0:T(8,128)(2,1)} %get-tuple-element.226), channel_id=1, source_target_pairs={{0,16},{8,24},{16,0},{24,8},{1,17},{9,25},{17,1},{25,9},{2,18},{10... | collective-permute-start | bytes 589832 | tf_op jit(solution)/shard_map/ppermute | solution.py:432
  (140 other events, 1008.3 us)
Sparse Core Ops, SparseCore 0:
  22.0 55.1 all-gather.6
  79.4 63.5 all-gather.8
  144.6 36.9 all-gather.10
  224.4 85.3 reduce-scatter.2
  328.9 47.5 reduce-scatter.4

commit v3 on v2

--- a/solution.py
+++ b/solution.py
@@ -390,7 +390,7 @@
     hidden_back_kernel: 5.0,
     second_grad_kernel: 7.5,
     down_kernel: 4.5,
-    attend_back_kernel: 5.0,
+    attend_back_kernel: 15,
     weight_grad_kernel: 5.0,
     chunk_first_kernel: 2.0,
     owner_first_kernel: 1.0,
@@ -606,7 +606,8 @@
     x_blocks = plane_far(grp, x_near)
     down_all = everywhere(tie(down_weight, x_blocks[3]).astype(BF16))
     grad_out = cotangent.astype(F32) * needle.astype(F32)[:, None]
-    dy_blocks = plane_gather(grp, tie(grad_out, x_blocks[3]).astype(BF16))
+    dy_near = plane_near(grp, tie(grad_out, x_blocks[3]).astype(BF16))
+    dy_blocks = plane_far(grp, dy_near)
     qkv_full, out_full, gains_full = call(
         place_first_kernel,
         (
@@ -614,7 +615,7 @@
             shaped(count, rows, width),
             shaped(8, width, dtype=F32),
         ),
-        (tie(first_all, *dy_blocks[1:]),),
+        (tie(first_all, x_blocks[3], *dy_near[1:]),),
         scratch=(pltpu.SemaphoreType.DMA((count * (PLANE + 1),)),),
         specs=[ANY],
     )
@@ -637,7 +638,7 @@
                 shaped(length, LOCAL_Q),
                 shaped(length, width),
             ),
-            (x_blocks[r], gain_one, qkv_full, out_full, lam, hg),
+            (x_blocks[r] if r else tie(x_blocks[r], dy_blocks[3]), gain_one, qkv_full, out_full, lam, hg),
         )
     residual = activations + add_up(plane_send(grp, parts))
     normed_two = (residual * rms_scale(residual) * gain_two).astype(BF16)
@@ -701,7 +702,9 @@
         (*flat(lefts), *flat(rights), *down_terms),
     )[0]
     second_sum = to_owner(second_message)
-    grad_residual = grad_out + norm_back(add_up(dn2_terms), residual, gain_two)
+    grad_residual = grad_out + norm_back(
+        add_up(late(dn2_terms, second_message)), residual, gain_two
+    )
 
     dh_near = plane_near(grp, grad_residual.astype(BF16))
     dh_blocks = plane_far(grp, dh_near)
@@ -723,11 +726,11 @@
             (block, projected[r], qkv_full, out_full, lam, hg),
             scratch=(pltpu.VMEM((length, LOCAL_Q), F32),),
         )
-    y_got = grp.plane(tie(y_parts[2], dp_blocks[0]), 1)
+    half = PLANE * count // 2
+    stat = grp.everyone(grp.everyone(add_up(stats), half), half // 2)
+    y_got = grp.plane(tie(y_parts[2], stat), 1)
     qkv_halves = weight_grad(grp, normed_one, dp_blocks, PLANE)
-    out_halves = weight_grad(grp, merged, dh_blocks, 1)
-    half = PLANE * count // 2
-    stat = grp.everyone(add_up(stats), half)
+    out_halves = weight_grad(grp, [tie(merged[0], stat), *merged[1:]], dh_blocks, 1)
     dn1_got = grp.plane(tie(jnp.concatenate([dn1_parts[2], dn1_parts[3]], axis=0), stat), 2)
     step = half // 4
     while step:
@@ -750,27 +753,27 @@
     gateup_pieces = exchange(grp, gateup_pieces)
     y_got = tie(y_got, gateup_pieces[0])
     y_sent, y_last = plane_scatter_second(grp, y_parts[1], 1, y_got)
-    dn1_got = tie(dn1_got, y_sent)
+    dn1_got = tie(dn1_got, y_sent, *gateup_pieces[1:])
     dn1_sent, dn1_last = plane_scatter_second(grp, dn1_parts[1], 2, dn1_got)
     *gateup_res, gateup_dot = adam_columns(
         grp, late(gateup_pieces, dn1_sent), gateup_weight, gateup_first, gateup_second, 2
     )
-    y_got, y_last = tie(y_got, gateup_dot), tie(y_last, gateup_dot)
+    *qkv_pieces, out_grad = owner(
+        grp,
+        owner_first_kernel,
+        tie(first_sum, gateup_dot, stat),
+        (rows, 3 * LOCAL_Q),
+        (shaped(*out_weight.shape, dtype=F32),),
+    )
+    qkv_pieces = exchange(grp, qkv_pieces)
+    y_got, y_last = tie(y_got, qkv_pieces[0]), tie(y_last, qkv_pieces[0])
     layer_output = (residual + add_up([y_parts[0], y_got[:length], y_last])).astype(BF16)
-    stat = grp.everyone(tie(stat, dn1_sent), half // 2)
     dn1_got, dn1_last = tie(dn1_got, layer_output), tie(dn1_last, layer_output)
     input_grad = grad_residual + norm_back(
         add_up([dn1_parts[0], dn1_got[:length], dn1_last]), activations, gain_one
     )
-    *qkv_pieces, out_grad = owner(
-        grp,
-        owner_first_kernel,
-        tie(first_sum, input_grad, stat),
-        (rows, 3 * LOCAL_Q),
-        (shaped(*out_weight.shape, dtype=F32),),
-    )
     *qkv_res, qkv_dot = adam_columns(
-        grp, exchange(grp, qkv_pieces), qkv_weight, qkv_first, qkv_second, 3
+        grp, late(qkv_pieces, input_grad), qkv_weight, qkv_first, qkv_second, 3
     )
     total_head, total_mixing = stat[0], stat[1, 0]
     gains_grad = jnp.concatenate([qkv_dot[:1], gateup_dot[:1]]) / gains_low.astype(F32)

time: 426 us -> 399 us (0.937)
  waiting for transfers between devices: 179 us -> 150 us
  local copies, waits for them, and re-layouts: 51.2 us -> 45.7 us
  starting transfers between devices: 47.4 us -> 52.6 us
    ppermute x38, waiting for transfers between devices: 149 us -> 120 us  [plane(): return lax.ppermute(value, 'j', [(i, i ^ r) for i in range(PLANE)])]
    ppermute x5, waiting for transfers between devices: 19.1 us -> 8.85 us  [everyone(): return value + lax.ppermute(value, AXES, [(i, i ^ step) for i in range(n)])]
    ppermute x38, starting transfers between devices: 39.6 us -> 46.4 us  [plane(): return lax.ppermute(value, 'j', [(i, i ^ r) for i in range(PLANE)])]
    all_gather x1, waiting for transfers between devices: 5.22 us -> 12 us  [per_device(): second_all = everywhere(tie(second_message, *x_near[1:]))]
    unnamed x221 -> x215, local copies, waits for them, and re-layouts: 45.8 us -> 39.6 us
  transfers between devices with their start and end apart: 55 -> 55, of which waited for: 30 -> 26; matrix products, arithmetic and copies ran while one was open for 8% -> 9% of each run, Pallas kernels for 20% -> 24%
where the time goes in v3:
time: 399 us; the launch traced here: 396 us
  waiting for transfers between devices  150 us (38%)
  Pallas kernels  99.1 us (25%)
  starting transfers between devices  52.6 us (13%)
  local copies, waits for them, and re-layouts  45.7 us (11%)
  other arithmetic  30.3 us (8%)
  between operations  18.1 us (5%)
    ppermute x38, waiting for transfers between devices, plane(): return lax.ppermute(value, 'j', [(i, i ^ r) for i in range(PLANE)])  120 us
    pallas_call x28, Pallas kernels, call(): pl.pallas_call(kernel, out_shape=tuple(outs), in_specs=specs or [VMEM] *...  99.1 us
    ppermute x38, starting transfers between devices, plane(): return lax.ppermute(value, 'j', [(i, i ^ r) for i in range(PLANE)])  46.4 us
    unnamed x215, local copies, waits for them, and re-layouts  39.6 us
    all_gather x1, waiting for transfers between devices, per_device(): second_all = everywhere(tie(second_message, *x_near[1:]))  12 us
    ppermute x5, waiting for transfers between devices, everyone(): return value + lax.ppermute(value, AXES, [(i, i ^ step) for i in range(n)])  8.85 us
  transfers between devices with their start and end apart: 55, of which 26 were waited for; matrix products, arithmetic and copies ran while one was open for 9% of the time, Pallas kernels for 24%

profile of v3, /device:TPU:0, one launch (start us, length us, event | category | flops | bytes accessed | tf_op | source)
XLA Modules:
  0.0 395.8 jit_solution(11756616515544261658)
XLA Ops:
  29.6 16.9 %collective-permute-done.15.refs_1_ = bf16[48,2048]{1,0:T(8,128)(2,1)S(1)} collective-permute-done((bf16[48,2048]{1,0:T(8,128)(2,1)S(1)}, bf16[48,2048]{1,0:T(8,128)(2,1)S(1)}, u32[]{:S(2)}, u32[]{:S(2)}) %collective-permute-start.15) | collective-permute-done | bytes 196640 | tf_op jit(solution)/shard_map/ppermute | solution.py:432
  54.8 7.9 %collective-permute-done.4 = bf16[128,1536]{1,0:T(8,128)(2,1)S(1)} collective-permute-done((bf16[128,1536]{1,0:T(8,128)(2,1)S(1)}, bf16[128,1536]{1,0:T(8,128)(2,1)S(1)}, u32[]{:S(2)}, u32[]{:S(2)}) %collective-permute-start.4) | collective-permute-done | bytes 393248 | tf_op jit(solution)/shard_map/ppermute | solution.py:432
  68.8 11.1 %collective-permute-done.9.refs_4_.refs_0_ = bf16[256,1536]{1,0:T(8,128)(2,1)S(1)} collective-permute-done((bf16[256,1536]{1,0:T(8,128)(2,1)S(1)}, bf16[256,1536]{1,0:T(8,128)(2,1)S(1)}, u32[]{:S(2)}, u32[]{:S(2)}) %collective-permute-start.9) | collective-permute-done | bytes 786464 | tf_op jit(solution)/shard_map/ppermute | solution.py:432
  112.3 4.3 %collective-permute-done.13 = bf16[256,1536]{1,0:T(8,128)(2,1)S(1)} collective-permute-done((bf16[256,1536]{1,0:T(8,128)(2,1)S(1)}, bf16[256,1536]{1,0:T(8,128)(2,1)S(1)}, u32[]{:S(2)}, u32[]{:S(2)}) %collective-permute-start.13) | collective-permute-done | bytes 786464 | tf_op jit(solution)/shard_map/ppermute | solution.py:432
  116.5 9.6 %collective-permute-done.12 = bf16[256,1536]{1,0:T(8,128)(2,1)S(1)} collective-permute-done((bf16[256,1536]{1,0:T(8,128)(2,1)S(1)}, bf16[256,1536]{1,0:T(8,128)(2,1)S(1)}, u32[]{:S(2)}, u32[]{:S(2)}) %collective-permute-start.12) | collective-permute-done | bytes 786464 | tf_op jit(solution)/shard_map/ppermute | solution.py:432
  131.0 12.0 %all-gather.9.cloned.1.call-done = bf16[32,48,2048]{2,1,0:T(8,128)(2,1)} async-done(((bf16[4,48,2048]{2,1,0:T(8,128)(2,1)}), bf16[32,48,2048]{2,1,0:T(8,128)(2,1)}) %all-gather.9.cloned.1.call-update) | async-done | bytes 6291472 | tf_op jit(solution)/shard_map/all_gather | solution.py:605
  153.2 5.2 %shard_map.417 = (bf16[512,1024]{1,0:T(8,128)(2,1)S(1)}, bf16[512,1024]{1,0:T(8,128)(2,1)S(1)}, bf16[512,1024]{1,0:T(8,128)(2,1)S(1)}, bf16[512,768]{1,0:T(8,128)(2,1)S(1)}, bf16[512,768]{1,0:T(8,128)(2,1)}) custom-call(s32[3]{0:T(128)S(1)} %pad_add_fusion.1.pos_ref, bf16[256,1536]{1,0:T(8,128)(2,1)S(1)} %multiply_convert_fusion.refs_0_, ...), custom_call_target="tpu_custom_call" | custom-call | flops 5750000128 | tf_op jit(solution)/shard_map/pallas_call | solution.py:406
  161.5 5.5 %shard_map.418 = (bf16[512,1024]{1,0:T(8,128)(2,1)S(1)}, bf16[512,1024]{1,0:T(8,128)(2,1)S(1)}, bf16[512,1024]{1,0:T(8,128)(2,1)S(1)}, bf16[512,768]{1,0:T(8,128)(2,1)S(1)}, bf16[512,768]{1,0:T(8,128)(2,1)}) custom-call(s32[3]{0:T(128)S(1)} %pad_add_fusion.1.pos_ref, bf16[256,1536]{1,0:T(8,128)(2,1)} %collective-permute-done.18.refs_0_, ...), custom_call_target="tpu_custom_call" | custom-call | flops 5750000128 | tf_op jit(solution)/shard_map/pallas_call | solution.py:406
  170.1 4.0 %shard_map.419 = (bf16[512,1536]{1,0:T(8,128)(2,1)S(1)}, bf16[512,1536]{1,0:T(8,128)(2,1)S(1)}) custom-call(s32[3]{0:T(128)S(1)} %pad_add_fusion.1.pos_ref, bf16[512,1024]{1,0:T(8,128)(2,1)S(1)} %get-tuple-element.167.refs_0_, bf16[512,1024]{1,0:T(8,128)(2,1)S(1)} %get-tuple-element.171.refs_1_, ...), custom_call_target="tpu_custom_call" | custom-call | flops 4600000000 | tf_op jit(solution)/shard_map/pallas_call | solution.py:406
  177.4 4.2 %all-gather.11.cloned.1.call-done = bf16[1024,1536]{1,0:T(8,128)(2,1)} async-done(((bf16[128,1536]{1,0:T(8,128)(2,1)}), bf16[1024,1536]{1,0:T(8,128)(2,1)}) %all-gather.11.cloned.1.call-update) | async-done | bytes 3145744 | tf_op jit(solution)/shard_map/all_gather | solution.py:607
  188.7 6.1 %shard_map.420 = (bf16[256,1536]{1,0:T(8,128)(2,1)S(1)}, bf16[256,1536]{1,0:T(8,128)(2,1)}, bf16[512,2048]{1,0:T(8,128)(2,1)S(1)}) custom-call(bf16[256,1536]{1,0:T(8,128)(2,1)S(1)} %convert_multiply_fusion.2.refs_2_.refs_0_, bf16[256,1536]{1,0:T(8,128)(2,1)S(1)} %collective-permute-done.7.refs_3_.refs_1_, bf16[512,1024]{1,0:T(8,128)(2,1)S(1)} %copy-done.43, ...), custom_call_target="tpu_custom_call" | custom-call | flops 5750000128 | tf_op jit(solution)/shard_map/pallas_call | solution.py:406
  195.3 5.2 %shard_map.421 = (bf16[256,1536]{1,0:T(8,128)(2,1)S(1)}, bf16[256,1536]{1,0:T(8,128)(2,1)S(1)}, bf16[512,2048]{1,0:T(8,128)(2,1)S(1)}) custom-call(bf16[256,1536]{1,0:T(8,128)(2,1)S(1)} %collective-permute-done.9.refs_4_.refs_0_, bf16[256,1536]{1,0:T(8,128)(2,1)S(1)} %copy-done.15, bf16[512,1024]{1,0:T(8,128)(2,1)S(1)} %copy-done.47, ...), custom_call_target="tpu_custom_call" | custom-call | flops 5750000128 | tf_op jit(solution)/shard_map/pallas_call | solution.py:406
  209.4 8.8 %shard_map.422 = bf16[4,288,2048]{2,1,0:T(8,128)(2,1)S(1)} custom-call(bf16[512,768]{1,0:T(8,128)(2,1)S(1)} %copy-done.73, bf16[512,768]{1,0:T(8,128)(2,1)} %collective-permute-done.22.refs_1_, bf16[512,768]{1,0:T(8,128)(2,1)S(1)} %copy-done.75, bf16[512,768]{1,0:T(8,128)(2,1)} %collective-permute-done.23.refs_3_, ...), custom_call_target="tpu_custom_call" | custom-call | flops 8625000448 | tf_op jit(solution)/shard_map/pallas_call | solution.py:406
  220.8 18.2 %collective-permute-done.28 = bf16[256,1536]{1,0:T(8,128)(2,1)} collective-permute-done((bf16[256,1536]{1,0:T(8,128)(2,1)S(1)}, bf16[256,1536]{1,0:T(8,128)(2,1)}, u32[]{:S(2)}, u32[]{:S(2)}) %collective-permute-start.28) | collective-permute-done | bytes 786464 | tf_op jit(solution)/shard_map/ppermute | solution.py:432
  252.1 4.8 %shard_map.424 = (bf16[256,1152]{1,0:T(8,128)(2,1)S(1)}, bf16[256,1536]{1,0:T(8,128)(2,1)S(1)}, f32[2,128]{1,0:T(2,128)S(1)}) custom-call(bf16[256,1536]{1,0:T(8,128)(2,1)S(1)} %get-tuple-element.197.dh_ref.refs_4_, bf16[256,1152]{1,0:T(8,128)(2,1)S(1)} %copy-done.71, bf16[1536,1280]{1,0:T(8,128)(2,1)S(1)} %bitcast.44, bf16[384,1536]{1,0:T(8,128)(2,1)S(1)} %bitcast.52, ...), custom_call_target="tpu_custom_call" | custom-call | flops 17250000896 | tf_op jit(solution)/shard_map/pallas_call | solution.py:406
  256.9 7.5 %collective-permute-done.30.dh_ref.refs_6_ = bf16[256,1536]{1,0:T(8,128)(2,1)S(1)} collective-permute-done((bf16[256,1536]{1,0:T(8,128)(2,1)S(1)}, bf16[256,1536]{1,0:T(8,128)(2,1)S(1)}, u32[]{:S(2)}, u32[]{:S(2)}) %collective-permute-start.30) | collective-permute-done | bytes 786464 | tf_op jit(solution)/shard_map/ppermute | solution.py:432
  266.5 4.8 %shard_map.425 = (bf16[256,1152]{1,0:T(8,128)(2,1)S(1)}, bf16[256,1536]{1,0:T(8,128)(2,1)S(1)}, f32[2,128]{1,0:T(2,128)S(1)}) custom-call(bf16[256,1536]{1,0:T(8,128)(2,1)S(1)} %collective-permute-done.29.dh_ref.refs_5_, bf16[256,1152]{1,0:T(8,128)(2,1)S(1)} %copy-done.69, bf16[1536,1280]{1,0:T(8,128)(2,1)S(1)} %bitcast.45, bf16[384,1536]{1,0:T(8,128)(2,1)S(1)} %bitcast.53, ...), custom_call_target="tpu_custom_call" | custom-call | flops 17250000896 | tf_op jit(solution)/shard_map/pallas_call | solution.py:406
  271.3 5.0 %shard_map.426 = (bf16[256,1152]{1,0:T(8,128)(2,1)S(1)}, bf16[256,1536]{1,0:T(8,128)(2,1)S(1)}, f32[2,128]{1,0:T(2,128)S(1)}) custom-call(bf16[256,1536]{1,0:T(8,128)(2,1)S(1)} %collective-permute-done.30.dh_ref.refs_6_, bf16[256,1152]{1,0:T(8,128)(2,1)S(1)} %copy-done.67, bf16[1536,1280]{1,0:T(8,128)(2,1)S(1)} %bitcast.46, bf16[384,1536]{1,0:T(8,128)(2,1)S(1)} %bitcast.54, ...), custom_call_target="tpu_custom_call" | custom-call | flops 17250000896 | tf_op jit(solution)/shard_map/pallas_call | solution.py:406
  278.2 4.8 %shard_map.427 = (bf16[256,1152]{1,0:T(8,128)(2,1)S(1)}, bf16[256,1536]{1,0:T(8,128)(2,1)S(1)}, f32[2,128]{1,0:T(2,128)S(1)}) custom-call(bf16[256,1536]{1,0:T(8,128)(2,1)S(1)} %constant_dynamic-update-slice_fusion.4.dh_ref.refs_7_, bf16[256,1152]{1,0:T(8,128)(2,1)S(1)} %copy-done.65, bf16[1536,1280]{1,0:T(8,128)(2,1)S(1)} %bitcast.47, ...), custom_call_target="tpu_custom_call" | custom-call | flops 17250000896 | tf_op jit(solution)/shard_map/pallas_call | solution.py:406
  283.9 5.6 %shard_map.428 = (bf16[4,192,1152]{2,1,0:T(8,128)(2,1)S(1)}, bf16[4,192,1152]{2,1,0:T(8,128)(2,1)S(1)}) custom-call(s32[3]{0:T(128)S(1)} %pad_add_fusion.1.pos_ref, bf16[256,1536]{1,0:T(8,128)(2,1)S(1)} %copy-done.59, bf16[256,1536]{1,0:T(8,128)(2,1)S(1)} %copy-done.57, bf16[256,1536]{1,0:T(8,128)(2,1)S(1)} %copy-done.55, bf16[256,1536]{1,0:T(8,128)(2,1)S(1)} %copy-done.53, ...), custom_call_target="tpu_custom_call" | custom-call | flops 5750000128 | tf_op jit(solution)/shard_map/pallas_call | solution.py:406
  320.6 20.6 %collective-permute-done.35 = bf16[512,1536]{1,0:T(8,128)(2,1)} collective-permute-done((bf16[512,1536]{1,0:T(8,128)(2,1)}, bf16[512,1536]{1,0:T(8,128)(2,1)}, u32[]{:S(2)}, u32[]{:S(2)}) %collective-permute-start.35) | collective-permute-done | bytes 1572896 | tf_op jit(solution)/shard_map/ppermute | solution.py:432
  350.3 5.9 %collective-permute-done.39 = bf16[512,1536]{1,0:T(8,128)(2,1)} collective-permute-done((bf16[512,1536]{1,0:T(8,128)(2,1)}, bf16[512,1536]{1,0:T(8,128)(2,1)}, u32[]{:S(2)}, u32[]{:S(2)}) %collective-permute-start.39) | collective-permute-done | bytes 1572896 | tf_op jit(solution)/shard_map/ppermute | solution.py:432
  356.3 4.1 %collective-permute-done.40.refs_2_ = bf16[48,2048]{1,0:T(8,128)(2,1)S(1)} collective-permute-done((bf16[48,2048]{1,0:T(8,128)(2,1)S(1)}, bf16[48,2048]{1,0:T(8,128)(2,1)S(1)}, u32[]{:S(2)}, u32[]{:S(2)}) %collective-permute-start.40) | collective-permute-done | bytes 196640 | tf_op jit(solution)/shard_map/ppermute | solution.py:432
  363.8 4.4 %shard_map.432 = (f32[48,8192]{1,0:T(8,128)}, f32[48,8192]{1,0:T(8,128)}, f32[48,8192]{1,0:T(8,128)}, f32[8,48]{1,0:T(8,128)S(1)}) custom-call(s32[3]{0:T(128)S(1)} %pad_add_fusion.1.pos_ref, bf16[48,2048]{1,0:T(8,128)(2,1)S(1)} %get-tuple-element.228.refs_0_, bf16[48,2048]{1,0:T(8,128)(2,1)S(1)} %collective-permute-done.38.refs_1_, ...), custom_call_target="tpu_custom_call" | custom-call | flops 4600000000 | tf_op jit(solution)/shard_map/pallas_call | solution.py:406
  (383 shorter events, 191.2 us)
Async XLA Ops:
  7.2 77.0 %all-gather.7.cloned.1.call-start = ((), (), s32[]{:S(2)}) async-start(), calls=%async_computation.4 | async-start | bytes 5750784 | tf_op jit(solution)/shard_map/all_gather | solution.py:603
  21.9 121.1 %all-gather.9.cloned.1.call-start = ((), (), s32[]{:S(2)}) async-start(), calls=%async_computation.5 | async-start | bytes 7077888 | tf_op jit(solution)/shard_map/all_gather | solution.py:605
  22.0 30.0 %collective-permute-start.5 = (bf16[256,1536]{1,0:T(8,128)(2,1)S(1)}, bf16[256,1536]{1,0:T(8,128)(2,1)S(1)}, u32[]{:S(2)}, u32[]{:S(2)}) collective-permute-start(bf16[256,1536]{1,0:T(8,128)(2,1)S(1)} %copy-done), channel_id=1, source_target_pairs={{0,16},{8,24},{16,0},{24,8},{1,17},{9,25},{17,1},{25,9},{2,18},{10... | collective-permute-start | bytes 2359304 | tf_op jit(solution)/shard_map/ppermute | solution.py:432
  23.5 28.5 %collective-permute-start.3 = (bf16[256,1536]{1,0:T(8,128)(2,1)S(1)}, bf16[256,1536]{1,0:T(8,128)(2,1)S(1)}, u32[]{:S(2)}, u32[]{:S(2)}) collective-permute-start(bf16[256,1536]{1,0:T(8,128)(2,1)S(1)} %copy-done), channel_id=1, source_target_pairs={{0,8},{8,0},{16,24},{24,16},{1,9},{9,1},{17,25},{25,17},{2,10},{10... | collective-permute-start | bytes 2359304 | tf_op jit(solution)/shard_map/ppermute | solution.py:432
  26.0 20.4 %collective-permute-start.15 = (bf16[48,2048]{1,0:T(8,128)(2,1)S(1)}, bf16[48,2048]{1,0:T(8,128)(2,1)S(1)}, u32[]{:S(2)}, u32[]{:S(2)}) collective-permute-start(bf16[48,2048]{1,0:T(8,128)(2,1)S(1)} %get-tuple-element.161), channel_id=1, source_target_pairs={{0,8},{8,0},{16,24},{24,16},{1,9},{9,1},{17,25},{25,17},{2,10},{10... | collective-permute-start | bytes 589832 | tf_op jit(solution)/shard_map/ppermute | solution.py:432
  28.2 21.2 %collective-permute-start.17 = (bf16[48,2048]{1,0:T(8,128)(2,1)S(1)}, bf16[48,2048]{1,0:T(8,128)(2,1)S(1)}, u32[]{:S(2)}, u32[]{:S(2)}) collective-permute-start(bf16[48,2048]{1,0:T(8,128)(2,1)S(1)} %get-tuple-element.163), channel_id=1, source_target_pairs={{0,24},{8,16},{16,8},{24,0},{1,25},{9,17},{17,9},{25,1},{2,26},{10... | collective-permute-start | bytes 589832 | tf_op jit(solution)/shard_map/ppermute | solution.py:432
  52.0 129.6 %all-gather.11.cloned.1.call-start = ((), (), s32[]{:S(2)}) async-start(), calls=%async_computation.6 | async-start | bytes 3538944 | tf_op jit(solution)/shard_map/all_gather | solution.py:607
  68.7 249.9 %reduce-scatter.3.cloned.1.call-start = ((), (), s32[]{:S(2)}) async-start(), calls=%async_computation.2 | async-start | bytes 5898240 | tf_op jit(solution)/shard_map/reduce_scatter | solution.py:704
  80.6 26.1 %collective-permute-start.10 = (bf16[128,1536]{1,0:T(8,128)(2,1)}, bf16[128,1536]{1,0:T(8,128)(2,1)}, u32[]{:S(2)}, u32[]{:S(2)}) collective-permute-start(bf16[128,1536]{1,0:T(8,128)(2,1)} %slice.95), channel_id=1, source_target_pairs={{0,8},{8,0},{16,24},{24,16},{1,9},{9,1},{17,25},{25,17},{2,10},{10... | collective-permute-start | bytes 1179656 | tf_op jit(solution)/shard_map/ppermute | solution.py:432
  82.5 23.1 %collective-permute-start.8 = (bf16[128,1536]{1,0:T(8,128)(2,1)}, bf16[128,1536]{1,0:T(8,128)(2,1)}, u32[]{:S(2)}, u32[]{:S(2)}) collective-permute-start(bf16[128,1536]{1,0:T(8,128)(2,1)} %slice.94), channel_id=1, source_target_pairs={{0,16},{8,24},{16,0},{24,8},{1,17},{9,25},{17,1},{25,9},{2,18},{10... | collective-permute-start | bytes 1179656 | tf_op jit(solution)/shard_map/ppermute | solution.py:432
  95.1 21.4 %collective-permute-start.13 = (bf16[256,1536]{1,0:T(8,128)(2,1)S(1)}, bf16[256,1536]{1,0:T(8,128)(2,1)S(1)}, u32[]{:S(2)}, u32[]{:S(2)}) collective-permute-start(bf16[256,1536]{1,0:T(8,128)(2,1)S(1)} %get-tuple-element.158), channel_id=1, source_target_pairs={{0,24},{8,16},{16,8},{24,0},{1,25},{9,17},{17,9},{25,1},{2,26},{10... | collective-permute-start | bytes 2359304 | tf_op jit(solution)/shard_map/ppermute | solution.py:432
  98.8 27.3 %collective-permute-start.12 = (bf16[256,1536]{1,0:T(8,128)(2,1)S(1)}, bf16[256,1536]{1,0:T(8,128)(2,1)S(1)}, u32[]{:S(2)}, u32[]{:S(2)}) collective-permute-start(bf16[256,1536]{1,0:T(8,128)(2,1)S(1)} %get-tuple-element.157), channel_id=1, source_target_pairs={{0,16},{8,24},{16,0},{24,8},{1,17},{9,25},{17,1},{25,9},{2,18},{10... | collective-permute-start | bytes 2359304 | tf_op jit(solution)/shard_map/ppermute | solution.py:432
  104.2 22.2 %collective-permute-start.11 = (bf16[256,1536]{1,0:T(8,128)(2,1)S(1)}, bf16[256,1536]{1,0:T(8,128)(2,1)S(1)}, u32[]{:S(2)}, u32[]{:S(2)}) collective-permute-start(bf16[256,1536]{1,0:T(8,128)(2,1)S(1)} %get-tuple-element.156), channel_id=1, source_target_pairs={{0,8},{8,0},{16,24},{24,16},{1,9},{9,1},{17,25},{25,17},{2,10},{10... | collective-permute-start | bytes 2359304 | tf_op jit(solution)/shard_map/ppermute | solution.py:432
  128.9 19.4 %collective-permute-start.18 = (bf16[256,1536]{1,0:T(8,128)(2,1)S(1)}, bf16[256,1536]{1,0:T(8,128)(2,1)}, u32[]{:S(2)}, u32[]{:S(2)}) collective-permute-start(bf16[256,1536]{1,0:T(8,128)(2,1)S(1)} %multiply_convert_fusion.refs_0_), channel_id=1, source_target_pairs={{0,16},{8,24},{16,0},{24,8},{1,17},{9,25},{17,1},{25,9},{2,18},{10... | collective-permute-start | bytes 2359304 | tf_op jit(solution)/shard_map/ppermute | solution.py:432
  130.4 20.0 %collective-permute-start.14 = (bf16[256,1536]{1,0:T(8,128)(2,1)S(1)}, bf16[256,1536]{1,0:T(8,128)(2,1)}, u32[]{:S(2)}, u32[]{:S(2)}) collective-permute-start(bf16[256,1536]{1,0:T(8,128)(2,1)S(1)} %multiply_convert_fusion.refs_0_), channel_id=1, source_target_pairs={{0,8},{8,0},{16,24},{24,16},{1,9},{9,1},{17,25},{25,17},{2,10},{10... | collective-permute-start | bytes 2359304 | tf_op jit(solution)/shard_map/ppermute | solution.py:432
  161.3 33.7 %collective-permute-start.22 = (bf16[512,768]{1,0:T(8,128)(2,1)}, bf16[512,768]{1,0:T(8,128)(2,1)}, u32[]{:S(2)}, u32[]{:S(2)}) collective-permute-start(bf16[512,768]{1,0:T(8,128)(2,1)} %get-tuple-element.180), channel_id=1, source_target_pairs={{0,4},{4,0},{1,5},{5,1},{2,6},{6,2},{3,7},{7,3},{8,12},{12,8},{9,1... | collective-permute-start | bytes 2359304 | tf_op jit(solution)/shard_map/ppermute | solution.py:435
  169.9 25.2 %collective-permute-start.23 = (bf16[512,768]{1,0:T(8,128)(2,1)}, bf16[512,768]{1,0:T(8,128)(2,1)}, u32[]{:S(2)}, u32[]{:S(2)}) collective-permute-start(bf16[512,768]{1,0:T(8,128)(2,1)} %get-tuple-element.182), channel_id=1, source_target_pairs={{0,4},{4,0},{1,5},{5,1},{2,6},{6,2},{3,7},{7,3},{8,12},{12,8},{9,1... | collective-permute-start | bytes 2359304 | tf_op jit(solution)/shard_map/ppermute | solution.py:435
  201.1 37.9 %collective-permute-start.21 = (bf16[256,1536]{1,0:T(8,128)(2,1)}, bf16[256,1536]{1,0:T(8,128)(2,1)S(1)}, u32[]{:S(2)}, u32[]{:S(2)}) collective-permute-start(bf16[256,1536]{1,0:T(8,128)(2,1)} %get-tuple-element.178), channel_id=1, source_target_pairs={{0,8},{8,0},{16,24},{24,16},{1,9},{9,1},{17,25},{25,17},{2,10},{10... | collective-permute-start | bytes 2359304 | tf_op jit(solution)/shard_map/ppermute | solution.py:432
  202.6 36.4 %collective-permute-start.27 = (bf16[256,1536]{1,0:T(8,128)(2,1)S(1)}, bf16[256,1536]{1,0:T(8,128)(2,1)}, u32[]{:S(2)}, u32[]{:S(2)}) collective-permute-start(bf16[256,1536]{1,0:T(8,128)(2,1)S(1)} %get-tuple-element.190), channel_id=1, source_target_pairs={{0,16},{8,24},{16,0},{24,8},{1,17},{9,25},{17,1},{25,9},{2,18},{10... | collective-permute-start | bytes 2359304 | tf_op jit(solution)/shard_map/ppermute | solution.py:432
  207.0 32.0 %collective-permute-start.28 = (bf16[256,1536]{1,0:T(8,128)(2,1)S(1)}, bf16[256,1536]{1,0:T(8,128)(2,1)}, u32[]{:S(2)}, u32[]{:S(2)}) collective-permute-start(bf16[256,1536]{1,0:T(8,128)(2,1)S(1)} %get-tuple-element.192), channel_id=1, source_target_pairs={{0,24},{8,16},{16,8},{24,0},{1,25},{9,17},{17,9},{25,1},{2,26},{10... | collective-permute-start | bytes 2359304 | tf_op jit(solution)/shard_map/ppermute | solution.py:432
  220.4 147.9 %reduce-scatter.5.cloned.1.call-start = ((), (), s32[]{:S(2)}) async-start(), calls=%async_computation.3 | async-start | bytes 2949120 | tf_op jit(solution)/shard_map/reduce_scatter | solution.py:744
  304.4 36.8 %collective-permute-start.35 = (bf16[512,1536]{1,0:T(8,128)(2,1)}, bf16[512,1536]{1,0:T(8,128)(2,1)}, u32[]{:S(2)}, u32[]{:S(2)}) collective-permute-start(bf16[512,1536]{1,0:T(8,128)(2,1)} %copy-done.27), channel_id=1, source_target_pairs={{0,8},{8,0},{16,24},{24,16},{1,9},{9,1},{17,25},{25,17},{2,10},{10... | collective-permute-start | bytes 4718600 | tf_op jit(solution)/shard_map/ppermute | solution.py:432
  314.4 41.9 %collective-permute-start.39 = (bf16[512,1536]{1,0:T(8,128)(2,1)}, bf16[512,1536]{1,0:T(8,128)(2,1)}, u32[]{:S(2)}, u32[]{:S(2)}) collective-permute-start(bf16[512,1536]{1,0:T(8,128)(2,1)} %pad_maximum_fusion), channel_id=1, source_target_pairs={{0,16},{8,24},{16,0},{24,8},{1,17},{9,25},{17,1},{25,9},{2,18},{10... | collective-permute-start | bytes 4718600 | tf_op jit(solution)/shard_map/ppermute | solution.py:432
  347.0 30.5 %collective-permute-start.45 = (bf16[256,1536]{1,0:T(8,128)(2,1)}, bf16[256,1536]{1,0:T(8,128)(2,1)}, u32[]{:S(2)}, u32[]{:S(2)}) collective-permute-start(bf16[256,1536]{1,0:T(8,128)(2,1)} %add_convert_fusion.2), channel_id=1, source_target_pairs={{0,16},{8,24},{16,0},{24,8},{1,17},{9,25},{17,1},{25,9},{2,18},{10... | collective-permute-start | bytes 2359304 | tf_op jit(solution)/shard_map/ppermute | solution.py:432
  (137 other events, 1003.2 us)
Sparse Core Ops, SparseCore 0:
  22.0 55.1 all-gather.6
  79.4 63.5 all-gather.8
  144.6 36.9 all-gather.10
  220.5 82.3 reduce-scatter.2
  305.0 48.5 reduce-scatter.4

commit v4 on v3

--- a/solution.py
+++ b/solution.py
@@ -727,19 +727,17 @@
             scratch=(pltpu.VMEM((length, LOCAL_Q), F32),),
         )
     half = PLANE * count // 2
-    stat = grp.everyone(grp.everyone(add_up(stats), half), half // 2)
-    y_got = grp.plane(tie(y_parts[2], stat), 1)
+    stat = grp.everyone(add_up(stats), half)
     qkv_halves = weight_grad(grp, normed_one, dp_blocks, PLANE)
     out_halves = weight_grad(grp, [tie(merged[0], stat), *merged[1:]], dh_blocks, 1)
-    dn1_got = grp.plane(tie(jnp.concatenate([dn1_parts[2], dn1_parts[3]], axis=0), stat), 2)
-    step = half // 4
-    while step:
-        stat = grp.everyone(stat, step)
-        step //= 2
+    stat = grp.everyone(stat, half // 2)
+    y_got = grp.plane(tie(y_parts[2], stat), 1)
+    dn1_message = jnp.concatenate([dn1_parts[2], dn1_parts[3]], axis=0)
+    dn1_got = grp.plane(dn1_message, 2)
     first_chunks = call(
         functools.partial(chunk_first_kernel, members),
         (shaped(d, rows, PLANE * 3 * LOCAL_Q + width),),
-        (*core_terms(grp, qkv_halves), *core_terms(grp, out_halves)),
+        (*core_terms(grp, qkv_halves), *late(core_terms(grp, out_halves), dn1_message, stat)),
     )[0]
     first_sum = to_owner(first_chunks)
 
@@ -750,6 +748,11 @@
         (rows, 2 * LOCAL_FF),
         (shaped(*down_weight.shape, dtype=F32),),
     )
+    stat = tie(stat, gateup_pieces[0])
+    step = half // 4
+    while step:
+        stat = grp.everyone(stat, step)
+        step //= 2
     gateup_pieces = exchange(grp, gateup_pieces)
     y_got = tie(y_got, gateup_pieces[0])
     y_sent, y_last = plane_scatter_second(grp, y_parts[1], 1, y_got)

time: 399 us -> 395 us (0.990)
  waiting for transfers between devices: 150 us -> 140 us
    ppermute x38, waiting for transfers between devices: 120 us -> 116 us  [plane(): return lax.ppermute(value, 'j', [(i, i ^ r) for i in range(PLANE)])]
    unnamed x215 -> x208, local copies, waits for them, and re-layouts: 39.6 us -> 41.7 us
  transfers between devices with their start and end apart: 55 -> 55, of which waited for: 26 -> 23; matrix products, arithmetic and copies ran while one was open for 9% -> 10% of each run, Pallas kernels for 24% -> 24%
where the time goes in v4:
time: 395 us; the launch traced here: 391 us
  waiting for transfers between devices  140 us (35%)
  Pallas kernels  100 us (25%)
  starting transfers between devices  53.2 us (13%)
  local copies, waits for them, and re-layouts  48.7 us (12%)
  other arithmetic  31.3 us (8%)
  between operations  18.1 us (5%)
    ppermute x38, waiting for transfers between devices, plane(): return lax.ppermute(value, 'j', [(i, i ^ r) for i in range(PLANE)])  116 us
    pallas_call x28, Pallas kernels, call(): pl.pallas_call(kernel, out_shape=tuple(outs), in_specs=specs or [VMEM] *...  100 us
    ppermute x38, starting transfers between devices, plane(): return lax.ppermute(value, 'j', [(i, i ^ r) for i in range(PLANE)])  46.1 us
    unnamed x208, local copies, waits for them, and re-layouts  41.7 us
    all_gather x1, waiting for transfers between devices, per_device(): second_all = everywhere(tie(second_message, *x_near[1:]))  12 us
  transfers between devices with their start and end apart: 55, of which 23 were waited for; matrix products, arithmetic and copies ran while one was open for 10% of the time, Pallas kernels for 24%

profile of v4, /device:TPU:0, one launch (start us, length us, event | category | flops | bytes accessed | tf_op | source)
XLA Modules:
  0.0 391.4 jit_solution(14512620241194324255)
XLA Ops:
  16.5 3.8 collective-permute-done.1.refs_2_
  29.6 16.9 %collective-permute-done.15.refs_1_ = bf16[48,2048]{1,0:T(8,128)(2,1)S(1)} collective-permute-done((bf16[48,2048]{1,0:T(8,128)(2,1)S(1)}, bf16[48,2048]{1,0:T(8,128)(2,1)S(1)}, u32[]{:S(2)}, u32[]{:S(2)}) %collective-permute-start.15) | collective-permute-done | bytes 196640 | tf_op jit(solution)/shard_map/ppermute | solution.py:432
  54.8 7.9 %collective-permute-done.4 = bf16[128,1536]{1,0:T(8,128)(2,1)S(1)} collective-permute-done((bf16[128,1536]{1,0:T(8,128)(2,1)S(1)}, bf16[128,1536]{1,0:T(8,128)(2,1)S(1)}, u32[]{:S(2)}, u32[]{:S(2)}) %collective-permute-start.4) | collective-permute-done | bytes 393248 | tf_op jit(solution)/shard_map/ppermute | solution.py:432
  68.7 11.1 %collective-permute-done.9.refs_4_.refs_0_ = bf16[256,1536]{1,0:T(8,128)(2,1)S(1)} collective-permute-done((bf16[256,1536]{1,0:T(8,128)(2,1)S(1)}, bf16[256,1536]{1,0:T(8,128)(2,1)S(1)}, u32[]{:S(2)}, u32[]{:S(2)}) %collective-permute-start.9) | collective-permute-done | bytes 786464 | tf_op jit(solution)/shard_map/ppermute | solution.py:432
  112.3 4.2 %collective-permute-done.13 = bf16[256,1536]{1,0:T(8,128)(2,1)S(1)} collective-permute-done((bf16[256,1536]{1,0:T(8,128)(2,1)S(1)}, bf16[256,1536]{1,0:T(8,128)(2,1)S(1)}, u32[]{:S(2)}, u32[]{:S(2)}) %collective-permute-start.13) | collective-permute-done | bytes 786464 | tf_op jit(solution)/shard_map/ppermute | solution.py:432
  116.6 9.6 %collective-permute-done.12 = bf16[256,1536]{1,0:T(8,128)(2,1)S(1)} collective-permute-done((bf16[256,1536]{1,0:T(8,128)(2,1)S(1)}, bf16[256,1536]{1,0:T(8,128)(2,1)S(1)}, u32[]{:S(2)}, u32[]{:S(2)}) %collective-permute-start.12) | collective-permute-done | bytes 786464 | tf_op jit(solution)/shard_map/ppermute | solution.py:432
  131.0 12.0 %all-gather.9.cloned.1.call-done = bf16[32,48,2048]{2,1,0:T(8,128)(2,1)} async-done(((bf16[4,48,2048]{2,1,0:T(8,128)(2,1)}), bf16[32,48,2048]{2,1,0:T(8,128)(2,1)}) %all-gather.9.cloned.1.call-update) | async-done | bytes 6291472 | tf_op jit(solution)/shard_map/all_gather | solution.py:605
  153.2 5.2 %shard_map.417 = (bf16[512,1024]{1,0:T(8,128)(2,1)S(1)}, bf16[512,1024]{1,0:T(8,128)(2,1)S(1)}, bf16[512,1024]{1,0:T(8,128)(2,1)S(1)}, bf16[512,768]{1,0:T(8,128)(2,1)S(1)}, bf16[512,768]{1,0:T(8,128)(2,1)}) custom-call(s32[3]{0:T(128)S(1)} %pad_add_fusion.1.pos_ref, bf16[256,1536]{1,0:T(8,128)(2,1)S(1)} %multiply_convert_fusion.refs_0_, ...), custom_call_target="tpu_custom_call" | custom-call | flops 5750000128 | tf_op jit(solution)/shard_map/pallas_call | solution.py:406
  161.6 5.5 %shard_map.418 = (bf16[512,1024]{1,0:T(8,128)(2,1)S(1)}, bf16[512,1024]{1,0:T(8,128)(2,1)S(1)}, bf16[512,1024]{1,0:T(8,128)(2,1)S(1)}, bf16[512,768]{1,0:T(8,128)(2,1)S(1)}, bf16[512,768]{1,0:T(8,128)(2,1)}) custom-call(s32[3]{0:T(128)S(1)} %pad_add_fusion.1.pos_ref, bf16[256,1536]{1,0:T(8,128)(2,1)} %collective-permute-done.18.refs_0_, ...), custom_call_target="tpu_custom_call" | custom-call | flops 5750000128 | tf_op jit(solution)/shard_map/pallas_call | solution.py:406
  170.2 4.1 %shard_map.419 = (bf16[512,1536]{1,0:T(8,128)(2,1)S(1)}, bf16[512,1536]{1,0:T(8,128)(2,1)S(1)}) custom-call(s32[3]{0:T(128)S(1)} %pad_add_fusion.1.pos_ref, bf16[512,1024]{1,0:T(8,128)(2,1)S(1)} %get-tuple-element.168.refs_0_, bf16[512,1024]{1,0:T(8,128)(2,1)S(1)} %get-tuple-element.172.refs_1_, ...), custom_call_target="tpu_custom_call" | custom-call | flops 4600000000 | tf_op jit(solution)/shard_map/pallas_call | solution.py:406
  177.5 4.0 %all-gather.11.cloned.1.call-done = bf16[1024,1536]{1,0:T(8,128)(2,1)} async-done(((bf16[128,1536]{1,0:T(8,128)(2,1)}), bf16[1024,1536]{1,0:T(8,128)(2,1)}) %all-gather.11.cloned.1.call-update) | async-done | bytes 3145744 | tf_op jit(solution)/shard_map/all_gather | solution.py:607
  188.7 6.1 %shard_map.420 = (bf16[256,1536]{1,0:T(8,128)(2,1)S(1)}, bf16[256,1536]{1,0:T(8,128)(2,1)}, bf16[512,2048]{1,0:T(8,128)(2,1)S(1)}) custom-call(bf16[256,1536]{1,0:T(8,128)(2,1)S(1)} %convert_multiply_fusion.2.refs_2_.refs_0_, bf16[256,1536]{1,0:T(8,128)(2,1)S(1)} %collective-permute-done.7.refs_3_.refs_1_, bf16[512,1024]{1,0:T(8,128)(2,1)S(1)} %copy-done.43, ...), custom_call_target="tpu_custom_call" | custom-call | flops 5750000128 | tf_op jit(solution)/shard_map/pallas_call | solution.py:406
  195.3 5.2 %shard_map.421 = (bf16[256,1536]{1,0:T(8,128)(2,1)S(1)}, bf16[256,1536]{1,0:T(8,128)(2,1)S(1)}, bf16[512,2048]{1,0:T(8,128)(2,1)S(1)}) custom-call(bf16[256,1536]{1,0:T(8,128)(2,1)S(1)} %collective-permute-done.9.refs_4_.refs_0_, bf16[256,1536]{1,0:T(8,128)(2,1)S(1)} %copy-done.13, bf16[512,1024]{1,0:T(8,128)(2,1)S(1)} %copy-done.47, ...), custom_call_target="tpu_custom_call" | custom-call | flops 5750000128 | tf_op jit(solution)/shard_map/pallas_call | solution.py:406
  209.4 8.8 %shard_map.422 = bf16[4,288,2048]{2,1,0:T(8,128)(2,1)S(1)} custom-call(bf16[512,768]{1,0:T(8,128)(2,1)S(1)} %copy-done.73, bf16[512,768]{1,0:T(8,128)(2,1)} %collective-permute-done.22.refs_1_, bf16[512,768]{1,0:T(8,128)(2,1)S(1)} %copy-done.75, bf16[512,768]{1,0:T(8,128)(2,1)} %collective-permute-done.23.refs_3_, ...), custom_call_target="tpu_custom_call" | custom-call | flops 8625000448 | tf_op jit(solution)/shard_map/pallas_call | solution.py:406
  220.8 18.2 %collective-permute-done.28 = bf16[256,1536]{1,0:T(8,128)(2,1)} collective-permute-done((bf16[256,1536]{1,0:T(8,128)(2,1)S(1)}, bf16[256,1536]{1,0:T(8,128)(2,1)}, u32[]{:S(2)}, u32[]{:S(2)}) %collective-permute-start.28) | collective-permute-done | bytes 786464 | tf_op jit(solution)/shard_map/ppermute | solution.py:432
  242.1 3.8 fusion.19
  252.5 4.8 %shard_map.424 = (bf16[256,1152]{1,0:T(8,128)(2,1)S(1)}, bf16[256,1536]{1,0:T(8,128)(2,1)S(1)}, f32[2,128]{1,0:T(2,128)S(1)}) custom-call(bf16[256,1536]{1,0:T(8,128)(2,1)S(1)} %get-tuple-element.198.dh_ref.refs_4_, bf16[256,1152]{1,0:T(8,128)(2,1)S(1)} %copy-done.71, bf16[1536,1280]{1,0:T(8,128)(2,1)S(1)} %bitcast.44, bf16[384,1536]{1,0:T(8,128)(2,1)S(1)} %bitcast.52, ...), custom_call_target="tpu_custom_call" | custom-call | flops 17250000896 | tf_op jit(solution)/shard_map/pallas_call | solution.py:406
  257.3 7.4 %collective-permute-done.30.dh_ref.refs_6_ = bf16[256,1536]{1,0:T(8,128)(2,1)S(1)} collective-permute-done((bf16[256,1536]{1,0:T(8,128)(2,1)S(1)}, bf16[256,1536]{1,0:T(8,128)(2,1)S(1)}, u32[]{:S(2)}, u32[]{:S(2)}) %collective-permute-start.30) | collective-permute-done | bytes 786464 | tf_op jit(solution)/shard_map/ppermute | solution.py:432
  266.9 4.8 %shard_map.425 = (bf16[256,1152]{1,0:T(8,128)(2,1)S(1)}, bf16[256,1536]{1,0:T(8,128)(2,1)S(1)}, f32[2,128]{1,0:T(2,128)S(1)}) custom-call(bf16[256,1536]{1,0:T(8,128)(2,1)S(1)} %collective-permute-done.29.dh_ref.refs_5_, bf16[256,1152]{1,0:T(8,128)(2,1)S(1)} %copy-done.69, bf16[1536,1280]{1,0:T(8,128)(2,1)S(1)} %bitcast.45, bf16[384,1536]{1,0:T(8,128)(2,1)S(1)} %bitcast.53, ...), custom_call_target="tpu_custom_call" | custom-call | flops 17250000896 | tf_op jit(solution)/shard_map/pallas_call | solution.py:406
  271.7 5.0 %shard_map.426 = (bf16[256,1152]{1,0:T(8,128)(2,1)S(1)}, bf16[256,1536]{1,0:T(8,128)(2,1)S(1)}, f32[2,128]{1,0:T(2,128)S(1)}) custom-call(bf16[256,1536]{1,0:T(8,128)(2,1)S(1)} %collective-permute-done.30.dh_ref.refs_6_, bf16[256,1152]{1,0:T(8,128)(2,1)S(1)} %copy-done.67, bf16[1536,1280]{1,0:T(8,128)(2,1)S(1)} %bitcast.46, bf16[384,1536]{1,0:T(8,128)(2,1)S(1)} %bitcast.54, ...), custom_call_target="tpu_custom_call" | custom-call | flops 17250000896 | tf_op jit(solution)/shard_map/pallas_call | solution.py:406
  277.8 4.8 %shard_map.427 = (bf16[256,1152]{1,0:T(8,128)(2,1)S(1)}, bf16[256,1536]{1,0:T(8,128)(2,1)S(1)}, f32[2,128]{1,0:T(2,128)S(1)}) custom-call(bf16[256,1536]{1,0:T(8,128)(2,1)S(1)} %constant_dynamic-update-slice_fusion.4.dh_ref.refs_7_, bf16[256,1152]{1,0:T(8,128)(2,1)S(1)} %copy-done.65, bf16[1536,1280]{1,0:T(8,128)(2,1)S(1)} %bitcast.47, ...), custom_call_target="tpu_custom_call" | custom-call | flops 17250000896 | tf_op jit(solution)/shard_map/pallas_call | solution.py:406
  282.6 5.6 %shard_map.428 = (bf16[4,192,1152]{2,1,0:T(8,128)(2,1)S(1)}, bf16[4,192,1152]{2,1,0:T(8,128)(2,1)S(1)}) custom-call(s32[3]{0:T(128)S(1)} %pad_add_fusion.1.pos_ref, bf16[256,1536]{1,0:T(8,128)(2,1)S(1)} %copy-done.59, bf16[256,1536]{1,0:T(8,128)(2,1)S(1)} %copy-done.57, bf16[256,1536]{1,0:T(8,128)(2,1)S(1)} %copy-done.55, bf16[256,1536]{1,0:T(8,128)(2,1)S(1)} %copy-done.53, ...), custom_call_target="tpu_custom_call" | custom-call | flops 5750000128 | tf_op jit(solution)/shard_map/pallas_call | solution.py:406
  312.4 26.7 %collective-permute-done.35 = bf16[512,1536]{1,0:T(8,128)(2,1)} collective-permute-done((bf16[512,1536]{1,0:T(8,128)(2,1)}, bf16[512,1536]{1,0:T(8,128)(2,1)}, u32[]{:S(2)}, u32[]{:S(2)}) %collective-permute-start.35) | collective-permute-done | bytes 1572896 | tf_op jit(solution)/shard_map/ppermute | solution.py:432
  358.6 5.0 %shard_map.432 = (f32[48,8192]{1,0:T(8,128)}, f32[48,8192]{1,0:T(8,128)}, f32[48,8192]{1,0:T(8,128)}, f32[8,48]{1,0:T(8,128)S(1)}) custom-call(s32[3]{0:T(128)S(1)} %pad_add_fusion.1.pos_ref, bf16[48,2048]{1,0:T(8,128)(2,1)S(1)} %copy-done.41, bf16[48,2048]{1,0:T(8,128)(2,1)} %collective-permute-done.38.refs_1_, ...), custom_call_target="tpu_custom_call" | custom-call | flops 4600000000 | tf_op jit(solution)/shard_map/pallas_call | solution.py:406
  (376 shorter events, 183.0 us)
Async XLA Ops:
  7.2 77.0 %all-gather.7.cloned.1.call-start = ((), (), s32[]{:S(2)}) async-start(), calls=%async_computation.4 | async-start | bytes 5750784 | tf_op jit(solution)/shard_map/all_gather | solution.py:603
  21.9 121.1 %all-gather.9.cloned.1.call-start = ((), (), s32[]{:S(2)}) async-start(), calls=%async_computation.5 | async-start | bytes 7077888 | tf_op jit(solution)/shard_map/all_gather | solution.py:605
  22.0 30.0 %collective-permute-start.5 = (bf16[256,1536]{1,0:T(8,128)(2,1)S(1)}, bf16[256,1536]{1,0:T(8,128)(2,1)S(1)}, u32[]{:S(2)}, u32[]{:S(2)}) collective-permute-start(bf16[256,1536]{1,0:T(8,128)(2,1)S(1)} %copy-done), channel_id=1, source_target_pairs={{0,16},{8,24},{16,0},{24,8},{1,17},{9,25},{17,1},{25,9},{2,18},{10... | collective-permute-start | bytes 2359304 | tf_op jit(solution)/shard_map/ppermute | solution.py:432
  23.5 28.5 %collective-permute-start.3 = (bf16[256,1536]{1,0:T(8,128)(2,1)S(1)}, bf16[256,1536]{1,0:T(8,128)(2,1)S(1)}, u32[]{:S(2)}, u32[]{:S(2)}) collective-permute-start(bf16[256,1536]{1,0:T(8,128)(2,1)S(1)} %copy-done), channel_id=1, source_target_pairs={{0,8},{8,0},{16,24},{24,16},{1,9},{9,1},{17,25},{25,17},{2,10},{10... | collective-permute-start | bytes 2359304 | tf_op jit(solution)/shard_map/ppermute | solution.py:432
  26.0 20.4 %collective-permute-start.15 = (bf16[48,2048]{1,0:T(8,128)(2,1)S(1)}, bf16[48,2048]{1,0:T(8,128)(2,1)S(1)}, u32[]{:S(2)}, u32[]{:S(2)}) collective-permute-start(bf16[48,2048]{1,0:T(8,128)(2,1)S(1)} %get-tuple-element.162), channel_id=1, source_target_pairs={{0,8},{8,0},{16,24},{24,16},{1,9},{9,1},{17,25},{25,17},{2,10},{10... | collective-permute-start | bytes 589832 | tf_op jit(solution)/shard_map/ppermute | solution.py:432
  28.2 21.2 %collective-permute-start.17 = (bf16[48,2048]{1,0:T(8,128)(2,1)S(1)}, bf16[48,2048]{1,0:T(8,128)(2,1)S(1)}, u32[]{:S(2)}, u32[]{:S(2)}) collective-permute-start(bf16[48,2048]{1,0:T(8,128)(2,1)S(1)} %get-tuple-element.164), channel_id=1, source_target_pairs={{0,24},{8,16},{16,8},{24,0},{1,25},{9,17},{17,9},{25,1},{2,26},{10... | collective-permute-start | bytes 589832 | tf_op jit(solution)/shard_map/ppermute | solution.py:432
  52.0 129.5 %all-gather.11.cloned.1.call-start = ((), (), s32[]{:S(2)}) async-start(), calls=%async_computation.6 | async-start | bytes 3538944 | tf_op jit(solution)/shard_map/all_gather | solution.py:607
  68.7 235.2 %reduce-scatter.3.cloned.1.call-start = ((), (), s32[]{:S(2)}) async-start(), calls=%async_computation.2 | async-start | bytes 5898240 | tf_op jit(solution)/shard_map/reduce_scatter | solution.py:704
  80.6 26.1 %collective-permute-start.10 = (bf16[128,1536]{1,0:T(8,128)(2,1)}, bf16[128,1536]{1,0:T(8,128)(2,1)}, u32[]{:S(2)}, u32[]{:S(2)}) collective-permute-start(bf16[128,1536]{1,0:T(8,128)(2,1)} %slice.95), channel_id=1, source_target_pairs={{0,8},{8,0},{16,24},{24,16},{1,9},{9,1},{17,25},{25,17},{2,10},{10... | collective-permute-start | bytes 1179656 | tf_op jit(solution)/shard_map/ppermute | solution.py:432
  82.5 23.2 %collective-permute-start.8 = (bf16[128,1536]{1,0:T(8,128)(2,1)}, bf16[128,1536]{1,0:T(8,128)(2,1)}, u32[]{:S(2)}, u32[]{:S(2)}) collective-permute-start(bf16[128,1536]{1,0:T(8,128)(2,1)} %slice.94), channel_id=1, source_target_pairs={{0,16},{8,24},{16,0},{24,8},{1,17},{9,25},{17,1},{25,9},{2,18},{10... | collective-permute-start | bytes 1179656 | tf_op jit(solution)/shard_map/ppermute | solution.py:432
  95.2 21.4 %collective-permute-start.13 = (bf16[256,1536]{1,0:T(8,128)(2,1)S(1)}, bf16[256,1536]{1,0:T(8,128)(2,1)S(1)}, u32[]{:S(2)}, u32[]{:S(2)}) collective-permute-start(bf16[256,1536]{1,0:T(8,128)(2,1)S(1)} %get-tuple-element.159), channel_id=1, source_target_pairs={{0,24},{8,16},{16,8},{24,0},{1,25},{9,17},{17,9},{25,1},{2,26},{10... | collective-permute-start | bytes 2359304 | tf_op jit(solution)/shard_map/ppermute | solution.py:432
  98.9 27.3 %collective-permute-start.12 = (bf16[256,1536]{1,0:T(8,128)(2,1)S(1)}, bf16[256,1536]{1,0:T(8,128)(2,1)S(1)}, u32[]{:S(2)}, u32[]{:S(2)}) collective-permute-start(bf16[256,1536]{1,0:T(8,128)(2,1)S(1)} %get-tuple-element.158), channel_id=1, source_target_pairs={{0,16},{8,24},{16,0},{24,8},{1,17},{9,25},{17,1},{25,9},{2,18},{10... | collective-permute-start | bytes 2359304 | tf_op jit(solution)/shard_map/ppermute | solution.py:432
  104.3 22.2 %collective-permute-start.11 = (bf16[256,1536]{1,0:T(8,128)(2,1)S(1)}, bf16[256,1536]{1,0:T(8,128)(2,1)S(1)}, u32[]{:S(2)}, u32[]{:S(2)}) collective-permute-start(bf16[256,1536]{1,0:T(8,128)(2,1)S(1)} %get-tuple-element.157), channel_id=1, source_target_pairs={{0,8},{8,0},{16,24},{24,16},{1,9},{9,1},{17,25},{25,17},{2,10},{10... | collective-permute-start | bytes 2359304 | tf_op jit(solution)/shard_map/ppermute | solution.py:432
  161.3 33.7 %collective-permute-start.22 = (bf16[512,768]{1,0:T(8,128)(2,1)}, bf16[512,768]{1,0:T(8,128)(2,1)}, u32[]{:S(2)}, u32[]{:S(2)}) collective-permute-start(bf16[512,768]{1,0:T(8,128)(2,1)} %get-tuple-element.181), channel_id=1, source_target_pairs={{0,4},{4,0},{1,5},{5,1},{2,6},{6,2},{3,7},{7,3},{8,12},{12,8},{9,1... | collective-permute-start | bytes 2359304 | tf_op jit(solution)/shard_map/ppermute | solution.py:435
  170.0 25.1 %collective-permute-start.23 = (bf16[512,768]{1,0:T(8,128)(2,1)}, bf16[512,768]{1,0:T(8,128)(2,1)}, u32[]{:S(2)}, u32[]{:S(2)}) collective-permute-start(bf16[512,768]{1,0:T(8,128)(2,1)} %get-tuple-element.183), channel_id=1, source_target_pairs={{0,4},{4,0},{1,5},{5,1},{2,6},{6,2},{3,7},{7,3},{8,12},{12,8},{9,1... | collective-permute-start | bytes 2359304 | tf_op jit(solution)/shard_map/ppermute | solution.py:435
  201.1 37.9 %collective-permute-start.21 = (bf16[256,1536]{1,0:T(8,128)(2,1)}, bf16[256,1536]{1,0:T(8,128)(2,1)}, u32[]{:S(2)}, u32[]{:S(2)}) collective-permute-start(bf16[256,1536]{1,0:T(8,128)(2,1)} %get-tuple-element.179), channel_id=1, source_target_pairs={{0,8},{8,0},{16,24},{24,16},{1,9},{9,1},{17,25},{25,17},{2,10},{10... | collective-permute-start | bytes 2359304 | tf_op jit(solution)/shard_map/ppermute | solution.py:432
  202.6 36.4 %collective-permute-start.27 = (bf16[256,1536]{1,0:T(8,128)(2,1)S(1)}, bf16[256,1536]{1,0:T(8,128)(2,1)}, u32[]{:S(2)}, u32[]{:S(2)}) collective-permute-start(bf16[256,1536]{1,0:T(8,128)(2,1)S(1)} %get-tuple-element.191), channel_id=1, source_target_pairs={{0,16},{8,24},{16,0},{24,8},{1,17},{9,25},{17,1},{25,9},{2,18},{10... | collective-permute-start | bytes 2359304 | tf_op jit(solution)/shard_map/ppermute | solution.py:432
  207.0 32.0 %collective-permute-start.28 = (bf16[256,1536]{1,0:T(8,128)(2,1)S(1)}, bf16[256,1536]{1,0:T(8,128)(2,1)}, u32[]{:S(2)}, u32[]{:S(2)}) collective-permute-start(bf16[256,1536]{1,0:T(8,128)(2,1)S(1)} %get-tuple-element.193), channel_id=1, source_target_pairs={{0,24},{8,16},{16,8},{24,0},{1,25},{9,17},{17,9},{25,1},{2,26},{10... | collective-permute-start | bytes 2359304 | tf_op jit(solution)/shard_map/ppermute | solution.py:432
  220.3 143.3 %reduce-scatter.5.cloned.1.call-start = ((), (), s32[]{:S(2)}) async-start(), calls=%async_computation.3 | async-start | bytes 2949120 | tf_op jit(solution)/shard_map/reduce_scatter | solution.py:742
  302.7 36.4 %collective-permute-start.35 = (bf16[512,1536]{1,0:T(8,128)(2,1)}, bf16[512,1536]{1,0:T(8,128)(2,1)}, u32[]{:S(2)}, u32[]{:S(2)}) collective-permute-start(bf16[512,1536]{1,0:T(8,128)(2,1)} %copy-done.25), channel_id=1, source_target_pairs={{0,8},{8,0},{16,24},{24,16},{1,9},{9,1},{17,25},{25,17},{2,10},{10... | collective-permute-start | bytes 4718600 | tf_op jit(solution)/shard_map/ppermute | solution.py:432
  306.5 45.9 %collective-permute-start.39 = (bf16[512,1536]{1,0:T(8,128)(2,1)}, bf16[512,1536]{1,0:T(8,128)(2,1)}, u32[]{:S(2)}, u32[]{:S(2)}) collective-permute-start(bf16[512,1536]{1,0:T(8,128)(2,1)} %constant_dynamic-update-slice_fusion.6), channel_id=1, source_target_pairs={{0,16},{8,24},{16,0},{24,8},{1,17},{9,25},{17,1},{25,9},{2,18},{10... | collective-permute-start | bytes 4718600 | tf_op jit(solution)/shard_map/ppermute | solution.py:432
  308.5 34.1 %collective-permute-start.43 = (f32[2,128]{1,0:T(2,128)S(1)}, f32[2,128]{1,0:T(2,128)S(1)}, u32[]{:S(2)}, u32[]{:S(2)}) collective-permute-start(f32[2,128]{1,0:T(2,128)S(1)} %add.188), channel_id=1, source_target_pairs={{0,2},{1,3},{2,0},{3,1},{4,6},{5,7},{6,4},{7,5},{8,10},{9,11},{10,... | collective-permute-start | bytes 3080 | tf_op jit(solution)/shard_map/ppermute | solution.py:439
  346.4 24.1 %collective-permute-start.45 = (bf16[256,1536]{1,0:T(8,128)(2,1)}, bf16[256,1536]{1,0:T(8,128)(2,1)}, u32[]{:S(2)}, u32[]{:S(2)}) collective-permute-start(bf16[256,1536]{1,0:T(8,128)(2,1)} %add_convert_fusion.2), channel_id=1, source_target_pairs={{0,16},{8,24},{16,0},{24,8},{1,17},{9,25},{17,1},{25,9},{2,18},{10... | collective-permute-start | bytes 2359304 | tf_op jit(solution)/shard_map/ppermute | solution.py:432
  354.8 20.8 %collective-permute-start.46 = (bf16[256,1536]{1,0:T(8,128)(2,1)}, bf16[256,1536]{1,0:T(8,128)(2,1)}, u32[]{:S(2)}, u32[]{:S(2)}) collective-permute-start(bf16[256,1536]{1,0:T(8,128)(2,1)} %add_convert_fusion.1), channel_id=1, source_target_pairs={{0,8},{8,0},{16,24},{24,16},{1,9},{9,1},{17,25},{25,17},{2,10},{10... | collective-permute-start | bytes 2359304 | tf_op jit(solution)/shard_map/ppermute | solution.py:432
  (133 other events, 915.4 us)
Sparse Core Ops, SparseCore 0:
  22.0 55.1 all-gather.6
  79.4 63.5 all-gather.8
  144.6 36.9 all-gather.10
  220.5 82.3 reduce-scatter.2
  305.0 48.5 reduce-scatter.4

commit v5 on v4

--- a/solution.py
+++ b/solution.py
@@ -164,11 +164,26 @@
         refs[:count],
         refs[count : 2 * count],
         refs[2 * count : 2 * count + down_terms],
-        refs[-1],
-    )
+        refs[-3],
+    )
+    held, sem = refs[-2:]
     d, tile = out.shape[0], 512
     tall = downs[0].shape[0] // d
     rows = lefts[0].shape[1] // PLANE // d
+    for z in range(d):
+        value = add_up([term[z * tall : (z + 1) * tall, :] for term in downs]).astype(BF16)
+        for row, col, to_row, to_col, size in down_blocks(tall):
+            held[z, PLANE * rows + to_row : PLANE * rows + to_row + size, to_col : to_col + 512] = (
+                value[row : row + size, col : col + 512]
+            )
+    copies, whole = [], rows % 16 != 0
+
+    def send(*at):
+        copies.append(pltpu.make_async_copy(held.at[at], out.at[at], sem.at[len(copies)]))
+        copies[-1].start()
+
+    if not whole:
+        send(slice(None), pl.ds(PLANE * rows, out.shape[1] - PLANE * rows))
     for at in range(0, rights[0].shape[1], tile):
         cols = slice(at, at + tile)
         value = sum(mm_tn(left[...], right[:, cols]) for left, right in zip(lefts, rights))
@@ -176,13 +191,13 @@
         for z in range(d):
             for j in range(PLANE):
                 start = (j * d + z) * rows
-                out[z, j * rows : (j + 1) * rows, cols] = value[start : start + rows]
-    for z in range(d):
-        value = add_up([term[z * tall : (z + 1) * tall, :] for term in downs]).astype(BF16)
-        for row, col, to_row, to_col, size in down_blocks(tall):
-            out[z, PLANE * rows + to_row : PLANE * rows + to_row + size, to_col : to_col + 512] = (
-                value[row : row + size, col : col + 512]
-            )
+                held[z, j * rows : (j + 1) * rows, cols] = value[start : start + rows]
+        if not whole:
+            send(slice(None), pl.ds(0, PLANE * rows), pl.ds(at, tile))
+    if whole:
+        send(slice(None))
+    for copy in copies:
+        copy.wait()
 
 
 def down_kernel(count, *refs):
@@ -700,6 +715,11 @@
         functools.partial(second_grad_kernel, 2 * members, members),
         (shaped(d, PLANE * rows + down_weight.shape[0] * 3 // 4, 2 * LOCAL_FF),),
         (*flat(lefts), *flat(rights), *down_terms),
+        scratch=(
+            pltpu.VMEM((d, PLANE * rows + down_weight.shape[0] * 3 // 4, 2 * LOCAL_FF), BF16),
+            pltpu.SemaphoreType.DMA((8,)),
+        ),
+        out_spec=ANY,
     )[0]
     second_sum = to_owner(second_message)
     grad_residual = grad_out + norm_back(

time: 395 us -> 396 us (level)
  transfers between devices with their start and end apart: 55 -> 55, of which waited for: 23 -> 22; matrix products, arithmetic and copies ran while one was open for 10% -> 10% of each run, Pallas kernels for 24% -> 25%
where the time goes in v5:
time: 396 us; the launch traced here: 392 us
  waiting for transfers between devices  138 us (35%)
  Pallas kernels  102 us (26%)
  starting transfers between devices  54.2 us (14%)
  local copies, waits for them, and re-layouts  48.7 us (12%)
  other arithmetic  31.2 us (8%)
  between operations  18.1 us (5%)
    ppermute x38, waiting for transfers between devices, plane(): return lax.ppermute(value, 'j', [(i, i ^ r) for i in range(PLANE)])  113 us
    pallas_call x28, Pallas kernels, call(): pl.pallas_call(kernel, out_shape=tuple(outs), in_specs=specs or [VMEM] *...  102 us
    ppermute x38, starting transfers between devices, plane(): return lax.ppermute(value, 'j', [(i, i ^ r) for i in range(PLANE)])  46.4 us
    unnamed x208, local copies, waits for them, and re-layouts  41.7 us
    all_gather x1, waiting for transfers between devices, per_device(): second_all = everywhere(tie(second_message, *x_near[1:]))  12 us
  transfers between devices with their start and end apart: 55, of which 22 were waited for; matrix products, arithmetic and copies ran while one was open for 10% of the time, Pallas kernels for 25%

profile of v5, /device:TPU:0, one launch (start us, length us, event | category | flops | bytes accessed | tf_op | source)
XLA Modules:
  0.0 392.2 jit_solution(3528947209072286680)
XLA Ops:
  16.5 3.8 collective-permute-done.1.refs_2_
  29.6 16.9 %collective-permute-done.15.refs_1_ = bf16[48,2048]{1,0:T(8,128)(2,1)S(1)} collective-permute-done((bf16[48,2048]{1,0:T(8,128)(2,1)S(1)}, bf16[48,2048]{1,0:T(8,128)(2,1)S(1)}, u32[]{:S(2)}, u32[]{:S(2)}) %collective-permute-start.15) | collective-permute-done | bytes 196640 | tf_op jit(solution)/shard_map/ppermute | solution.py:447
  54.8 7.9 %collective-permute-done.4 = bf16[128,1536]{1,0:T(8,128)(2,1)S(1)} collective-permute-done((bf16[128,1536]{1,0:T(8,128)(2,1)S(1)}, bf16[128,1536]{1,0:T(8,128)(2,1)S(1)}, u32[]{:S(2)}, u32[]{:S(2)}) %collective-permute-start.4) | collective-permute-done | bytes 393248 | tf_op jit(solution)/shard_map/ppermute | solution.py:447
  68.7 11.1 %collective-permute-done.9.refs_4_.refs_0_ = bf16[256,1536]{1,0:T(8,128)(2,1)S(1)} collective-permute-done((bf16[256,1536]{1,0:T(8,128)(2,1)S(1)}, bf16[256,1536]{1,0:T(8,128)(2,1)S(1)}, u32[]{:S(2)}, u32[]{:S(2)}) %collective-permute-start.9) | collective-permute-done | bytes 786464 | tf_op jit(solution)/shard_map/ppermute | solution.py:447
  112.3 4.2 %collective-permute-done.13 = bf16[256,1536]{1,0:T(8,128)(2,1)S(1)} collective-permute-done((bf16[256,1536]{1,0:T(8,128)(2,1)S(1)}, bf16[256,1536]{1,0:T(8,128)(2,1)S(1)}, u32[]{:S(2)}, u32[]{:S(2)}) %collective-permute-start.13) | collective-permute-done | bytes 786464 | tf_op jit(solution)/shard_map/ppermute | solution.py:447
  116.6 9.6 %collective-permute-done.12 = bf16[256,1536]{1,0:T(8,128)(2,1)S(1)} collective-permute-done((bf16[256,1536]{1,0:T(8,128)(2,1)S(1)}, bf16[256,1536]{1,0:T(8,128)(2,1)S(1)}, u32[]{:S(2)}, u32[]{:S(2)}) %collective-permute-start.12) | collective-permute-done | bytes 786464 | tf_op jit(solution)/shard_map/ppermute | solution.py:447
  131.0 12.0 %all-gather.9.cloned.1.call-done = bf16[32,48,2048]{2,1,0:T(8,128)(2,1)} async-done(((bf16[4,48,2048]{2,1,0:T(8,128)(2,1)}), bf16[32,48,2048]{2,1,0:T(8,128)(2,1)}) %all-gather.9.cloned.1.call-update) | async-done | bytes 6291472 | tf_op jit(solution)/shard_map/all_gather | solution.py:620
  153.2 5.2 %shard_map.417 = (bf16[512,1024]{1,0:T(8,128)(2,1)S(1)}, bf16[512,1024]{1,0:T(8,128)(2,1)S(1)}, bf16[512,1024]{1,0:T(8,128)(2,1)S(1)}, bf16[512,768]{1,0:T(8,128)(2,1)S(1)}, bf16[512,768]{1,0:T(8,128)(2,1)}) custom-call(s32[3]{0:T(128)S(1)} %pad_add_fusion.1.pos_ref, bf16[256,1536]{1,0:T(8,128)(2,1)S(1)} %multiply_convert_fusion.refs_0_, ...), custom_call_target="tpu_custom_call" | custom-call | flops 5750000128 | tf_op jit(solution)/shard_map/pallas_call | solution.py:421
  161.6 5.5 %shard_map.418 = (bf16[512,1024]{1,0:T(8,128)(2,1)S(1)}, bf16[512,1024]{1,0:T(8,128)(2,1)S(1)}, bf16[512,1024]{1,0:T(8,128)(2,1)S(1)}, bf16[512,768]{1,0:T(8,128)(2,1)S(1)}, bf16[512,768]{1,0:T(8,128)(2,1)}) custom-call(s32[3]{0:T(128)S(1)} %pad_add_fusion.1.pos_ref, bf16[256,1536]{1,0:T(8,128)(2,1)} %collective-permute-done.18.refs_0_, ...), custom_call_target="tpu_custom_call" | custom-call | flops 5750000128 | tf_op jit(solution)/shard_map/pallas_call | solution.py:421
  170.2 4.1 %shard_map.419 = (bf16[512,1536]{1,0:T(8,128)(2,1)S(1)}, bf16[512,1536]{1,0:T(8,128)(2,1)S(1)}) custom-call(s32[3]{0:T(128)S(1)} %pad_add_fusion.1.pos_ref, bf16[512,1024]{1,0:T(8,128)(2,1)S(1)} %get-tuple-element.168.refs_0_, bf16[512,1024]{1,0:T(8,128)(2,1)S(1)} %get-tuple-element.172.refs_1_, ...), custom_call_target="tpu_custom_call" | custom-call | flops 4600000000 | tf_op jit(solution)/shard_map/pallas_call | solution.py:421
  177.5 4.0 %all-gather.11.cloned.1.call-done = bf16[1024,1536]{1,0:T(8,128)(2,1)} async-done(((bf16[128,1536]{1,0:T(8,128)(2,1)}), bf16[1024,1536]{1,0:T(8,128)(2,1)}) %all-gather.11.cloned.1.call-update) | async-done | bytes 3145744 | tf_op jit(solution)/shard_map/all_gather | solution.py:622
  188.7 6.1 %shard_map.420 = (bf16[256,1536]{1,0:T(8,128)(2,1)S(1)}, bf16[256,1536]{1,0:T(8,128)(2,1)}, bf16[512,2048]{1,0:T(8,128)(2,1)S(1)}) custom-call(bf16[256,1536]{1,0:T(8,128)(2,1)S(1)} %convert_multiply_fusion.2.refs_2_.refs_0_, bf16[256,1536]{1,0:T(8,128)(2,1)S(1)} %collective-permute-done.7.refs_3_.refs_1_, bf16[512,1024]{1,0:T(8,128)(2,1)S(1)} %copy-done.43, ...), custom_call_target="tpu_custom_call" | custom-call | flops 5750000128 | tf_op jit(solution)/shard_map/pallas_call | solution.py:421
  195.3 5.2 %shard_map.421 = (bf16[256,1536]{1,0:T(8,128)(2,1)S(1)}, bf16[256,1536]{1,0:T(8,128)(2,1)S(1)}, bf16[512,2048]{1,0:T(8,128)(2,1)S(1)}) custom-call(bf16[256,1536]{1,0:T(8,128)(2,1)S(1)} %collective-permute-done.9.refs_4_.refs_0_, bf16[256,1536]{1,0:T(8,128)(2,1)S(1)} %copy-done.13, bf16[512,1024]{1,0:T(8,128)(2,1)S(1)} %copy-done.47, ...), custom_call_target="tpu_custom_call" | custom-call | flops 5750000128 | tf_op jit(solution)/shard_map/pallas_call | solution.py:421
  209.4 10.0 %shard_map.422 = bf16[4,288,2048]{2,1,0:T(8,128)(2,1)S(1)} custom-call(bf16[512,768]{1,0:T(8,128)(2,1)S(1)} %copy-done.73, bf16[512,768]{1,0:T(8,128)(2,1)} %collective-permute-done.22.refs_1_, bf16[512,768]{1,0:T(8,128)(2,1)S(1)} %copy-done.75, bf16[512,768]{1,0:T(8,128)(2,1)} %collective-permute-done.23.refs_3_, ...), custom_call_target="tpu_custom_call" | custom-call | flops 8625000448 | tf_op jit(solution)/shard_map/pallas_call | solution.py:421
  222.0 16.9 %collective-permute-done.28 = bf16[256,1536]{1,0:T(8,128)(2,1)} collective-permute-done((bf16[256,1536]{1,0:T(8,128)(2,1)S(1)}, bf16[256,1536]{1,0:T(8,128)(2,1)}, u32[]{:S(2)}, u32[]{:S(2)}) %collective-permute-start.28) | collective-permute-done | bytes 786464 | tf_op jit(solution)/shard_map/ppermute | solution.py:447
  242.0 3.8 fusion.19
  252.4 4.8 %shard_map.424 = (bf16[256,1152]{1,0:T(8,128)(2,1)S(1)}, bf16[256,1536]{1,0:T(8,128)(2,1)S(1)}, f32[2,128]{1,0:T(2,128)S(1)}) custom-call(bf16[256,1536]{1,0:T(8,128)(2,1)S(1)} %get-tuple-element.198.dh_ref.refs_4_, bf16[256,1152]{1,0:T(8,128)(2,1)S(1)} %copy-done.71, bf16[1536,1280]{1,0:T(8,128)(2,1)S(1)} %bitcast.44, bf16[384,1536]{1,0:T(8,128)(2,1)S(1)} %bitcast.52, ...), custom_call_target="tpu_custom_call" | custom-call | flops 17250000896 | tf_op jit(solution)/shard_map/pallas_call | solution.py:421
  257.3 7.4 %collective-permute-done.30.dh_ref.refs_6_ = bf16[256,1536]{1,0:T(8,128)(2,1)S(1)} collective-permute-done((bf16[256,1536]{1,0:T(8,128)(2,1)S(1)}, bf16[256,1536]{1,0:T(8,128)(2,1)S(1)}, u32[]{:S(2)}, u32[]{:S(2)}) %collective-permute-start.30) | collective-permute-done | bytes 786464 | tf_op jit(solution)/shard_map/ppermute | solution.py:447
  266.9 4.8 %shard_map.425 = (bf16[256,1152]{1,0:T(8,128)(2,1)S(1)}, bf16[256,1536]{1,0:T(8,128)(2,1)S(1)}, f32[2,128]{1,0:T(2,128)S(1)}) custom-call(bf16[256,1536]{1,0:T(8,128)(2,1)S(1)} %collective-permute-done.29.dh_ref.refs_5_, bf16[256,1152]{1,0:T(8,128)(2,1)S(1)} %copy-done.69, bf16[1536,1280]{1,0:T(8,128)(2,1)S(1)} %bitcast.45, bf16[384,1536]{1,0:T(8,128)(2,1)S(1)} %bitcast.53, ...), custom_call_target="tpu_custom_call" | custom-call | flops 17250000896 | tf_op jit(solution)/shard_map/pallas_call | solution.py:421
  271.7 5.0 %shard_map.426 = (bf16[256,1152]{1,0:T(8,128)(2,1)S(1)}, bf16[256,1536]{1,0:T(8,128)(2,1)S(1)}, f32[2,128]{1,0:T(2,128)S(1)}) custom-call(bf16[256,1536]{1,0:T(8,128)(2,1)S(1)} %collective-permute-done.30.dh_ref.refs_6_, bf16[256,1152]{1,0:T(8,128)(2,1)S(1)} %copy-done.67, bf16[1536,1280]{1,0:T(8,128)(2,1)S(1)} %bitcast.46, bf16[384,1536]{1,0:T(8,128)(2,1)S(1)} %bitcast.54, ...), custom_call_target="tpu_custom_call" | custom-call | flops 17250000896 | tf_op jit(solution)/shard_map/pallas_call | solution.py:421
  277.7 4.8 %shard_map.427 = (bf16[256,1152]{1,0:T(8,128)(2,1)S(1)}, bf16[256,1536]{1,0:T(8,128)(2,1)S(1)}, f32[2,128]{1,0:T(2,128)S(1)}) custom-call(bf16[256,1536]{1,0:T(8,128)(2,1)S(1)} %constant_dynamic-update-slice_fusion.4.dh_ref.refs_7_, bf16[256,1152]{1,0:T(8,128)(2,1)S(1)} %copy-done.65, bf16[1536,1280]{1,0:T(8,128)(2,1)S(1)} %bitcast.47, ...), custom_call_target="tpu_custom_call" | custom-call | flops 17250000896 | tf_op jit(solution)/shard_map/pallas_call | solution.py:421
  282.6 5.6 %shard_map.428 = (bf16[4,192,1152]{2,1,0:T(8,128)(2,1)S(1)}, bf16[4,192,1152]{2,1,0:T(8,128)(2,1)S(1)}) custom-call(s32[3]{0:T(128)S(1)} %pad_add_fusion.1.pos_ref, bf16[256,1536]{1,0:T(8,128)(2,1)S(1)} %copy-done.59, bf16[256,1536]{1,0:T(8,128)(2,1)S(1)} %copy-done.57, bf16[256,1536]{1,0:T(8,128)(2,1)S(1)} %copy-done.55, bf16[256,1536]{1,0:T(8,128)(2,1)S(1)} %copy-done.53, ...), custom_call_target="tpu_custom_call" | custom-call | flops 5750000128 | tf_op jit(solution)/shard_map/pallas_call | solution.py:421
  313.7 25.4 %collective-permute-done.35 = bf16[512,1536]{1,0:T(8,128)(2,1)} collective-permute-done((bf16[512,1536]{1,0:T(8,128)(2,1)}, bf16[512,1536]{1,0:T(8,128)(2,1)}, u32[]{:S(2)}, u32[]{:S(2)}) %collective-permute-start.35) | collective-permute-done | bytes 1572896 | tf_op jit(solution)/shard_map/ppermute | solution.py:447
  359.2 5.0 %shard_map.432 = (f32[48,8192]{1,0:T(8,128)}, f32[48,8192]{1,0:T(8,128)}, f32[48,8192]{1,0:T(8,128)}, f32[8,48]{1,0:T(8,128)S(1)}) custom-call(s32[3]{0:T(128)S(1)} %pad_add_fusion.1.pos_ref, bf16[48,2048]{1,0:T(8,128)(2,1)S(1)} %copy-done.41, bf16[48,2048]{1,0:T(8,128)(2,1)} %collective-permute-done.38.refs_1_, ...), custom_call_target="tpu_custom_call" | custom-call | flops 4600000000 | tf_op jit(solution)/shard_map/pallas_call | solution.py:421
  (376 shorter events, 185.0 us)
Async XLA Ops:
  7.2 77.0 %all-gather.7.cloned.1.call-start = ((), (), s32[]{:S(2)}) async-start(), calls=%async_computation.4 | async-start | bytes 5750784 | tf_op jit(solution)/shard_map/all_gather | solution.py:618
  21.9 121.1 %all-gather.9.cloned.1.call-start = ((), (), s32[]{:S(2)}) async-start(), calls=%async_computation.5 | async-start | bytes 7077888 | tf_op jit(solution)/shard_map/all_gather | solution.py:620
  22.0 30.0 %collective-permute-start.5 = (bf16[256,1536]{1,0:T(8,128)(2,1)S(1)}, bf16[256,1536]{1,0:T(8,128)(2,1)S(1)}, u32[]{:S(2)}, u32[]{:S(2)}) collective-permute-start(bf16[256,1536]{1,0:T(8,128)(2,1)S(1)} %copy-done), channel_id=1, source_target_pairs={{0,16},{8,24},{16,0},{24,8},{1,17},{9,25},{17,1},{25,9},{2,18},{10... | collective-permute-start | bytes 2359304 | tf_op jit(solution)/shard_map/ppermute | solution.py:447
  23.5 28.5 %collective-permute-start.3 = (bf16[256,1536]{1,0:T(8,128)(2,1)S(1)}, bf16[256,1536]{1,0:T(8,128)(2,1)S(1)}, u32[]{:S(2)}, u32[]{:S(2)}) collective-permute-start(bf16[256,1536]{1,0:T(8,128)(2,1)S(1)} %copy-done), channel_id=1, source_target_pairs={{0,8},{8,0},{16,24},{24,16},{1,9},{9,1},{17,25},{25,17},{2,10},{10... | collective-permute-start | bytes 2359304 | tf_op jit(solution)/shard_map/ppermute | solution.py:447
  26.0 20.4 %collective-permute-start.15 = (bf16[48,2048]{1,0:T(8,128)(2,1)S(1)}, bf16[48,2048]{1,0:T(8,128)(2,1)S(1)}, u32[]{:S(2)}, u32[]{:S(2)}) collective-permute-start(bf16[48,2048]{1,0:T(8,128)(2,1)S(1)} %get-tuple-element.162), channel_id=1, source_target_pairs={{0,8},{8,0},{16,24},{24,16},{1,9},{9,1},{17,25},{25,17},{2,10},{10... | collective-permute-start | bytes 589832 | tf_op jit(solution)/shard_map/ppermute | solution.py:447
  28.2 21.2 %collective-permute-start.17 = (bf16[48,2048]{1,0:T(8,128)(2,1)S(1)}, bf16[48,2048]{1,0:T(8,128)(2,1)S(1)}, u32[]{:S(2)}, u32[]{:S(2)}) collective-permute-start(bf16[48,2048]{1,0:T(8,128)(2,1)S(1)} %get-tuple-element.164), channel_id=1, source_target_pairs={{0,24},{8,16},{16,8},{24,0},{1,25},{9,17},{17,9},{25,1},{2,26},{10... | collective-permute-start | bytes 589832 | tf_op jit(solution)/shard_map/ppermute | solution.py:447
  52.0 129.5 %all-gather.11.cloned.1.call-start = ((), (), s32[]{:S(2)}) async-start(), calls=%async_computation.6 | async-start | bytes 3538944 | tf_op jit(solution)/shard_map/all_gather | solution.py:622
  68.7 235.4 %reduce-scatter.3.cloned.1.call-start = ((), (), s32[]{:S(2)}) async-start(), calls=%async_computation.2 | async-start | bytes 5898240 | tf_op jit(solution)/shard_map/reduce_scatter | solution.py:724
  80.6 26.1 %collective-permute-start.10 = (bf16[128,1536]{1,0:T(8,128)(2,1)}, bf16[128,1536]{1,0:T(8,128)(2,1)}, u32[]{:S(2)}, u32[]{:S(2)}) collective-permute-start(bf16[128,1536]{1,0:T(8,128)(2,1)} %slice.95), channel_id=1, source_target_pairs={{0,8},{8,0},{16,24},{24,16},{1,9},{9,1},{17,25},{25,17},{2,10},{10... | collective-permute-start | bytes 1179656 | tf_op jit(solution)/shard_map/ppermute | solution.py:447
  82.5 23.2 %collective-permute-start.8 = (bf16[128,1536]{1,0:T(8,128)(2,1)}, bf16[128,1536]{1,0:T(8,128)(2,1)}, u32[]{:S(2)}, u32[]{:S(2)}) collective-permute-start(bf16[128,1536]{1,0:T(8,128)(2,1)} %slice.94), channel_id=1, source_target_pairs={{0,16},{8,24},{16,0},{24,8},{1,17},{9,25},{17,1},{25,9},{2,18},{10... | collective-permute-start | bytes 1179656 | tf_op jit(solution)/shard_map/ppermute | solution.py:447
  95.2 21.4 %collective-permute-start.13 = (bf16[256,1536]{1,0:T(8,128)(2,1)S(1)}, bf16[256,1536]{1,0:T(8,128)(2,1)S(1)}, u32[]{:S(2)}, u32[]{:S(2)}) collective-permute-start(bf16[256,1536]{1,0:T(8,128)(2,1)S(1)} %get-tuple-element.159), channel_id=1, source_target_pairs={{0,24},{8,16},{16,8},{24,0},{1,25},{9,17},{17,9},{25,1},{2,26},{10... | collective-permute-start | bytes 2359304 | tf_op jit(solution)/shard_map/ppermute | solution.py:447
  98.9 27.3 %collective-permute-start.12 = (bf16[256,1536]{1,0:T(8,128)(2,1)S(1)}, bf16[256,1536]{1,0:T(8,128)(2,1)S(1)}, u32[]{:S(2)}, u32[]{:S(2)}) collective-permute-start(bf16[256,1536]{1,0:T(8,128)(2,1)S(1)} %get-tuple-element.158), channel_id=1, source_target_pairs={{0,16},{8,24},{16,0},{24,8},{1,17},{9,25},{17,1},{25,9},{2,18},{10... | collective-permute-start | bytes 2359304 | tf_op jit(solution)/shard_map/ppermute | solution.py:447
  104.3 22.2 %collective-permute-start.11 = (bf16[256,1536]{1,0:T(8,128)(2,1)S(1)}, bf16[256,1536]{1,0:T(8,128)(2,1)S(1)}, u32[]{:S(2)}, u32[]{:S(2)}) collective-permute-start(bf16[256,1536]{1,0:T(8,128)(2,1)S(1)} %get-tuple-element.157), channel_id=1, source_target_pairs={{0,8},{8,0},{16,24},{24,16},{1,9},{9,1},{17,25},{25,17},{2,10},{10... | collective-permute-start | bytes 2359304 | tf_op jit(solution)/shard_map/ppermute | solution.py:447
  161.3 33.7 %collective-permute-start.22 = (bf16[512,768]{1,0:T(8,128)(2,1)}, bf16[512,768]{1,0:T(8,128)(2,1)}, u32[]{:S(2)}, u32[]{:S(2)}) collective-permute-start(bf16[512,768]{1,0:T(8,128)(2,1)} %get-tuple-element.181), channel_id=1, source_target_pairs={{0,4},{4,0},{1,5},{5,1},{2,6},{6,2},{3,7},{7,3},{8,12},{12,8},{9,1... | collective-permute-start | bytes 2359304 | tf_op jit(solution)/shard_map/ppermute | solution.py:450
  170.0 25.1 %collective-permute-start.23 = (bf16[512,768]{1,0:T(8,128)(2,1)}, bf16[512,768]{1,0:T(8,128)(2,1)}, u32[]{:S(2)}, u32[]{:S(2)}) collective-permute-start(bf16[512,768]{1,0:T(8,128)(2,1)} %get-tuple-element.183), channel_id=1, source_target_pairs={{0,4},{4,0},{1,5},{5,1},{2,6},{6,2},{3,7},{7,3},{8,12},{12,8},{9,1... | collective-permute-start | bytes 2359304 | tf_op jit(solution)/shard_map/ppermute | solution.py:450
  201.1 37.9 %collective-permute-start.21 = (bf16[256,1536]{1,0:T(8,128)(2,1)}, bf16[256,1536]{1,0:T(8,128)(2,1)}, u32[]{:S(2)}, u32[]{:S(2)}) collective-permute-start(bf16[256,1536]{1,0:T(8,128)(2,1)} %get-tuple-element.179), channel_id=1, source_target_pairs={{0,8},{8,0},{16,24},{24,16},{1,9},{9,1},{17,25},{25,17},{2,10},{10... | collective-permute-start | bytes 2359304 | tf_op jit(solution)/shard_map/ppermute | solution.py:447
  202.6 36.4 %collective-permute-start.27 = (bf16[256,1536]{1,0:T(8,128)(2,1)S(1)}, bf16[256,1536]{1,0:T(8,128)(2,1)}, u32[]{:S(2)}, u32[]{:S(2)}) collective-permute-start(bf16[256,1536]{1,0:T(8,128)(2,1)S(1)} %get-tuple-element.191), channel_id=1, source_target_pairs={{0,16},{8,24},{16,0},{24,8},{1,17},{9,25},{17,1},{25,9},{2,18},{10... | collective-permute-start | bytes 2359304 | tf_op jit(solution)/shard_map/ppermute | solution.py:447
  207.0 32.0 %collective-permute-start.28 = (bf16[256,1536]{1,0:T(8,128)(2,1)S(1)}, bf16[256,1536]{1,0:T(8,128)(2,1)}, u32[]{:S(2)}, u32[]{:S(2)}) collective-permute-start(bf16[256,1536]{1,0:T(8,128)(2,1)S(1)} %get-tuple-element.193), channel_id=1, source_target_pairs={{0,24},{8,16},{16,8},{24,0},{1,25},{9,17},{17,9},{25,1},{2,26},{10... | collective-permute-start | bytes 2359304 | tf_op jit(solution)/shard_map/ppermute | solution.py:447
  221.6 142.7 %reduce-scatter.5.cloned.1.call-start = ((), (), s32[]{:S(2)}) async-start(), calls=%async_computation.3 | async-start | bytes 2949120 | tf_op jit(solution)/shard_map/reduce_scatter | solution.py:762
  302.7 36.4 %collective-permute-start.35 = (bf16[512,1536]{1,0:T(8,128)(2,1)}, bf16[512,1536]{1,0:T(8,128)(2,1)}, u32[]{:S(2)}, u32[]{:S(2)}) collective-permute-start(bf16[512,1536]{1,0:T(8,128)(2,1)} %copy-done.25), channel_id=1, source_target_pairs={{0,8},{8,0},{16,24},{24,16},{1,9},{9,1},{17,25},{25,17},{2,10},{10... | collective-permute-start | bytes 4718600 | tf_op jit(solution)/shard_map/ppermute | solution.py:447
  306.7 46.6 %collective-permute-start.39 = (bf16[512,1536]{1,0:T(8,128)(2,1)}, bf16[512,1536]{1,0:T(8,128)(2,1)}, u32[]{:S(2)}, u32[]{:S(2)}) collective-permute-start(bf16[512,1536]{1,0:T(8,128)(2,1)} %constant_dynamic-update-slice_fusion.6), channel_id=1, source_target_pairs={{0,16},{8,24},{16,0},{24,8},{1,17},{9,25},{17,1},{25,9},{2,18},{10... | collective-permute-start | bytes 4718600 | tf_op jit(solution)/shard_map/ppermute | solution.py:447
  308.9 33.7 %collective-permute-start.43 = (f32[2,128]{1,0:T(2,128)S(1)}, f32[2,128]{1,0:T(2,128)S(1)}, u32[]{:S(2)}, u32[]{:S(2)}) collective-permute-start(f32[2,128]{1,0:T(2,128)S(1)} %add.188), channel_id=1, source_target_pairs={{0,2},{1,3},{2,0},{3,1},{4,6},{5,7},{6,4},{7,5},{8,10},{9,11},{10,... | collective-permute-start | bytes 3080 | tf_op jit(solution)/shard_map/ppermute | solution.py:454
  347.3 23.7 %collective-permute-start.45 = (bf16[256,1536]{1,0:T(8,128)(2,1)}, bf16[256,1536]{1,0:T(8,128)(2,1)}, u32[]{:S(2)}, u32[]{:S(2)}) collective-permute-start(bf16[256,1536]{1,0:T(8,128)(2,1)} %add_convert_fusion.2), channel_id=1, source_target_pairs={{0,16},{8,24},{16,0},{24,8},{1,17},{9,25},{17,1},{25,9},{2,18},{10... | collective-permute-start | bytes 2359304 | tf_op jit(solution)/shard_map/ppermute | solution.py:447
  355.6 20.7 %collective-permute-start.46 = (bf16[256,1536]{1,0:T(8,128)(2,1)}, bf16[256,1536]{1,0:T(8,128)(2,1)}, u32[]{:S(2)}, u32[]{:S(2)}) collective-permute-start(bf16[256,1536]{1,0:T(8,128)(2,1)} %add_convert_fusion.1), channel_id=1, source_target_pairs={{0,8},{8,0},{16,24},{24,16},{1,9},{9,1},{17,25},{25,17},{2,10},{10... | collective-permute-start | bytes 2359304 | tf_op jit(solution)/shard_map/ppermute | solution.py:447
  (133 other events, 923.6 us)
Sparse Core Ops, SparseCore 0:
  22.0 55.1 all-gather.6
  79.4 63.5 all-gather.8
  144.6 36.9 all-gather.10
  221.7 82.3 reduce-scatter.2
  306.2 48.5 reduce-scatter.4
